TPU v7x, 128 devices: a whole 4x4x4 slice. The times are simulated.
128 devices in a mesh: tp: 8 (over y, x_lo), ep: 16 (over x_hi, z, core).
Axes of the slice: x: 4 (x_hi: 2, x_lo: 2; x = x_hi * 2 + x_lo), y: 4, z: 4, core: 2. Of those that a mesh axis runs over, the one named last changes fastest.
Arguments:
- hidden: bfloat16 [16384, 18432], P(('ep', 'tp')), may hold values from -6 to 6
- output_gradient: bfloat16 [16384, 4608], P(('ep', 'tp')), may hold values from -6 to 6
- specialist_pairs: int32 [16384, 2], P(('ep', 'tp')), may hold values from 0 to 127, all different within a row; in each aligned block of 128 rows (0 to 127, 128 to 255, ...) at most 3 rows name the same one
- chosen_router_logits: float32 [16384, 2], P(('ep', 'tp')), may hold values from -6 to 6
- lowering_maps: bfloat16 [128, 18432, 32], P(('ep', 'tp')), may hold values from -0.046875 to 0.046875
- raising_maps: bfloat16 [128, 32, 4608], P(('ep', 'tp')), may hold values from -1 to 1
- dispatcher_map: bfloat16 [4608, 128], replicated, may hold values from -0.09375 to 0.09375
- queries: bfloat16 [16384, 2048], P('ep', 'tp'), may hold values from -15 to 15
- keys: bfloat16 [16384, 1024], P('ep', 'tp'), may hold values from -15 to 15
- values: bfloat16 [16384, 1024], P('ep', 'tp'), may hold values from -6 to 6
- context_gradient: bfloat16 [16384, 2048], P('ep', 'tp'), may hold values from -6 to 6
- query_projection: bfloat16 [4608, 2048], P(None, 'tp'), may hold values from -0.09375 to 0.09375
- key_projection: bfloat16 [4608, 1024], P(None, 'tp'), may hold values from -0.09375 to 0.09375
- value_projection: bfloat16 [4608, 1024], P(None, 'tp'), may hold values from -0.09375 to 0.09375
- lengths: int32 [16, 8], P('ep'), may hold values from 1 to 512, 1024 in all within a row
Outputs:
- residual_input_gradient: bfloat16 [16384, 4608], P(('ep', 'tp'))
- gated_hidden_gradient: bfloat16 [16384, 18432], P(('ep', 'tp'))
- router_logit_gradient: float32 [16384, 2], P(('ep', 'tp'))
- down_factors_gradient: bfloat16 [128, 18432, 32], P(('ep', 'tp'))
- up_factors_gradient: bfloat16 [128, 32, 4608], P(('ep', 'tp'))
Inputs may be any that keep to these rules, and one draw needn't show every extreme that they name: `specialist_pairs`: each row names two different experts. In each aligned block of 128 rows (the rows of one device) no expert is named by more than 3 rows, and in every draw some expert is named by exactly 3 rows of some block. `lengths`: each row sums to 1024 and its largest entry is exactly 512.
All inputs are finite; a program needn't handle non-finite values.
Results may differ from a plain program's by a relative error of at most 0.015.
Values may be sent and summed in bfloat16 or wider, within the bound.
No kernel may reach another device: no remote copies, remote signals or barrier semaphores. Data moves between devices by JAX's collectives and lax.ppermute only.
A program may use at most 320 MiB of HBM per device.

v0:
```python
import jax
import jax.numpy as jnp
from jax import lax
from jax.sharding import PartitionSpec as P

HD = 128


adapter_scale = 2.0
score_cap = 50.0
query_scale = 144.0 ** (-0.5)


def attend_backward(
    queries,
    keys,
    values,
    context_gradient,
    lengths,
    query_projection,
    key_projection,
    value_projection,
):
    rows = queries.shape[0]
    kv_count = keys.shape[1] // HD
    group = queries.shape[1] // keys.shape[1]
    query4 = queries.reshape(rows, kv_count, group, HD)
    ctx4 = context_gradient.reshape(rows, kv_count, group, HD)
    key3 = keys.reshape(rows, kv_count, HD)
    value3 = values.reshape(rows, kv_count, HD)
    places = jnp.arange(rows, dtype=jnp.int32)
    bounds = jnp.cumsum(lengths)
    docs = jnp.sum((places[:, None] >= bounds[None, :]).astype(jnp.int32), axis=1)
    allowed = (docs[:, None] == docs[None, :]) & (places[:, None] >= places[None, :])
    raw = (
        jnp.einsum("ikgd,jkd->kgij", query4, key3, preferred_element_type=jnp.float32) * query_scale
    )
    bent = jnp.tanh(raw / score_cap)
    expo = jnp.where(allowed, jnp.exp(score_cap * bent), 0.0)
    probs = expo / jnp.sum(expo, axis=-1, keepdims=True)
    dprobs = jnp.einsum("ikgd,jkd->kgij", ctx4, value3, preferred_element_type=jnp.float32)
    dsoft = probs * (dprobs - jnp.sum(probs * dprobs, axis=-1, keepdims=True))
    dscore = (dsoft * (1.0 - bent * bent)).astype(jnp.bfloat16)
    probs_b = probs.astype(jnp.bfloat16)
    dquery = (
        (
            jnp.einsum("kgij,jkd->ikgd", dscore, key3, preferred_element_type=jnp.float32)
            * query_scale
        )
        .astype(jnp.bfloat16)
        .reshape(rows, -1)
    )
    dkey = (
        (
            jnp.einsum("kgij,ikgd->jkd", dscore, query4, preferred_element_type=jnp.float32)
            * query_scale
        )
        .astype(jnp.bfloat16)
        .reshape(rows, -1)
    )
    dvalue = (
        jnp.einsum("kgij,ikgd->jkd", probs_b, ctx4, preferred_element_type=jnp.float32)
        .astype(jnp.bfloat16)
        .reshape(rows, -1)
    )
    part = jnp.einsum("te,de->td", dquery, query_projection, preferred_element_type=jnp.float32)
    part = part + jnp.einsum("te,de->td", dkey, key_projection, preferred_element_type=jnp.float32)
    part = part + jnp.einsum(
        "te,de->td", dvalue, value_projection, preferred_element_type=jnp.float32
    )
    return part


def single_expert_backward(rows_h, width_rows, rows_w, a_mat, up_factor_matrix):
    latent_value = jnp.dot(rows_h, a_mat, preferred_element_type=jnp.float32).astype(jnp.bfloat16)
    output_change = adapter_scale * jnp.dot(
        latent_value, up_factor_matrix, preferred_element_type=jnp.float32
    )
    gate_weight_value = jnp.sum(width_rows.astype(jnp.float32) * output_change, axis=-1).astype(
        jnp.bfloat16
    )
    expert_weight = rows_w.astype(jnp.float32)[:, None]
    projected_rows = jnp.einsum(
        "sd,rd->sr", width_rows, up_factor_matrix, preferred_element_type=jnp.float32
    )
    latent_gradient = (adapter_scale * expert_weight * projected_rows).astype(jnp.bfloat16)
    weighted_latent = (expert_weight * latent_value.astype(jnp.float32)).astype(jnp.bfloat16)
    up_factor_grad = (
        adapter_scale
        * jnp.einsum("km,kv->mv", weighted_latent, width_rows, preferred_element_type=jnp.float32)
    ).astype(jnp.bfloat16)
    down_factor_grad = jnp.einsum(
        "sf,sr->fr", rows_h, latent_gradient, preferred_element_type=jnp.float32
    ).astype(jnp.bfloat16)
    hidden_unit_grad = jnp.einsum(
        "sr,fr->sf", latent_gradient, a_mat, preferred_element_type=jnp.float32
    ).astype(jnp.bfloat16)
    return (hidden_unit_grad, gate_weight_value, down_factor_grad, up_factor_grad)


def router_term(specialist_pairs, weights, gates, dispatcher_map, experts):
    gate_val = gates.astype(jnp.float32)
    router_logit_gradient = weights * (
        gate_val - jnp.sum(weights * gate_val, axis=-1, keepdims=True)
    )
    ids = jnp.arange(experts, dtype=jnp.int32)
    expert_table = jnp.sum(
        jnp.where(
            specialist_pairs[:, :, None] == ids[None, None, :],
            router_logit_gradient[:, :, None],
            0.0,
        ),
        axis=1,
    )
    expert_table = expert_table.astype(jnp.bfloat16)
    term = jnp.einsum("te,de->td", expert_table, dispatcher_map, preferred_element_type=jnp.float32)
    return (router_logit_gradient, term)


def local(
    hidden,
    output_gradient,
    specialist_pairs,
    chosen_router_logits,
    lowering_maps,
    raising_maps,
    dispatcher_map,
    queries,
    keys,
    values,
    context_gradient,
    query_projection,
    key_projection,
    value_projection,
    lengths,
):
    tok_rows = hidden.shape[0]
    width_h = hidden.shape[1]
    width_d = output_gradient.shape[1]
    n_tp = lax.axis_size("tp")
    n_ep = lax.axis_size("ep")
    experts = n_tp * n_ep
    slots = max(2, 3 * tok_rows // experts)
    part = attend_backward(
        queries,
        keys,
        values,
        context_gradient,
        lengths[0],
        query_projection,
        key_projection,
        value_projection,
    )
    attention_rows = lax.psum_scatter(
        part.astype(jnp.bfloat16), "tp", scatter_dimension=0, tiled=True
    ).astype(jnp.float32)
    weights = jax.nn.softmax(chosen_router_logits, axis=-1)
    weights_b = weights.astype(jnp.bfloat16)
    flat = specialist_pairs.reshape(-1)
    hot = (flat[:, None] == jnp.arange(experts, dtype=jnp.int32)[None, :]).astype(jnp.int32)
    slot = jnp.sum(hot * (jnp.cumsum(hot, axis=0) - 1), axis=1)
    place = (flat % n_tp * n_ep + flat // n_tp) * slots + slot
    entries = jnp.arange(2 * tok_rows, dtype=jnp.int32)
    index = jnp.full((experts * slots,), 2 * tok_rows, jnp.int32).at[place].set(entries)
    token_index = index // 2
    send_h = jnp.concatenate([hidden, jnp.zeros((1, width_h), jnp.bfloat16)], axis=0)[token_index]
    send_d = jnp.concatenate([output_gradient, jnp.zeros((1, width_d), jnp.bfloat16)], axis=0)[
        token_index
    ]
    send_w = jnp.concatenate([weights_b.reshape(-1), jnp.zeros((1,), jnp.bfloat16)], axis=0)[index]
    received_hidden, received_width, received_weight = (
        lax.all_to_all(send_h, ("tp", "ep"), split_axis=0, concat_axis=0, tiled=True),
        lax.all_to_all(send_d, ("tp", "ep"), split_axis=0, concat_axis=0, tiled=True),
        lax.all_to_all(send_w, ("tp", "ep"), split_axis=0, concat_axis=0, tiled=True),
    )
    hidden_unit_grad, gate_weight_value, down_factor_grad, up_factor_grad = single_expert_backward(
        received_hidden, received_width, received_weight, lowering_maps[0], raising_maps[0]
    )
    back_h, back_g = (
        lax.all_to_all(hidden_unit_grad, ("tp", "ep"), split_axis=0, concat_axis=0, tiled=True),
        lax.all_to_all(gate_weight_value, ("tp", "ep"), split_axis=0, concat_axis=0, tiled=True),
    )
    entry_hidden = back_h[place].reshape(tok_rows, 2, width_h).astype(jnp.float32)
    gated_hidden_gradient = (entry_hidden[:, 0] + entry_hidden[:, 1]).astype(jnp.bfloat16)
    gates = back_g[place].reshape(tok_rows, 2)
    router_logit_gradient, term = router_term(
        specialist_pairs, weights, gates, dispatcher_map, experts
    )
    residual_input_gradient = (output_gradient.astype(jnp.float32) + term + attention_rows).astype(
        jnp.bfloat16
    )
    return (
        residual_input_gradient,
        gated_hidden_gradient,
        router_logit_gradient,
        down_factor_grad[None],
        up_factor_grad[None],
    )


def solution(mesh):
    in_specs = (
        P(("ep", "tp"), None),
        P(("ep", "tp"), None),
        P(("ep", "tp"), None),
        P(("ep", "tp"), None),
        P(("ep", "tp"), None, None),
        P(("ep", "tp"), None, None),
        P(),
        P("ep", "tp"),
        P("ep", "tp"),
        P("ep", "tp"),
        P("ep", "tp"),
        P(None, "tp"),
        P(None, "tp"),
        P(None, "tp"),
        P("ep", None),
    )
    out_specs = (
        P(("ep", "tp"), None),
        P(("ep", "tp"), None),
        P(("ep", "tp"), None),
        P(("ep", "tp"), None, None),
        P(("ep", "tp"), None, None),
    )
    return jax.shard_map(local, mesh=mesh, in_specs=in_specs, out_specs=out_specs, check_vma=False)
```

profile of v0, /device:TPU:68, one launch (start us, length us, event | category | flops | bytes accessed | tf_op | source)
XLA Modules:
  0.0 986.0 jit_solution(9344567126131691489)
XLA Ops:
  17.3 10.0 %all-to-all-start.3 = ((bf16[128,3,1]{1,2,0:T(2,128)(2,1)}), bf16[128,3,1]{1,2,0:T(2,128)(2,1)S(1)}, u32[]{:S(2)}, u32[]{:S(2)}) async-start(bf16[128,3,1]{1,2,0:T(2,128)(2,1)} %all_to_all.49), calls=%async_computation.4 | async-start | bytes 131072 | tf_op jit(solution)/shard_map/all_to_all | solution.py:174
  29.7 10.7 %gather_fusion = bf16[384,4608]{1,0:T(8,128)(2,1)} fusion(bf16[129,4608]{1,0:T(8,128)(2,1)} %concatenate.9, s32[1024]{0:T(1024)S(1)} %get-tuple-element.31), kind=kCustom, calls=%fused_computation | custom fusion | bytes 7079424 | tf_op jit(solution)/shard_map/gather | solution.py:167
  40.4 7.2 all_to_all.36
  47.7 10.2 %all-to-all-start = ((bf16[128,3,4608]{2,1,0:T(4,128)(2,1)}), bf16[128,3,4608]{2,1,0:T(4,128)(2,1)}, u32[]{:S(2)}, u32[]{:S(2)}) async-start(bf16[128,3,4608]{2,1,0:T(4,128)(2,1)} %all_to_all.36), calls=%async_computation | async-start | bytes 9437184 | tf_op jit(solution)/shard_map/all_to_all | solution.py:173
  57.8 5.0 concatenate.10
  62.9 45.4 %gather_fusion.1 = bf16[384,18432]{1,0:T(8,128)(2,1)} fusion(bf16[129,18432]{1,0:T(8,128)(2,1)} %concatenate.10, s32[1024]{0:T(1024)S(1)} %get-tuple-element.31), kind=kCustom, calls=%fused_computation.1 | custom fusion | bytes 28313088 | tf_op jit(solution)/shard_map/gather | solution.py:166
  108.2 19.5 %all_to_all.39 = bf16[128,3,18432]{2,1,0:T(4,128)(2,1)} reshape(bf16[384,18432]{1,0:T(8,128)(2,1)} %gather_fusion.1) | data formatting | bytes 28311552 | tf_op jit(solution)/shard_map/all_to_all | solution.py:172
  127.7 10.2 %all-to-all-start.1 = ((bf16[128,3,18432]{2,1,0:T(4,128)(2,1)}), bf16[128,3,18432]{2,1,0:T(4,128)(2,1)}, u32[]{:S(2)}, u32[]{:S(2)}) async-start(bf16[128,3,18432]{2,1,0:T(4,128)(2,1)} %all_to_all.39), calls=%async_computation.1 | async-start | bytes 37748736 | tf_op jit(solution)/shard_map/all_to_all | solution.py:172
  138.8 4.2 fusion.9
  143.0 6.4 fusion.3
  149.8 7.8 all_to_all.38
  157.6 3.2 fusion.35
  160.8 234.2 %all-to-all-done.1 = bf16[128,3,18432]{2,1,0:T(4,128)(2,1)} async-done(((bf16[128,3,18432]{2,1,0:T(4,128)(2,1)}), bf16[128,3,18432]{2,1,0:T(4,128)(2,1)}, u32[]{:S(2)}, u32[]{:S(2)}) %all-to-all-start.1) | async-done | bytes 14155808 | tf_op jit(solution)/shard_map/all_to_all | solution.py:172
  395.0 20.7 %all_to_all.41 = bf16[384,18432]{1,0:T(8,128)(2,1)} reshape(bf16[128,3,18432]{2,1,0:T(4,128)(2,1)} %all-to-all-done.1) | data formatting | bytes 28311552 | tf_op jit(solution)/shard_map/all_to_all | solution.py:172
  415.7 9.7 fusion.36
  427.6 12.5 %all-to-all-start.2 = ((bf16[128,3,1]{1,2,0:T(2,128)(2,1)}), bf16[128,3,1]{1,2,0:T(2,128)(2,1)S(1)}, u32[]{:S(2)}, u32[]{:S(2)}) async-start(bf16[128,3,1]{1,2,0:T(2,128)(2,1)} %convert_element_type.161), calls=%async_computation.2 | async-start | bytes 131072 | tf_op jit(solution)/shard_map/all_to_all | solution.py:181
  440.0 8.5 convolution_convert_fusion
  448.5 19.4 %all_to_all.46 = bf16[128,3,18432]{2,1,0:T(4,128)(2,1)} reshape(bf16[384,18432]{1,0:T(8,128)(2,1)} %convolution_convert_fusion) | data formatting | bytes 28311552 | tf_op jit(solution)/shard_map/all_to_all | solution.py:180
  468.0 10.2 %all-to-all-start.4 = ((bf16[128,3,18432]{2,1,0:T(4,128)(2,1)}), bf16[128,3,18432]{2,1,0:T(4,128)(2,1)}, u32[]{:S(2)}, u32[]{:S(2)}) async-start(bf16[128,3,18432]{2,1,0:T(4,128)(2,1)} %all_to_all.46), calls=%async_computation.5 | async-start | bytes 37748736 | tf_op jit(solution)/shard_map/all_to_all | solution.py:180
  478.2 7.8 fusion.13
  488.8 7.9 fusion.83
  496.8 14.7 %fusion.34 = f32[1024,4608]{1,0:T(8,128)} fusion(bf16[4608,128]{1,0:T(8,128)(2,1)} %param.27, bf16[2,1024,1024]{1,2,0:T(8,128)(2,1)} %copy-done.3, bf16[1024,256]{1,0:T(8,128)(2,1)} %param.22), kind=kOutput, calls=%fused_computation.48 | convolution fusion | flops 1745092608 | bytes 24772608 | tf_op jit(solution)/shard_map/te,de->td/dot_general | solution.py:67
  511.5 21.5 %add_convert_fusion = bf16[1024,4608]{1,0:T(8,128)(2,1)} fusion(f32[1024,4608]{1,0:T(8,128)} %fusion.83, f32[1024,4608]{1,0:T(8,128)} %fusion.34, bf16[4608,128]{1,0:T(8,128)(2,1)} %param.28, f32[2,1024]{1,0:T(2,128)S(1)} %get-tuple-element.26, f32[1024,1024,2]{1,0,2:T(8,128)} %copy-done.2, pred[1024,1024]{0,1:T(8,128)(4,1)S(1)} %fusion.17, ...), kind=kOutput, calls=%fused_computation.9 | convolution fusion | flops 1769603072 | bytes 58335232 | tf_op jit(solution)/shard_map/te,de->td/dot_general | solution.py:68
  533.7 3.4 fusion.11
  537.1 8.6 fusion
  549.1 324.0 %all-to-all-done.4 = bf16[128,3,18432]{2,1,0:T(4,128)(2,1)} async-done(((bf16[128,3,18432]{2,1,0:T(4,128)(2,1)}), bf16[128,3,18432]{2,1,0:T(4,128)(2,1)}, u32[]{:S(2)}, u32[]{:S(2)}) %all-to-all-start.4) | async-done | bytes 14155808 | tf_op jit(solution)/shard_map/all_to_all | solution.py:180
  873.1 20.8 %all_to_all.48 = bf16[384,18432]{1,0:T(8,128)(2,1)} reshape(bf16[128,3,18432]{2,1,0:T(4,128)(2,1)} %all-to-all-done.4) | data formatting | bytes 28311552 | tf_op jit(solution)/shard_map/all_to_all | solution.py:180
  893.9 25.3 %gather_fusion.4 = bf16[256,18432]{1,0:T(8,128)(2,1)} fusion(bf16[384,18432]{1,0:T(8,128)(2,1)} %all_to_all.48, s32[1024]{0:T(1024)S(1)} %pad_clamp_fusion.1), kind=kCustom, calls=%fused_computation.4 | custom fusion | bytes 18875392 | tf_op jit(solution)/shard_map/gather | solution.py:183
  919.2 19.5 %reshape.304 = f32[128,2,18432]{2,1,0:T(2,128)} reshape(bf16[256,18432]{1,0:T(8,128)(2,1)} %gather_fusion.4) | data formatting | bytes 28311552 | tf_op jit(solution)/shard_map/convert_element_type | solution.py:183
  938.7 23.3 %fusion.82 = (f32[128,1,18432]{2,1,0:T(1,128)}, f32[128,1,18432]{2,1,0:T(1,128)}) fusion(f32[128,2,18432]{2,1,0:T(2,128)} %reshape.304), kind=kLoop, calls=%fused_computation.119 | loop fusion | bytes 37748736 | tf_op jit(solution)/shard_map/slice | solution.py:184
  962.0 13.7 %fusion.12 = bf16[128,18432]{1,0:T(8,128)(2,1)} fusion(f32[128,1,18432]{2,1,0:T(1,128)} %get-tuple-element.23, f32[128,1,18432]{2,1,0:T(1,128)} %get-tuple-element.22), kind=kLoop, calls=%fused_computation.30 | loop fusion | flops 4718592 | bytes 23592960 | tf_op jit(solution)/shard_map/convert_element_type | solution.py:184
  975.7 3.2 fusion.7
  (82 shorter events, 22.7 us)
Async XLA Ops:
  7.2 481.7 %copy-start = (bf16[4608,256]{1,0:T(8,128)(2,1)S(1)}, bf16[4608,256]{1,0:T(8,128)(2,1)}, u32[]{:S(2)}) copy-start(bf16[4608,256]{1,0:T(8,128)(2,1)} %param.26) | copy-start | bytes 7077892
  11.9 1.4 copy-start.10
  17.3 30.3 %all-to-all-start.3 = ((bf16[128,3,1]{1,2,0:T(2,128)(2,1)}), bf16[128,3,1]{1,2,0:T(2,128)(2,1)S(1)}, u32[]{:S(2)}, u32[]{:S(2)}) async-start(bf16[128,3,1]{1,2,0:T(2,128)(2,1)} %all_to_all.49), calls=%async_computation.4 | async-start | bytes 131072 | tf_op jit(solution)/shard_map/all_to_all | solution.py:174
  47.7 80.1 %all-to-all-start = ((bf16[128,3,4608]{2,1,0:T(4,128)(2,1)}), bf16[128,3,4608]{2,1,0:T(4,128)(2,1)}, u32[]{:S(2)}, u32[]{:S(2)}) async-start(bf16[128,3,4608]{2,1,0:T(4,128)(2,1)} %all_to_all.36), calls=%async_computation | async-start | bytes 9437184 | tf_op jit(solution)/shard_map/all_to_all | solution.py:173
  127.7 10.2 %copy-start.15 = (s32[1,8]{1,0:T(1,128)S(1)}, s32[1,8]{1,0:T(1,128)}, u32[]{:S(2)}) copy-start(s32[1,8]{1,0:T(1,128)} %param.29) | copy-start | bytes 100
  127.7 267.3 %all-to-all-start.1 = ((bf16[128,3,18432]{2,1,0:T(4,128)(2,1)}), bf16[128,3,18432]{2,1,0:T(4,128)(2,1)}, u32[]{:S(2)}, u32[]{:S(2)}) async-start(bf16[128,3,18432]{2,1,0:T(4,128)(2,1)} %all_to_all.39), calls=%async_computation.1 | async-start | bytes 37748736 | tf_op jit(solution)/shard_map/all_to_all | solution.py:172
  138.8 4.3 copy-start.5
  138.8 4.3 copy-start.13
  143.0 6.4 copy-start.2
  415.7 9.7 copy-start.1
  415.7 9.7 copy-start.6
  427.6 40.4 %all-to-all-start.2 = ((bf16[128,3,1]{1,2,0:T(2,128)(2,1)}), bf16[128,3,1]{1,2,0:T(2,128)(2,1)S(1)}, u32[]{:S(2)}, u32[]{:S(2)}) async-start(bf16[128,3,1]{1,2,0:T(2,128)(2,1)} %convert_element_type.161), calls=%async_computation.2 | async-start | bytes 131072 | tf_op jit(solution)/shard_map/all_to_all | solution.py:181
  468.0 10.2 %copy-start.8 = (f32[2,1024]{1,0:T(2,128)S(1)}, f32[2,1024]{1,0:T(2,128)}, u32[]{:S(2)}) copy-start(f32[2,1024]{1,0:T(2,128)} %get-tuple-element.28) | copy-start | bytes 24580
  468.0 405.1 %all-to-all-start.4 = ((bf16[128,3,18432]{2,1,0:T(4,128)(2,1)}), bf16[128,3,18432]{2,1,0:T(4,128)(2,1)}, u32[]{:S(2)}, u32[]{:S(2)}) async-start(bf16[128,3,18432]{2,1,0:T(4,128)(2,1)} %all_to_all.46), calls=%async_computation.5 | async-start | bytes 37748736 | tf_op jit(solution)/shard_map/all_to_all | solution.py:180
  478.2 497.6 %reduce-scatter.2.cloned.1.call-start = ((), (), s32[]{:S(2)}) async-start(), calls=%async_computation.6 | async-start | bytes 10616832 | tf_op jit(solution)/shard_map/reduce_scatter | solution.py:154
  478.2 9.8 copy-start.14
  486.0 2.0 copy-start.3
  533.0 0.7 copy-start.11
  537.1 11.2 %copy-start.7 = (f32[128,2]{0,1:T(2,128)S(1)}, f32[128,2]{0,1:T(2,128)}, u32[]{:S(2)}) copy-start(f32[128,2]{0,1:T(2,128)} %get-tuple-element.21) | copy-start | bytes 3076
  537.1 11.2 %copy-start.9 = (s32[128,2]{0,1:T(2,128)S(1)}, s32[128,2]{0,1:T(2,128)}, u32[]{:S(2)}) copy-start(s32[128,2]{0,1:T(2,128)} %param.17) | copy-start | bytes 3076
  548.3 345.6 %copy-start.12 = (f32[128,2]{0,1:T(2,128)}, f32[128,2]{0,1:T(2,128)S(1)}, u32[]{:S(2)}) copy-start(f32[128,2]{0,1:T(2,128)S(1)} %subtract_multiply_fusion) | copy-start | bytes 3076
  962.0 13.7 %copy-start.4 = (bf16[128,4608]{1,0:T(8,128)(2,1)S(1)}, bf16[128,4608]{1,0:T(8,128)(2,1)}, u32[]{:S(2)}) copy-start(bf16[128,4608]{1,0:T(8,128)(2,1)} %param.16) | copy-start | bytes 3538948
Sparse Core Ops, SparseCore 0:
  533.1 355.9 reduce-scatter.1
where the time goes:
time: 996 us; the launch traced here: 986 us
  waiting for transfers between devices  558 us (56%)
  local copies, waits for them, and re-layouts  240 us (24%)
  matrix products  93.3 us (9%)
  starting transfers between devices  53 us (5%)
  other arithmetic  26.7 us (3%)
  between operations  14.7 us (1%)
    all_to_all x1, waiting for transfers between devices, local(): lax.all_to_all(hidden_unit_grad, ('tp', 'ep'), split_axis=0, concat_axis=...  324 us
    all_to_all x1, waiting for transfers between devices, local(): lax.all_to_all(send_h, ('tp', 'ep'), split_axis=0, concat_axis=0, tiled=T...  234 us
    gather x1, local copies, waits for them, and re-layouts, local(): jnp.concatenate([hidden, jnp.zeros((1, width_h), jnp.bfloat16)], axis=0)  45.4 us
    all_to_all x2, local copies, waits for them, and re-layouts, local(): lax.all_to_all(hidden_unit_grad, ('tp', 'ep'), split_axis=0, concat_axis=...  40.2 us
    all_to_all x2, local copies, waits for them, and re-layouts, local(): lax.all_to_all(send_h, ('tp', 'ep'), split_axis=0, concat_axis=0, tiled=T...  40.2 us
    gather x1, local copies, waits for them, and re-layouts, local(): back_h[place].reshape(tok_rows, 2, width_h).astype(jnp.float32)  25.3 us
    slice x1, local copies, waits for them, and re-layouts, local(): entry_hidden[:, 0] + entry_hidden[:, 1]  23.3 us
    dot_general x1, matrix products, attend_backward(): jnp.einsum('te,de->td', dvalue, value_projection, preferred_element_type=...  21.5 us
  transfers between devices with their start and end apart: 6, of which 2 were waited for; matrix products, arithmetic and copies ran while one was open for 24% of the time, Pallas kernels for 0%

commit v1 on v0

v1 whole, which is shorter than its diff:
```python
import jax
import jax.numpy as jnp
from jax import lax
from jax.experimental import pallas as pl
from jax.experimental.pallas import tpu as pltpu
from jax.sharding import Mesh, PartitionSpec as P

HD = 128
RANK = 32
PLANE = ("xl", "xh", "z", "c")
LINE = "y"
TP = ("y", "xl")
EP = ("xh", "z", "c")
ROWS = ("xh", "z", "c", "y", "xl")

SLICES = 32
WIDTH = 768
HWIDE = 640

adapter_scale = 2.0
score_cap = 50.0
query_scale = 144.0 ** (-0.5)
F32 = jnp.float32
BF16 = jnp.bfloat16
VMEM = 60 * 1024 * 1024


def attend_backward(
    queries,
    keys,
    values,
    context_gradient,
    lengths,
    query_projection,
    key_projection,
    value_projection,
):
    rows = queries.shape[0]
    kv_count = keys.shape[1] // HD
    group = queries.shape[1] // keys.shape[1]
    query4 = queries.reshape(rows, kv_count, group, HD)
    ctx4 = context_gradient.reshape(rows, kv_count, group, HD)
    key3 = keys.reshape(rows, kv_count, HD)
    value3 = values.reshape(rows, kv_count, HD)
    places = jnp.arange(rows, dtype=jnp.int32)
    bounds = jnp.cumsum(lengths)
    docs = jnp.sum((places[:, None] >= bounds[None, :]).astype(jnp.int32), axis=1)
    allowed = (docs[:, None] == docs[None, :]) & (places[:, None] >= places[None, :])
    raw = (
        jnp.einsum("ikgd,jkd->kgij", query4, key3, preferred_element_type=jnp.float32) * query_scale
    )
    bent = jnp.tanh(raw / score_cap)
    expo = jnp.where(allowed, jnp.exp(score_cap * bent), 0.0)
    probs = expo / jnp.sum(expo, axis=-1, keepdims=True)
    dprobs = jnp.einsum("ikgd,jkd->kgij", ctx4, value3, preferred_element_type=jnp.float32)
    dsoft = probs * (dprobs - jnp.sum(probs * dprobs, axis=-1, keepdims=True))
    dscore = (dsoft * (1.0 - bent * bent)).astype(jnp.bfloat16)
    probs_b = probs.astype(jnp.bfloat16)
    dquery = (
        (
            jnp.einsum("kgij,jkd->ikgd", dscore, key3, preferred_element_type=jnp.float32)
            * query_scale
        )
        .astype(jnp.bfloat16)
        .reshape(rows, -1)
    )
    dkey = (
        (
            jnp.einsum("kgij,ikgd->jkd", dscore, query4, preferred_element_type=jnp.float32)
            * query_scale
        )
        .astype(jnp.bfloat16)
        .reshape(rows, -1)
    )
    dvalue = (
        jnp.einsum("kgij,ikgd->jkd", probs_b, ctx4, preferred_element_type=jnp.float32)
        .astype(jnp.bfloat16)
        .reshape(rows, -1)
    )
    grads = jnp.concatenate([dquery, dkey, dvalue], axis=1)
    maps = jnp.concatenate([query_projection, key_projection, value_projection], axis=1)
    return jnp.einsum("te,de->td", grads, maps, preferred_element_type=jnp.float32)


def lanes_of(shape):
    return lax.broadcasted_iota(jnp.int32, shape, len(shape) - 1)


def pack_kernel(hm_ref, hr_ref, gm_ref, gr_ref, id_ref, out_ref):
    rows = hm_ref.shape[0]
    lane = lanes_of((rows, 128))
    ids = id_ref[...]
    extra = gr_ref[...].astype(F32)
    extra = jnp.where(pl.program_id(0) % 2 == 0, extra, pltpu.roll(extra, 64, 1))
    for q in range(4):
        out_ref[q, :, 0:512] = hm_ref[:, 512 * q : 512 * q + 512]
        hid = hr_ref[:, 128 * (q // 2) : 128 * (q // 2) + 128].astype(F32)
        if q % 2:
            hid = pltpu.roll(hid, 64, 1)
        grad = pltpu.roll(extra, 64 - 16 * q, 1)
        tail = jnp.where(lane < 64, hid, jnp.where(lane < 80, grad, ids))
        out_ref[q, :, 512:640] = tail.astype(BF16)
        out_ref[q, :, 640:768] = gm_ref[:, 128 * q : 128 * q + 128]


def pack(hid, grad, ids):
    rows = hid.shape[0]
    return pl.pallas_call(
        pack_kernel,
        grid=(8,),
        in_specs=[
            pl.BlockSpec((rows, 2048), lambda i: (0, i)),
            pl.BlockSpec((rows, 256), lambda i: (0, 64 + i)),
            pl.BlockSpec((rows, 512), lambda i: (0, i)),
            pl.BlockSpec((rows, 128), lambda i: (0, 32 + i // 2)),
            pl.BlockSpec((rows, 128), lambda i: (0, 0)),
        ],
        out_specs=pl.BlockSpec((4, rows, WIDTH), lambda i: (i, 0, 0)),
        out_shape=jax.ShapeDtypeStruct((SLICES, rows, WIDTH), BF16),
        compiler_params=pltpu.CompilerParams(vmem_limit_bytes=VMEM),
        cost_estimate=pl.CostEstimate(
            flops=rows * 2 * 24576, bytes_accessed=rows * 2 * 49152, transcendentals=0
        ),
        name="pack_slices",
    )(hid, hid, grad, grad, ids)


def unpack_kernel(main_ref, rem_ref, out_ref):
    @pl.when(pl.program_id(0) < 8)
    def _():
        for q in range(4):
            out_ref[:, 512 * q : 512 * q + 512] = main_ref[q]

    @pl.when(pl.program_id(0) == 8)
    def _():
        lane = lanes_of(rem_ref.shape[1:])
        for d in range(16):
            low = rem_ref[2 * d].astype(F32)
            high = pltpu.roll(rem_ref[2 * d + 1].astype(F32), 64, 1)
            out_ref[:, 128 * d : 128 * d + 128] = jnp.where(lane < 64, low, high).astype(BF16)


def unpack(blocks):
    rows = blocks.shape[1]
    return pl.pallas_call(
        unpack_kernel,
        grid=(9,),
        in_specs=[
            pl.BlockSpec((4, rows, 512), lambda i: (jnp.minimum(i, 7), 0, 0)),
            pl.BlockSpec((SLICES, rows, 128), lambda i: (0, 0, 4)),
        ],
        out_specs=pl.BlockSpec((rows, 2048), lambda i: (0, i)),
        out_shape=jax.ShapeDtypeStruct((rows, 18432), BF16),
        compiler_params=pltpu.CompilerParams(vmem_limit_bytes=VMEM),
        cost_estimate=pl.CostEstimate(
            flops=rows * 18432, bytes_accessed=rows * 4 * 19000, transcendentals=0
        ),
        name="unpack_slices",
    )(blocks, blocks)


def fold_matrix(k):
    r = lax.broadcasted_iota(jnp.int32, (128, 128), 0)
    c = lax.broadcasted_iota(jnp.int32, (128, 128), 1)
    return (c == r % RANK + RANK * k).astype(F32).astype(BF16)


def spread_matrix(k):
    r = lax.broadcasted_iota(jnp.int32, (128, 128), 0)
    c = lax.broadcasted_iota(jnp.int32, (128, 128), 1)
    return (r == c % RANK + RANK * k).astype(F32).astype(BF16)


def contract_kernel(x_ref, w_ref, id_ref, out_ref, h_ref, g_ref, a0, a1, b0, b1):
    rows = x_ref.shape[0]
    step = 512
    lane = lanes_of((rows, 128))
    tail = x_ref[:, 512:640]
    zero = jnp.zeros_like(tail)
    h_ref[:, 0:512] = x_ref[:, 0:512]
    h_ref[:, 512:640] = jnp.where(lane < 64, tail, zero)
    g_ref[:, 0:128] = jnp.where((lane >= 64) & (lane < 80), tail, zero)
    g_ref[:, 128:256] = x_ref[:, 640:768]
    for acc in (a0, a1, b0, b1):
        acc[...] = jnp.zeros_like(acc)
    e0 = id_ref[:, 0:1] - lane // RANK
    e1 = id_ref[:, 1:2] - lane // RANK
    dims = (((1,), (1,)), ((), ()))

    def body(n, carry):
        start = pl.multiple_of(n * step, step)
        w_h = w_ref[pl.ds(start, step), 0:640]
        w_g = w_ref[pl.ds(start, step), 512:768]
        z = lax.dot_general(h_ref[...], w_h, dims, preferred_element_type=F32)
        p = lax.dot_general(g_ref[...], w_g, dims, preferred_element_type=F32)
        for refs, part in (((a0, a1), z), ((b0, b1), p)):
            for ref, e in zip(refs, (e0, e1)):
                acc = ref[...]
                for j in range(step // 128):
                    here = e == n * (step // RANK) + 4 * j
                    acc = jnp.where(here, part[:, 128 * j : 128 * j + 128], acc)
                ref[...] = acc
        return carry

    lax.fori_loop(0, w_ref.shape[0] // step, body, 0)
    out = jnp.zeros((rows, 128), F32)
    for k, acc in enumerate((a0, b0, a1, b1)):
        out += jnp.dot(acc[...].astype(BF16), fold_matrix(k), preferred_element_type=F32)
    out_ref[...] = out.astype(BF16)


def contract(x, w, ids):
    rows, tile = x.shape[0], 512
    return pl.pallas_call(
        contract_kernel,
        grid=(rows // tile,),
        in_specs=[
            pl.BlockSpec((tile, WIDTH), lambda i: (i, 0)),
            pl.BlockSpec(w.shape, lambda i: (0, 0)),
            pl.BlockSpec((tile, 2), lambda i: (i, 0)),
        ],
        out_specs=pl.BlockSpec((tile, 128), lambda i: (i, 0)),
        out_shape=jax.ShapeDtypeStruct((rows, 128), BF16),
        scratch_shapes=[pltpu.VMEM((tile, HWIDE), BF16), pltpu.VMEM((tile, 256), BF16)]
        + [pltpu.VMEM((tile, 128), F32)] * 4,
        compiler_params=pltpu.CompilerParams(vmem_limit_bytes=VMEM),
        cost_estimate=pl.CostEstimate(
            flops=2 * rows * w.shape[0] * 1024,
            bytes_accessed=2 * (rows + w.shape[0]) * WIDTH,
            transcendentals=0,
        ),
        name="contract_experts",
    )(x, w, ids)


def factors_kernel(x_ref, dt_ref, it_ref, out_ref, acc_h, acc_g):
    tile, total = out_ref.shape[0], x_ref.shape[0]
    step = 1024
    acc_h[...] = jnp.zeros_like(acc_h)
    acc_g[...] = jnp.zeros_like(acc_g)
    first = pl.program_id(0) * (tile // RANK)

    def body(n, carry):
        start = pl.multiple_of(n * step, step)
        at = pl.ds(start, step)
        e0, e1 = it_ref[0:1, at], it_ref[1:2, at]
        d0, w0 = dt_ref[0:32, at], dt_ref[32:64, at]
        d1, w1 = dt_ref[64:96, at], dt_ref[96:128, at]
        d_parts, w_parts = [], []
        for j in range(tile // RANK):
            m0, m1 = e0 == first + j, e1 == first + j
            d_parts.append(jnp.where(m0, d0, jnp.where(m1, d1, 0.0)).astype(BF16))
            w_parts.append(jnp.where(m0, w0, jnp.where(m1, w1, 0.0)).astype(BF16))
        d_all = jnp.concatenate(d_parts, axis=0)
        w_all = jnp.concatenate(w_parts, axis=0)
        acc_h[...] += jnp.dot(d_all, x_ref[at, 0:640], preferred_element_type=F32)
        acc_g[...] += jnp.dot(w_all, x_ref[at, 512:768], preferred_element_type=F32)
        return carry

    lax.fori_loop(0, total // step, body, 0)
    lane = lanes_of((tile, 128))
    out_ref[:, 0:512] = acc_h[:, 0:512].astype(BF16)
    out_ref[:, 512:640] = jnp.where(lane < 64, acc_h[:, 512:640], acc_g[:, 0:128]).astype(BF16)
    out_ref[:, 640:768] = acc_g[:, 128:256].astype(BF16)


def factors(x, dt, it, columns):
    tile = 512
    return pl.pallas_call(
        factors_kernel,
        grid=(columns // tile,),
        in_specs=[
            pl.BlockSpec(x.shape, lambda i: (0, 0)),
            pl.BlockSpec(dt.shape, lambda i: (0, 0)),
            pl.BlockSpec(it.shape, lambda i: (0, 0)),
        ],
        out_specs=pl.BlockSpec((tile, WIDTH), lambda i: (i, 0)),
        out_shape=jax.ShapeDtypeStruct((columns, WIDTH), BF16),
        scratch_shapes=[pltpu.VMEM((tile, HWIDE), F32), pltpu.VMEM((tile, 256), F32)],
        compiler_params=pltpu.CompilerParams(vmem_limit_bytes=VMEM),
        cost_estimate=pl.CostEstimate(
            flops=2 * x.shape[0] * columns * 1024,
            bytes_accessed=2 * (x.shape[0] + columns) * WIDTH,
            transcendentals=0,
        ),
        name="factor_gradients",
    )(x, dt, it)


def expand_kernel(d_ref, w_ref, id_ref, out_ref, acc):
    rows = d_ref.shape[0]
    step = 512
    lane = lanes_of((rows, 128))
    e0 = id_ref[:, 0:1] - lane // RANK
    e1 = id_ref[:, 1:2] - lane // RANK
    d0 = jnp.dot(d_ref[...], spread_matrix(0), preferred_element_type=F32)
    d1 = jnp.dot(d_ref[...], spread_matrix(2), preferred_element_type=F32)
    acc[...] = jnp.zeros_like(acc)

    def body(n, carry):
        start = pl.multiple_of(n * step, step)
        parts = []
        for j in range(step // 128):
            at = n * (step // RANK) + 4 * j
            parts.append(jnp.where(e0 == at, d0, jnp.where(e1 == at, d1, 0.0)).astype(BF16))
        spread = jnp.concatenate(parts, axis=1)
        acc[...] += jnp.dot(spread, w_ref[pl.ds(start, step), 0:640], preferred_element_type=F32)
        return carry

    lax.fori_loop(0, w_ref.shape[0] // step, body, 0)
    out_ref[...] = acc[...].astype(BF16)


def expand(d, w, ids):
    rows, tile = d.shape[0], 512
    return pl.pallas_call(
        expand_kernel,
        grid=(rows // tile,),
        in_specs=[
            pl.BlockSpec((tile, 128), lambda i: (i, 0)),
            pl.BlockSpec(w.shape, lambda i: (0, 0)),
            pl.BlockSpec((tile, 2), lambda i: (i, 0)),
        ],
        out_specs=pl.BlockSpec((tile, HWIDE), lambda i: (i, 0)),
        out_shape=jax.ShapeDtypeStruct((rows, HWIDE), BF16),
        scratch_shapes=[pltpu.VMEM((tile, HWIDE), F32)],
        compiler_params=pltpu.CompilerParams(vmem_limit_bytes=VMEM),
        cost_estimate=pl.CostEstimate(
            flops=2 * rows * w.shape[0] * HWIDE,
            bytes_accessed=2 * (rows + w.shape[0]) * WIDTH,
            transcendentals=0,
        ),
        name="expand_entries",
    )(d, w, ids)


def router_term(specialist_pairs, weights, gates, dispatcher_map, experts):
    gate_val = gates.astype(jnp.float32)
    router_logit_gradient = weights * (
        gate_val - jnp.sum(weights * gate_val, axis=-1, keepdims=True)
    )
    ids = jnp.arange(experts, dtype=jnp.int32)
    expert_table = jnp.sum(
        jnp.where(
            specialist_pairs[:, :, None] == ids[None, None, :],
            router_logit_gradient[:, :, None],
            0.0,
        ),
        axis=1,
    )
    expert_table = expert_table.astype(jnp.bfloat16)
    term = jnp.einsum("te,de->td", expert_table, dispatcher_map, preferred_element_type=jnp.float32)
    return (router_logit_gradient, term)


def exchange(x, axes):
    return lax.all_to_all(x, axes, split_axis=0, concat_axis=0, tiled=True)


def local(
    hidden,
    output_gradient,
    specialist_pairs,
    chosen_router_logits,
    lowering_maps,
    raising_maps,
    dispatcher_map,
    queries,
    keys,
    values,
    context_gradient,
    query_projection,
    key_projection,
    value_projection,
    lengths,
):
    tok_rows = hidden.shape[0]
    width_d = output_gradient.shape[1]
    experts = 128
    tokens = tok_rows * SLICES
    columns = experts * RANK
    place = specialist_pairs % 8 * 16 + specialist_pairs // 8
    lane = jnp.arange(128, dtype=jnp.int32)[None, :]
    id_lanes = jnp.where(lane == 80, place[:, 0:1], jnp.where(lane == 81, place[:, 1:2], 0))
    w_mine = pack(lowering_maps[0].T, raising_maps[0], jnp.zeros((RANK, 128), F32))
    w_rows = exchange(w_mine, PLANE).reshape(SLICES * RANK, WIDTH)
    w_all = lax.all_gather(w_rows, LINE, axis=0, tiled=True)
    x_mine = pack(hidden, output_gradient, id_lanes.astype(F32))
    x = exchange(x_mine, PLANE).reshape(tokens, WIDTH)
    ids = x[:, 592:594].astype(jnp.int32)

    part = attend_backward(
        queries,
        keys,
        values,
        context_gradient,
        lengths[0],
        query_projection,
        key_projection,
        value_projection,
    ).astype(BF16)

    sums = contract(x, w_all, ids)
    sums = exchange(sums.reshape(SLICES, tok_rows, 128), PLANE).astype(F32)
    sums = jnp.sum(sums, axis=0)
    attention = exchange(part.reshape(8, tok_rows, width_d), TP)

    weights = jax.nn.softmax(chosen_router_logits, axis=-1)
    weights_b = weights.astype(BF16).astype(F32)
    sent, gates = [], []
    for k in range(2):
        z = sums[:, 64 * k : 64 * k + 32].astype(BF16).astype(F32)
        p = sums[:, 64 * k + 32 : 64 * k + 64]
        w = weights_b[:, k : k + 1]
        gates.append(jnp.sum(adapter_scale * z * p, axis=-1, keepdims=True).astype(BF16))
        sent.append((adapter_scale * w * p).astype(BF16))
        sent.append(adapter_scale * (w * z).astype(BF16))
    d = lax.all_gather(jnp.concatenate(sent, axis=1), PLANE, axis=0, tiled=True)
    gates = jnp.concatenate(gates, axis=1)

    factor_part = factors(x, d.T.astype(F32), jnp.pad(ids.T, ((0, 6), (0, 0))), columns)
    factor_rows = lax.psum_scatter(factor_part, LINE, scatter_dimension=0, tiled=True)
    hidden_part = expand(d, w_all, ids)
    hidden_back = exchange(hidden_part.reshape(SLICES, tok_rows, HWIDE), PLANE)
    factor_back = exchange(factor_rows.reshape(SLICES, RANK, WIDTH), PLANE)

    gated_hidden_gradient = unpack(hidden_back)
    down_factor_grad = unpack(factor_back).T
    up_main = factor_back[:, :, 640:768].transpose(1, 0, 2).reshape(RANK, 4096)
    up_rest = factor_back[:, :, 576:592].transpose(1, 0, 2).reshape(RANK, 512)
    up_factor_grad = jnp.concatenate([up_main, up_rest], axis=1)

    router_logit_gradient, term = router_term(
        specialist_pairs, weights, gates, dispatcher_map, experts
    )
    attention_rows = jnp.sum(attention.astype(F32), axis=0)
    residual_input_gradient = (output_gradient.astype(jnp.float32) + term + attention_rows).astype(
        jnp.bfloat16
    )
    return (
        residual_input_gradient,
        gated_hidden_gradient,
        router_logit_gradient,
        down_factor_grad[None],
        up_factor_grad[None],
    )


def solution(mesh):
    fine = Mesh(mesh.devices.reshape(4, 2, 2, 4, 2), ("y", "xl", "xh", "z", "c"))
    rows2, rows3, heads = P(ROWS, None), P(ROWS, None, None), P(EP, TP)
    in_specs = (
        rows2,
        rows2,
        rows2,
        rows2,
        rows3,
        rows3,
        P(),
        heads,
        heads,
        heads,
        heads,
        P(None, TP),
        P(None, TP),
        P(None, TP),
        P(EP, None),
    )
    out_specs = (rows2, rows2, rows2, rows3, rows3)
    return jax.shard_map(local, mesh=fine, in_specs=in_specs, out_specs=out_specs, check_vma=False)
```

time: 996 us -> 496 us (0.50)
  the two profiles are of different devices: /device:TPU:68 before, /device:TPU:1 now
where the time goes in v1:
time: 496 us; the launch traced here: 494 us
  Pallas kernels  177 us (36%)
  waiting for transfers between devices  119 us (24%)
  blocking collectives  99.7 us (20%)
  matrix products  32 us (6%)
  starting transfers between devices  27 us (5%)
  other arithmetic  19.6 us (4%)
  between operations  14.2 us (3%)
  local copies, waits for them, and re-layouts  5.42 us (1%)
    all_to_all x2, blocking collectives, exchange(): return lax.all_to_all(x, axes, split_axis=0, concat_axis=0, tiled=True)  99.7 us
    all_to_all x4, waiting for transfers between devices, exchange(): return lax.all_to_all(x, axes, split_axis=0, concat_axis=0, tiled=True)  81.2 us
    pallas_call x1, Pallas kernels, contract(): pl.pallas_call(contract_kernel, grid=(rows // tile,), in_specs=[pl.BlockS...  57.3 us
    pallas_call x1, Pallas kernels, factors(): pl.pallas_call(factors_kernel, grid=(columns // tile,), in_specs=[pl.Bloc...  47.8 us
    pallas_call x1, Pallas kernels, expand(): pl.pallas_call(expand_kernel, grid=(rows // tile,), in_specs=[pl.BlockSpe...  45.1 us
    all_gather x1, waiting for transfers between devices, local(): d = lax.all_gather(jnp.concatenate(sent, axis=1), PLANE, axis=0, tiled=True)  37.8 us
    all_to_all x4, starting transfers between devices, exchange(): return lax.all_to_all(x, axes, split_axis=0, concat_axis=0, tiled=True)  26.7 us
    pallas_call x2, Pallas kernels, pack(): pl.pallas_call(pack_kernel, grid=(8,), in_specs=[pl.BlockSpec((rows, 2048...  14.1 us
  transfers between devices with their start and end apart: 7, of which 4 were waited for; matrix products, arithmetic and copies ran while one was open for 11% of the time, Pallas kernels for 22%

profile of v1, /device:TPU:1, one launch (start us, length us, event | category | flops | bytes accessed | tf_op | source)
XLA Modules:
  0.0 494.2 jit_solution(18244916591391721004)
XLA Ops:
  7.8 5.9 %pack_slices.3 = bf16[32,32,768]{2,1,0:T(8,128)(2,1)} custom-call(bf16[32,18432]{1,0:T(8,128)(2,1)} %bitcast.139, bf16[32,18432]{1,0:T(8,128)(2,1)} %bitcast.140, bf16[32,4608]{1,0:T(8,128)(2,1)} %bitcast.142, bf16[32,4608]{1,0:T(8,128)(2,1)} %bitcast.143, f32[32,128]{1,0:T(8,128)} %broadcast_in_dim.93.id_ref), custom_call_target="tpu_custom_call" | custom-call | flops 1572864 | bytes 3145728 | tf_op jit(solution)/shard_map/pack_slices/pallas_call | solution.py:108
  13.8 32.6 %all_to_all.30 = bf16[32,32,768]{2,1,0:T(8,128)(2,1)} all-to-all(bf16[32,32,768]{2,1,0:T(8,128)(2,1)} %pack_slices.3), channel_id=1, replica_groups=mesh['y'=4,'xl'=2,'xh'=2,'z'=4,'c'=2] {'xl','xh','z','c'}, dimensions={0} | all-to-all | bytes 3145728 | tf_op jit(solution)/shard_map/all_to_all | solution.py:357
  46.4 0.7 select_convert_fusion.id_ref
  47.1 8.2 %pack_slices.2 = bf16[32,128,768]{2,1,0:T(8,128)(2,1)} custom-call(bf16[128,18432]{1,0:T(8,128)(2,1)} %hr_ref.1, bf16[128,18432]{1,0:T(8,128)(2,1)} %hr_ref.1, bf16[128,4608]{1,0:T(8,128)(2,1)} %gr_ref.1, bf16[128,4608]{1,0:T(8,128)(2,1)} %gr_ref.1, f32[128,128]{1,0:T(8,128)} %select_convert_fusion.id_ref), custom_call_target="tpu_custom_call" | custom-call | flops 6291456 | bytes 12582912 | tf_op jit(solution)/shard_map/pack_slices/pallas_call | solution.py:108
  55.3 4.8 all-to-all-start
  61.6 4.2 fusion.6
  65.9 3.7 fusion.1
  69.6 5.1 %fusion.12 = bf16[2,1024,1024]{1,2,0:T(8,128)(2,1)} fusion(f32[1024,1024,2]{1,0,2:T(8,128)S(1)} %get-tuple-element.22, f32[1024,1024,2]{1,0,2:T(8,128)S(1)} %get-tuple-element.24, f32[2,1024]{1,0:T(2,128)S(1)} %get-tuple-element.23, f32[2,1024]{1,0:T(2,128)S(1)} %get-tuple-element.21, pred[1024,1024]{0,1:T(8,128)(4,1)S(1)} %fusion.16), kind=kLoop, calls=%fused_computation.20 | loop fusion | flops 20971520 | bytes 22036480 | tf_op jit(solution)/shard_map/reshape.13
  74.7 64.3 %all-to-all-done = bf16[32,128,768]{2,1,0:T(8,128)(2,1)} async-done(((bf16[32,128,768]{2,1,0:T(8,128)(2,1)}), bf16[32,128,768]{2,1,0:T(8,128)(2,1)}, u32[]{:S(2)}, u32[]{:S(2)}) %all-to-all-start) | async-done | bytes 6291488 | tf_op jit(solution)/shard_map/all_to_all | solution.py:357
  139.1 3.0 slice_convert_fusion.id_ref
  142.1 57.3 %contract_experts.1 = bf16[4096,128]{1,0:T(8,128)(2,1)} custom-call(bf16[4096,768]{1,0:T(8,128)(2,1)} %bitcast.2.x_ref, bf16[4096,768]{1,0:T(8,128)(2,1)} %all-gather.3.cloned.1.call-done.w_ref, s32[4096,2]{1,0:T(8,128)} %slice_convert_fusion.id_ref), custom_call_target="tpu_custom_call" | custom-call | flops 34359738368 | bytes 12582912 | tf_op jit(solution)/shard_map/contract_experts/pallas_call | solution.py:214
  199.4 12.7 %all-to-all-start.2 = ((bf16[32,128,128]{2,1,0:T(8,128)(2,1)}), bf16[32,128,128]{2,1,0:T(8,128)(2,1)S(1)}, u32[]{:S(2)}, u32[]{:S(2)}) async-start(bf16[32,128,128]{2,1,0:T(8,128)(2,1)} %bitcast.145), calls=%async_computation.2 | async-start | bytes 2097152 | tf_op jit(solution)/shard_map/all_to_all | solution.py:357
  212.4 3.8 fusion.18
  216.2 4.6 fusion.26
  220.8 8.6 %all-to-all-done.2 = bf16[32,128,128]{2,1,0:T(8,128)(2,1)S(1)} async-done(((bf16[32,128,128]{2,1,0:T(8,128)(2,1)}), bf16[32,128,128]{2,1,0:T(8,128)(2,1)S(1)}, u32[]{:S(2)}, u32[]{:S(2)}) %all-to-all-start.2) | async-done | bytes 1048608 | tf_op jit(solution)/shard_map/all_to_all | solution.py:357
  230.4 6.7 %fusion.23 = bf16[1024,128]{0,1:T(8,128)(2,1)S(1)} fusion(bf16[1024,2,128]{0,2,1:T(8,128)(2,1)} %bitcast.148, f32[2,1024]{1,0:T(2,128)S(1)} %get-tuple-element.21, f32[1024,1024,2]{1,0,2:T(8,128)} %copy-done.3, pred[1024,1024]{0,1:T(8,128)(4,1)S(1)} %fusion.16), kind=kOutput, calls=%fused_computation.33 | convolution fusion | flops 547487744 | bytes 10231808 | tf_op jit(solution)/shard_map/kgij,ikgd->jkd/dot_general | solution.py:76
  237.2 7.5 %convolution_convert_fusion = bf16[1024,4608]{1,0:T(8,128)(2,1)} fusion(bf16[4608,128]{1,0:T(8,128)(2,1)S(1)} %copy-done.15, bf16[4608,128]{1,0:T(8,128)(2,1)S(1)} %copy-done.16, bf16[4608,256]{1,0:T(8,128)(2,1)S(1)} %copy-done.14, bf16[1024,128]{0,1:T(8,128)(2,1)S(1)} %fusion.23, bf16[1024,128]{0,1:T(8,128)(2,1)S(1)} %copy-done.20, ...), kind=kOutput, calls=%fused_computation.1 | convolution fusion | flops 4853858304 | bytes 15204352 | tf_op jit(solution)/shard_map/te,de->td/dot_general | solution.py:82
  244.7 5.2 %all-to-all-start.3 = ((bf16[8,128,4608]{2,1,0:T(8,128)(2,1)}), bf16[8,128,4608]{2,1,0:T(8,128)(2,1)}, u32[]{:S(2)}, u32[]{:S(2)}) async-start(bf16[8,128,4608]{2,1,0:T(8,128)(2,1)} %bitcast.136), calls=%async_computation.3 | async-start | bytes 18874368 | tf_op jit(solution)/shard_map/all_to_all | solution.py:357
  251.2 37.8 %all-gather.5.cloned.1.call-done = bf16[4096,128]{0,1:T(8,128)(2,1)} async-done(((bf16[128,128]{0,1:T(8,128)(2,1)}), bf16[4096,128]{0,1:T(8,128)(2,1)}) %all-gather.5.cloned.1.call-update) | async-done | bytes 1048592 | tf_op jit(solution)/shard_map/all_gather | solution.py:418
  289.0 2.8 convert_bitcast_fusion.dt_ref
  291.8 47.8 %factor_gradients.1 = bf16[4096,768]{1,0:T(8,128)(2,1)} custom-call(bf16[4096,768]{1,0:T(8,128)(2,1)} %bitcast.2.x_ref, f32[128,4096]{1,0:T(8,128)} %convert_bitcast_fusion.dt_ref, s32[8,4096]{1,0:T(8,128)} %pad.4.it_ref), custom_call_target="tpu_custom_call" | custom-call | flops 34359738368 | bytes 12582912 | tf_op jit(solution)/shard_map/factor_gradients/pallas_call | solution.py:269
  339.5 1.2 copy-done.5
  340.7 1.3 copy.83.d_ref
  342.0 45.1 %expand_entries.1 = bf16[4096,640]{1,0:T(8,128)(2,1)} custom-call(bf16[4096,128]{1,0:T(8,128)(2,1)} %copy.83.d_ref, bf16[4096,768]{1,0:T(8,128)(2,1)} %all-gather.3.cloned.1.call-done.w_ref, s32[4096,2]{1,0:T(8,128)} %slice_convert_fusion.id_ref), custom_call_target="tpu_custom_call" | custom-call | flops 21474836480 | bytes 12582912 | tf_op jit(solution)/shard_map/expand_entries/pallas_call | solution.py:316
  387.1 67.1 %all_to_all.31.main_ref.rem_ref = bf16[32,128,640]{2,1,0:T(8,128)(2,1)} all-to-all(bf16[32,128,640]{2,1,0:T(8,128)(2,1)} %bitcast.138), channel_id=1, replica_groups=mesh['y'=4,'xl'=2,'xh'=2,'z'=4,'c'=2] {'xl','xh','z','c'}, dimensions={0} | all-to-all | bytes 10485760 | tf_op jit(solution)/shard_map/all_to_all | solution.py:357
  454.2 4.0 all-to-all-start.5
  458.2 5.3 %convert_reduce_fusion = f32[128,4608]{1,0:T(8,128)S(1)} fusion(bf16[8,128,4608]{2,1,0:T(8,128)(2,1)} %all-to-all-done.3), kind=kLoop, calls=%fused_computation | loop fusion | flops 8847360 | bytes 11796480 | tf_op jit(solution)/shard_map/reduce_sum | solution.py:436
  463.7 1.5 fusion.4
  465.2 7.4 %unpack_slices.2 = bf16[128,18432]{1,0:T(8,128)(2,1)} custom-call(bf16[32,128,640]{2,1,0:T(8,128)(2,1)} %all_to_all.31.main_ref.rem_ref, bf16[32,128,640]{2,1,0:T(8,128)(2,1)} %all_to_all.31.main_ref.rem_ref), custom_call_target="tpu_custom_call" | custom-call | flops 2359296 | bytes 9728000 | tf_op jit(solution)/shard_map/unpack_slices/pallas_call | solution.py:145
  472.6 8.2 %all-to-all-done.5.main_ref.rem_ref = bf16[32,32,768]{2,1,0:T(8,128)(2,1)S(1)} async-done(((bf16[32,32,768]{2,1,0:T(8,128)(2,1)}), bf16[32,32,768]{2,1,0:T(8,128)(2,1)S(1)}, u32[]{:S(2)}, u32[]{:S(2)}) %all-to-all-start.5) | async-done | bytes 1572896 | tf_op jit(solution)/shard_map/all_to_all | solution.py:357
  481.3 0.8 maximum_bitcast_fusion
  482.1 5.6 %unpack_slices.3 = bf16[32,18432]{1,0:T(8,128)(2,1)} custom-call(bf16[32,32,768]{2,1,0:T(8,128)(2,1)} %copy-done.1, bf16[32,32,768]{2,1,0:T(8,128)(2,1)} %copy-done.1), custom_call_target="tpu_custom_call" | custom-call | flops 589824 | bytes 2432000 | tf_op jit(solution)/shard_map/unpack_slices/pallas_call | solution.py:145
  (78 shorter events, 5.2 us)
Async XLA Ops:
  7.2 456.6 %copy-start = (bf16[4608,128]{1,0:T(8,128)(2,1)S(1)}, bf16[4608,128]{1,0:T(8,128)(2,1)}, u32[]{:S(2)}) copy-start(bf16[4608,128]{1,0:T(8,128)(2,1)} %param.21) | copy-start | bytes 3538948
  7.2 39.2 %copy-start.12 = (s32[128,2]{0,1:T(2,128)S(1)}, s32[128,2]{0,1:T(2,128)}, u32[]{:S(2)}) copy-start(s32[128,2]{0,1:T(2,128)} %param.17) | copy-start | bytes 3076
  7.2 134.9 %all-gather.3.cloned.1.call-start = ((), (), s32[]{:S(2)}) async-start(), calls=%async_computation.7 | async-start | bytes 7864320 | tf_op jit(solution)/shard_map/all_gather | solution.py:387
  55.3 4.9 copy-start.6
  55.3 5.1 %copy-start.7 = (bf16[1024,256]{1,0:T(8,128)(2,1)S(1)}, bf16[1024,256]{1,0:T(8,128)(2,1)}, u32[]{:S(2)}) copy-start(bf16[1024,256]{1,0:T(8,128)(2,1)} %param.22) | copy-start | bytes 1572868
  55.3 5.3 %copy-start.18 = (s32[1,8]{1,0:T(1,128)S(1)}, s32[1,8]{1,0:T(1,128)}, u32[]{:S(2)}) copy-start(s32[1,8]{1,0:T(1,128)} %param.29) | copy-start | bytes 100
  55.3 5.5 %copy-start.10 = (f32[128,2]{0,1:T(2,128)S(1)}, f32[128,2]{0,1:T(2,128)}, u32[]{:S(2)}) copy-start(f32[128,2]{0,1:T(2,128)} %param.18) | copy-start | bytes 3076
  55.3 83.7 %all-to-all-start = ((bf16[32,128,768]{2,1,0:T(8,128)(2,1)}), bf16[32,128,768]{2,1,0:T(8,128)(2,1)}, u32[]{:S(2)}, u32[]{:S(2)}) async-start(bf16[32,128,768]{2,1,0:T(8,128)(2,1)} %pack_slices.2), calls=%async_computation | async-start | bytes 12582912 | tf_op jit(solution)/shard_map/all_to_all | solution.py:357
  60.4 5.4 %copy-start.8 = (bf16[1024,256]{0,1:T(8,128)(2,1)}, bf16[1024,256]{0,1:T(8,128)(2,1)S(1)}, u32[]{:S(2)}) copy-start(bf16[1024,256]{0,1:T(8,128)(2,1)S(1)} %copy.97) | copy-start | bytes 1572868
  60.6 5.2 %copy-start.9 = (bf16[1024,256]{0,1:T(8,128)(2,1)}, bf16[1024,256]{0,1:T(8,128)(2,1)S(1)}, u32[]{:S(2)}) copy-start(bf16[1024,256]{0,1:T(8,128)(2,1)S(1)} %copy.96) | copy-start | bytes 1572868
  61.6 4.3 copy-start.17
  65.8 3.7 copy-start.3
  199.4 30.0 %all-to-all-start.2 = ((bf16[32,128,128]{2,1,0:T(8,128)(2,1)}), bf16[32,128,128]{2,1,0:T(8,128)(2,1)S(1)}, u32[]{:S(2)}, u32[]{:S(2)}) async-start(bf16[32,128,128]{2,1,0:T(8,128)(2,1)} %bitcast.145), calls=%async_computation.2 | async-start | bytes 2097152 | tf_op jit(solution)/shard_map/all_to_all | solution.py:357
  212.1 76.9 %all-gather.5.cloned.1.call-start = ((), (), s32[]{:S(2)}) async-start(), calls=%async_computation.8 | async-start | bytes 1081344 | tf_op jit(solution)/shard_map/all_gather | solution.py:418
  230.4 6.7 %copy-start.14 = (bf16[4608,256]{1,0:T(8,128)(2,1)S(1)}, bf16[4608,256]{1,0:T(8,128)(2,1)}, u32[]{:S(2)}) copy-start(bf16[4608,256]{1,0:T(8,128)(2,1)} %param.26) | copy-start | bytes 7077892
  230.4 6.7 %copy-start.15 = (bf16[4608,128]{1,0:T(8,128)(2,1)S(1)}, bf16[4608,128]{1,0:T(8,128)(2,1)}, u32[]{:S(2)}) copy-start(bf16[4608,128]{1,0:T(8,128)(2,1)} %param.28) | copy-start | bytes 3538948
  230.4 6.7 %copy-start.16 = (bf16[4608,128]{1,0:T(8,128)(2,1)S(1)}, bf16[4608,128]{1,0:T(8,128)(2,1)}, u32[]{:S(2)}) copy-start(bf16[4608,128]{1,0:T(8,128)(2,1)} %param.27) | copy-start | bytes 3538948
  230.4 6.7 %copy-start.19 = (bf16[2,1024,128]{1,2,0:T(8,128)(2,1)S(1)}, bf16[2,1024,128]{1,2,0:T(8,128)(2,1)}, u32[]{:S(2)}) copy-start(bf16[2,1024,128]{1,2,0:T(8,128)(2,1)} %fusion.18) | copy-start | bytes 1572868
  230.4 6.7 %copy-start.20 = (bf16[1024,128]{0,1:T(8,128)(2,1)S(1)}, bf16[1024,128]{0,1:T(8,128)(2,1)}, u32[]{:S(2)}) copy-start(bf16[1024,128]{0,1:T(8,128)(2,1)} %fusion.26) | copy-start | bytes 786436
  244.7 5.2 %copy-start.4 = (s32[4096,2]{1,0:T(8,128)S(1)}, s32[4096,2]{1,0:T(8,128)}, u32[]{:S(2)}) copy-start(s32[4096,2]{1,0:T(8,128)} %slice_convert_fusion.id_ref) | copy-start | bytes 98308
  244.7 142.4 %all-to-all-start.3 = ((bf16[8,128,4608]{2,1,0:T(8,128)(2,1)}), bf16[8,128,4608]{2,1,0:T(8,128)(2,1)}, u32[]{:S(2)}, u32[]{:S(2)}) async-start(bf16[8,128,4608]{2,1,0:T(8,128)(2,1)} %bitcast.136), calls=%async_computation.3 | async-start | bytes 18874368 | tf_op jit(solution)/shard_map/all_to_all | solution.py:357
  249.9 204.3 %reduce-scatter.2.cloned.1.call-start = ((), (), s32[]{:S(2)}) async-start(), calls=%async_computation.9 | async-start | bytes 7864320 | tf_op jit(solution)/shard_map/reduce_scatter | solution.py:422
  339.5 1.2 copy-start.5
  454.2 26.6 %all-to-all-start.5 = ((bf16[32,32,768]{2,1,0:T(8,128)(2,1)}), bf16[32,32,768]{2,1,0:T(8,128)(2,1)S(1)}, u32[]{:S(2)}, u32[]{:S(2)}) async-start(bf16[32,32,768]{2,1,0:T(8,128)(2,1)} %bitcast.141), calls=%async_computation.6 | async-start | bytes 3145728 | tf_op jit(solution)/shard_map/all_to_all | solution.py:357
  458.2 5.4 %copy-start.13 = (s32[128,2]{0,1:T(2,128)S(1)}, s32[128,2]{0,1:T(2,128)}, u32[]{:S(2)}) copy-start(s32[128,2]{0,1:T(2,128)} %param.17) | copy-start | bytes 3076
  458.2 5.5 %copy-start.2 = (bf16[128,4608]{1,0:T(8,128)(2,1)S(1)}, bf16[128,4608]{1,0:T(8,128)(2,1)}, u32[]{:S(2)}) copy-start(bf16[128,4608]{1,0:T(8,128)(2,1)} %gr_ref.1) | copy-start | bytes 3538948
  463.6 9.1 %copy-start.11 = (f32[128,2]{0,1:T(2,128)}, f32[128,2]{0,1:T(2,128)S(1)}, u32[]{:S(2)}) copy-start(f32[128,2]{0,1:T(2,128)S(1)} %fusion.47) | copy-start | bytes 3076
  480.8 1.2 copy-start.1
Sparse Core Ops, SparseCore 0:
  46.5 62.9 all-gather.2
  230.5 58.4 all-gather.4
  339.7 71.8 reduce-scatter.1

commit v2 on v1

--- a/solution.py
+++ b/solution.py
@@ -16,6 +16,13 @@
 SLICES = 32
 WIDTH = 768
 HWIDE = 640
+PAIRS = 16
+GROUPS = 16
+PAIR_ROWS = 48
+SLOTS = GROUPS * PAIR_ROWS
+GROUP_ROWS = PAIRS * PAIR_ROWS
+STEP = 2
+UNROLL = 4
 
 adapter_scale = 2.0
 score_cap = 50.0
@@ -159,179 +166,232 @@
     )(blocks, blocks)
 
 
-def fold_matrix(k):
-    r = lax.broadcasted_iota(jnp.int32, (128, 128), 0)
+def hot(shape, axis, *slots):
+    places = lax.broadcasted_iota(jnp.int32, shape, axis)
+    found = places == slots[0]
+    for s in slots[1:]:
+        found = found | (places == s)
+    return jnp.where(found, 1.0, 0.0).astype(BF16)
+
+
+def slots_in_rows(tail):
+    t = tail.astype(F32).T[80:88].astype(jnp.int32)
+    second = jnp.where(lanes_of((1, 256)) >= 128, 3, 0)
+    return [6 * t[k : k + 1] + t[2 + k : 3 + k] + second for k in range(2)]
+
+
+def slots_in_columns(tail):
+    t = tail.astype(F32)[:, 80:84].astype(jnp.int32)
+    second = jnp.where(lax.broadcasted_iota(jnp.int32, (256, 1), 0) >= 128, 3, 0)
+    return [6 * t[:, k : k + 1] + t[:, 2 + k : 3 + k] + second for k in range(2)]
+
+
+def own_lanes(axis):
+    shape = (GROUP_ROWS, 256) if axis == 0 else (256, GROUP_ROWS)
+    slot = lax.broadcasted_iota(jnp.int32, shape, axis) % PAIR_ROWS // 6
+    return slot == lax.broadcasted_iota(jnp.int32, shape, 1 - axis) // RANK
+
+
+def repeat_lanes(k, axis):
+    shape = (128, 256) if axis == 0 else (256, 128)
+    a = lax.broadcasted_iota(jnp.int32, shape, axis)
+    b = lax.broadcasted_iota(jnp.int32, shape, 1 - axis)
+    return (a == b % RANK + RANK * k).astype(F32).astype(BF16)
+
+
+def pair_at(q):
+    return pl.ds(pl.multiple_of(q * 256, 256), 256)
+
+
+def spread_pair(x):
+    place = hot((SLOTS, 256), 0, *slots_in_rows(x[:, 512:640]))
+    rows = jnp.dot(place, x, preferred_element_type=F32).astype(BF16)
+    return rows.reshape(GROUPS, PAIR_ROWS, WIDTH)
+
+
+def spread_kernel(x_ref, out_ref):
+    for q in range(out_ref.shape[1]):
+        out_ref[:, q] = spread_pair(x_ref[256 * q : 256 * q + 256])
+
+
+def spread(x):
+    return pl.pallas_call(
+        spread_kernel,
+        grid=(PAIRS // 2,),
+        in_specs=[pl.BlockSpec((512, WIDTH), lambda i: (i, 0))],
+        out_specs=pl.BlockSpec((GROUPS, 2, PAIR_ROWS, WIDTH), lambda i: (0, i, 0, 0)),
+        out_shape=jax.ShapeDtypeStruct((GROUPS, PAIRS, PAIR_ROWS, WIDTH), BF16),
+        compiler_params=pltpu.CompilerParams(vmem_limit_bytes=VMEM),
+        cost_estimate=pl.CostEstimate(
+            flops=2 * PAIRS * SLOTS * 256 * WIDTH,
+            bytes_accessed=2 * PAIRS * (SLOTS + 256) * WIDTH,
+            transcendentals=0,
+        ),
+        name="spread_rows",
+    )(x)
+
+
+def contract_kernel(x_ref, w_ref, out_ref, xs_ref, zs_ref):
+    step = pl.program_id(0)
+
+    @pl.when(step == 0)
+    def _():
+        def body(q, carry):
+            xs_ref[:, q] = spread_pair(x_ref[pair_at(q)])
+            return carry
+
+        lax.fori_loop(0, PAIRS, body, 0, unroll=UNROLL)
+
+    lane = lanes_of((256, 128))
+    dims = (((1,), (1,)), ((), ()))
+    mine = own_lanes(0)
+    r = lax.broadcasted_iota(jnp.int32, (128, 128), 0) % RANK
     c = lax.broadcasted_iota(jnp.int32, (128, 128), 1)
-    return (c == r % RANK + RANK * k).astype(F32).astype(BF16)
-
-
-def spread_matrix(k):
-    r = lax.broadcasted_iota(jnp.int32, (128, 128), 0)
-    c = lax.broadcasted_iota(jnp.int32, (128, 128), 1)
-    return (r == c % RANK + RANK * k).astype(F32).astype(BF16)
-
-
-def contract_kernel(x_ref, w_ref, id_ref, out_ref, h_ref, g_ref, a0, a1, b0, b1):
-    rows = x_ref.shape[0]
-    step = 512
-    lane = lanes_of((rows, 128))
-    tail = x_ref[:, 512:640]
-    zero = jnp.zeros_like(tail)
-    h_ref[:, 0:512] = x_ref[:, 0:512]
-    h_ref[:, 512:640] = jnp.where(lane < 64, tail, zero)
-    g_ref[:, 0:128] = jnp.where((lane >= 64) & (lane < 80), tail, zero)
-    g_ref[:, 128:256] = x_ref[:, 640:768]
-    for acc in (a0, a1, b0, b1):
-        acc[...] = jnp.zeros_like(acc)
-    e0 = id_ref[:, 0:1] - lane // RANK
-    e1 = id_ref[:, 1:2] - lane // RANK
-    dims = (((1,), (1,)), ((), ()))
-
-    def body(n, carry):
-        start = pl.multiple_of(n * step, step)
-        w_h = w_ref[pl.ds(start, step), 0:640]
-        w_g = w_ref[pl.ds(start, step), 512:768]
-        z = lax.dot_general(h_ref[...], w_h, dims, preferred_element_type=F32)
-        p = lax.dot_general(g_ref[...], w_g, dims, preferred_element_type=F32)
-        for refs, part in (((a0, a1), z), ((b0, b1), p)):
-            for ref, e in zip(refs, (e0, e1)):
-                acc = ref[...]
-                for j in range(step // 128):
-                    here = e == n * (step // RANK) + 4 * j
-                    acc = jnp.where(here, part[:, 128 * j : 128 * j + 128], acc)
-                ref[...] = acc
-        return carry
-
-    lax.fori_loop(0, w_ref.shape[0] // step, body, 0)
-    out = jnp.zeros((rows, 128), F32)
-    for k, acc in enumerate((a0, b0, a1, b1)):
-        out += jnp.dot(acc[...].astype(BF16), fold_matrix(k), preferred_element_type=F32)
-    out_ref[...] = out.astype(BF16)
-
-
-def contract(x, w, ids):
-    rows, tile = x.shape[0], 512
+    for n in range(STEP):
+        group = step * STEP + n
+        x = xs_ref[group].reshape(GROUP_ROWS, WIDTH)
+        w = w_ref[256 * n : 256 * n + 256]
+        tail = w[:, 512:640]
+        zero = jnp.zeros_like(tail)
+        w_h = jnp.concatenate([w[:, 0:512], jnp.where(lane < 64, tail, zero)], axis=1)
+        w_g = jnp.concatenate([jnp.where(lane < 64, zero, tail), w[:, 640:768]], axis=1)
+        out = jnp.zeros((GROUP_ROWS, 128), F32)
+        for k, (w, cut) in enumerate(((w_h, slice(0, 640)), (w_g, slice(512, 768)))):
+            full = lax.dot_general(x[:, cut], w, dims, preferred_element_type=F32)
+            full = jnp.where(mine, full, 0.0)
+            kept = (full[:, 0:128] + full[:, 128:256]).astype(BF16)
+            fold = (c == r + RANK * k).astype(F32).astype(BF16)
+            out += jnp.dot(kept, fold, preferred_element_type=F32)
+        zs_ref[group] = out.astype(BF16).reshape(PAIRS, PAIR_ROWS, 128)
+
+    @pl.when(step == GROUPS // STEP - 1)
+    def _():
+        half = lanes_of((256, 128))
+
+        def body(q, carry):
+            s0, s1 = slots_in_columns(x_ref[pair_at(q), 512:640])
+            z = zs_ref[:, q].reshape(SLOTS, 128)
+            first = jnp.dot(hot((256, SLOTS), 1, s0), z, preferred_element_type=F32)
+            second = jnp.dot(hot((256, SLOTS), 1, s1), z, preferred_element_type=F32)
+            out = jnp.where(half < 64, first, pltpu.roll(second, 64, 1))
+            out_ref[pair_at(q)] = out.astype(BF16)
+            return carry
+
+        lax.fori_loop(0, PAIRS, body, 0, unroll=UNROLL)
+
+
+def contract(x, w):
     return pl.pallas_call(
         contract_kernel,
-        grid=(rows // tile,),
+        grid=(GROUPS // STEP,),
         in_specs=[
-            pl.BlockSpec((tile, WIDTH), lambda i: (i, 0)),
-            pl.BlockSpec(w.shape, lambda i: (0, 0)),
-            pl.BlockSpec((tile, 2), lambda i: (i, 0)),
-        ],
-        out_specs=pl.BlockSpec((tile, 128), lambda i: (i, 0)),
-        out_shape=jax.ShapeDtypeStruct((rows, 128), BF16),
-        scratch_shapes=[pltpu.VMEM((tile, HWIDE), BF16), pltpu.VMEM((tile, 256), BF16)]
-        + [pltpu.VMEM((tile, 128), F32)] * 4,
+            pl.BlockSpec(x.shape, lambda i: (0, 0), pipeline_mode=pl.Buffered(1)),
+            pl.BlockSpec((256 * STEP, WIDTH), lambda i: (i, 0)),
+        ],
+        out_specs=pl.BlockSpec((x.shape[0], 128), lambda i: (0, 0)),
+        out_shape=jax.ShapeDtypeStruct((x.shape[0], 128), BF16),
+        scratch_shapes=[
+            pltpu.VMEM((GROUPS, PAIRS, PAIR_ROWS, WIDTH), BF16),
+            pltpu.VMEM((GROUPS, PAIRS, PAIR_ROWS, 128), BF16),
+        ],
         compiler_params=pltpu.CompilerParams(vmem_limit_bytes=VMEM),
         cost_estimate=pl.CostEstimate(
-            flops=2 * rows * w.shape[0] * 1024,
-            bytes_accessed=2 * (rows + w.shape[0]) * WIDTH,
+            flops=2 * GROUPS * GROUP_ROWS * 256 * 1024,
+            bytes_accessed=4 * x.shape[0] * WIDTH,
             transcendentals=0,
         ),
         name="contract_experts",
-    )(x, w, ids)
-
-
-def factors_kernel(x_ref, dt_ref, it_ref, out_ref, acc_h, acc_g):
-    tile, total = out_ref.shape[0], x_ref.shape[0]
-    step = 1024
-    acc_h[...] = jnp.zeros_like(acc_h)
-    acc_g[...] = jnp.zeros_like(acc_g)
-    first = pl.program_id(0) * (tile // RANK)
-
-    def body(n, carry):
-        start = pl.multiple_of(n * step, step)
-        at = pl.ds(start, step)
-        e0, e1 = it_ref[0:1, at], it_ref[1:2, at]
-        d0, w0 = dt_ref[0:32, at], dt_ref[32:64, at]
-        d1, w1 = dt_ref[64:96, at], dt_ref[96:128, at]
-        d_parts, w_parts = [], []
-        for j in range(tile // RANK):
-            m0, m1 = e0 == first + j, e1 == first + j
-            d_parts.append(jnp.where(m0, d0, jnp.where(m1, d1, 0.0)).astype(BF16))
-            w_parts.append(jnp.where(m0, w0, jnp.where(m1, w1, 0.0)).astype(BF16))
-        d_all = jnp.concatenate(d_parts, axis=0)
-        w_all = jnp.concatenate(w_parts, axis=0)
-        acc_h[...] += jnp.dot(d_all, x_ref[at, 0:640], preferred_element_type=F32)
-        acc_g[...] += jnp.dot(w_all, x_ref[at, 512:768], preferred_element_type=F32)
+    )(x, w)
+
+
+def place_latents(t_ref, d_ref, ds_ref):
+    half = lanes_of((256, 128))
+
+    def body(q, carry):
+        s0, s1 = slots_in_rows(t_ref[pair_at(q)])
+        d = d_ref[pair_at(q)].astype(F32)
+        d0 = jnp.where(half < 64, d, 0.0).astype(BF16)
+        d1 = jnp.where(half < 64, pltpu.roll(d, 64, 1), 0.0).astype(BF16)
+        rows = jnp.dot(hot((SLOTS, 256), 0, s0), d0, preferred_element_type=F32)
+        rows += jnp.dot(hot((SLOTS, 256), 0, s1), d1, preferred_element_type=F32)
+        ds_ref[:, q] = rows.astype(BF16).reshape(GROUPS, PAIR_ROWS, 128)
         return carry
 
-    lax.fori_loop(0, total // step, body, 0)
-    lane = lanes_of((tile, 128))
-    out_ref[:, 0:512] = acc_h[:, 0:512].astype(BF16)
-    out_ref[:, 512:640] = jnp.where(lane < 64, acc_h[:, 512:640], acc_g[:, 0:128]).astype(BF16)
-    out_ref[:, 640:768] = acc_g[:, 128:256].astype(BF16)
-
-
-def factors(x, dt, it, columns):
-    tile = 512
+    lax.fori_loop(0, PAIRS, body, 0, unroll=UNROLL)
+
+
+def gradients_kernel(t_ref, d_ref, x_ref, w_ref, factor_ref, hidden_ref, ds_ref, gs_ref):
+    step = pl.program_id(0)
+
+    @pl.when(step == 0)
+    def _():
+        place_latents(t_ref, d_ref, ds_ref)
+
+    dims = (((1,), (1,)), ((), ()))
+    across, along = own_lanes(0), own_lanes(1)
+    for n in range(STEP):
+        group = step * STEP + n
+        x = x_ref[n].reshape(GROUP_ROWS, WIDTH)
+        d = ds_ref[group].reshape(GROUP_ROWS, 128)
+        outs = []
+        for k, cut in ((0, slice(0, 640)), (1, slice(512, 768))):
+            wide = lax.dot_general(repeat_lanes(k, 1), d, dims, preferred_element_type=F32)
+            wide = jnp.where(along, wide, 0.0).astype(BF16)
+            outs.append(jnp.dot(wide, x[:, cut], preferred_element_type=F32))
+        hid, grad = outs
+        at = slice(256 * n, 256 * n + 256)
+        factor_ref[at, 0:512] = hid[:, 0:512].astype(BF16)
+        tail = jnp.where(lanes_of((256, 128)) < 64, hid[:, 512:640], grad[:, 0:128])
+        factor_ref[at, 512:640] = tail.astype(BF16)
+        factor_ref[at, 640:768] = grad[:, 128:256].astype(BF16)
+        wide = jnp.dot(d, repeat_lanes(0, 0), preferred_element_type=F32)
+        wide = jnp.where(across, wide, 0.0).astype(BF16)
+        out = jnp.dot(wide, w_ref[at, 0:640], preferred_element_type=F32).astype(BF16)
+        gs_ref[group] = out.reshape(PAIRS, PAIR_ROWS, HWIDE)
+
+    @pl.when(step == GROUPS // STEP - 1)
+    def _():
+        def body(q, carry):
+            both = hot((256, SLOTS), 1, *slots_in_columns(t_ref[pair_at(q)]))
+            g = gs_ref[:, q].reshape(SLOTS, HWIDE)
+            hidden_ref[pair_at(q)] = jnp.dot(both, g, preferred_element_type=F32).astype(BF16)
+            return carry
+
+        lax.fori_loop(0, PAIRS, body, 0, unroll=UNROLL)
+
+
+def gradients(x, d, xs, w):
+    rows = x.shape[0]
+    once = pl.Buffered(1)
     return pl.pallas_call(
-        factors_kernel,
-        grid=(columns // tile,),
+        gradients_kernel,
+        grid=(GROUPS // STEP,),
         in_specs=[
-            pl.BlockSpec(x.shape, lambda i: (0, 0)),
-            pl.BlockSpec(dt.shape, lambda i: (0, 0)),
-            pl.BlockSpec(it.shape, lambda i: (0, 0)),
-        ],
-        out_specs=pl.BlockSpec((tile, WIDTH), lambda i: (i, 0)),
-        out_shape=jax.ShapeDtypeStruct((columns, WIDTH), BF16),
-        scratch_shapes=[pltpu.VMEM((tile, HWIDE), F32), pltpu.VMEM((tile, 256), F32)],
+            pl.BlockSpec((rows, 128), lambda i: (0, 4), pipeline_mode=once),
+            pl.BlockSpec((rows, 128), lambda i: (0, 0), pipeline_mode=once),
+            pl.BlockSpec((STEP, PAIRS, PAIR_ROWS, WIDTH), lambda i: (i, 0, 0, 0)),
+            pl.BlockSpec((256 * STEP, WIDTH), lambda i: (i, 0)),
+        ],
+        out_specs=[
+            pl.BlockSpec((256 * STEP, WIDTH), lambda i: (i, 0)),
+            pl.BlockSpec((rows, HWIDE), lambda i: (0, 0), pipeline_mode=once),
+        ],
+        out_shape=[
+            jax.ShapeDtypeStruct((GROUPS * 256, WIDTH), BF16),
+            jax.ShapeDtypeStruct((rows, HWIDE), BF16),
+        ],
+        scratch_shapes=[
+            pltpu.VMEM((GROUPS, PAIRS, PAIR_ROWS, 128), BF16),
+            pltpu.VMEM((GROUPS, PAIRS, PAIR_ROWS, HWIDE), BF16),
+        ],
         compiler_params=pltpu.CompilerParams(vmem_limit_bytes=VMEM),
         cost_estimate=pl.CostEstimate(
-            flops=2 * x.shape[0] * columns * 1024,
-            bytes_accessed=2 * (x.shape[0] + columns) * WIDTH,
+            flops=4 * GROUPS * GROUP_ROWS * 256 * 1024,
+            bytes_accessed=2 * GROUPS * GROUP_ROWS * WIDTH + 8 * rows * WIDTH,
             transcendentals=0,
         ),
-        name="factor_gradients",
-    )(x, dt, it)
-
-
-def expand_kernel(d_ref, w_ref, id_ref, out_ref, acc):
-    rows = d_ref.shape[0]
-    step = 512
-    lane = lanes_of((rows, 128))
-    e0 = id_ref[:, 0:1] - lane // RANK
-    e1 = id_ref[:, 1:2] - lane // RANK
-    d0 = jnp.dot(d_ref[...], spread_matrix(0), preferred_element_type=F32)
-    d1 = jnp.dot(d_ref[...], spread_matrix(2), preferred_element_type=F32)
-    acc[...] = jnp.zeros_like(acc)
-
-    def body(n, carry):
-        start = pl.multiple_of(n * step, step)
-        parts = []
-        for j in range(step // 128):
-            at = n * (step // RANK) + 4 * j
-            parts.append(jnp.where(e0 == at, d0, jnp.where(e1 == at, d1, 0.0)).astype(BF16))
-        spread = jnp.concatenate(parts, axis=1)
-        acc[...] += jnp.dot(spread, w_ref[pl.ds(start, step), 0:640], preferred_element_type=F32)
-        return carry
-
-    lax.fori_loop(0, w_ref.shape[0] // step, body, 0)
-    out_ref[...] = acc[...].astype(BF16)
-
-
-def expand(d, w, ids):
-    rows, tile = d.shape[0], 512
-    return pl.pallas_call(
-        expand_kernel,
-        grid=(rows // tile,),
-        in_specs=[
-            pl.BlockSpec((tile, 128), lambda i: (i, 0)),
-            pl.BlockSpec(w.shape, lambda i: (0, 0)),
-            pl.BlockSpec((tile, 2), lambda i: (i, 0)),
-        ],
-        out_specs=pl.BlockSpec((tile, HWIDE), lambda i: (i, 0)),
-        out_shape=jax.ShapeDtypeStruct((rows, HWIDE), BF16),
-        scratch_shapes=[pltpu.VMEM((tile, HWIDE), F32)],
-        compiler_params=pltpu.CompilerParams(vmem_limit_bytes=VMEM),
-        cost_estimate=pl.CostEstimate(
-            flops=2 * rows * w.shape[0] * HWIDE,
-            bytes_accessed=2 * (rows + w.shape[0]) * WIDTH,
-            transcendentals=0,
-        ),
-        name="expand_entries",
-    )(d, w, ids)
+        name="factor_and_hidden_gradients",
+    )(x, d, xs, w)
 
 
 def router_term(specialist_pairs, weights, gates, dispatcher_map, experts):
@@ -378,16 +438,21 @@
     width_d = output_gradient.shape[1]
     experts = 128
     tokens = tok_rows * SLICES
-    columns = experts * RANK
     place = specialist_pairs % 8 * 16 + specialist_pairs // 8
     lane = jnp.arange(128, dtype=jnp.int32)[None, :]
-    id_lanes = jnp.where(lane == 80, place[:, 0:1], jnp.where(lane == 81, place[:, 1:2], 0))
+    named = (place[:, :, None] == lane[None]).astype(F32)
+    earlier = jnp.tril(jnp.ones((tok_rows, tok_rows), BF16), -1)
+    before = jnp.dot(earlier, jnp.sum(named, axis=1).astype(BF16), preferred_element_type=F32)
+    rank = jnp.sum(named * before[:, None, :], axis=2)
+    id_lanes = jnp.zeros((tok_rows, 128), F32)
+    for at, column in enumerate((place[:, 0], place[:, 1], rank[:, 0], rank[:, 1])):
+        id_lanes = jnp.where(lane == 80 + at, column.astype(F32)[:, None], id_lanes)
     w_mine = pack(lowering_maps[0].T, raising_maps[0], jnp.zeros((RANK, 128), F32))
-    w_rows = exchange(w_mine, PLANE).reshape(SLICES * RANK, WIDTH)
-    w_all = lax.all_gather(w_rows, LINE, axis=0, tiled=True)
-    x_mine = pack(hidden, output_gradient, id_lanes.astype(F32))
+    x_mine = pack(hidden, output_gradient, id_lanes)
+    w_rows = exchange(w_mine, PLANE)
+    w_rows, x_mine = lax.optimization_barrier((w_rows, x_mine))
+    w_all = lax.all_gather(w_rows.reshape(SLICES * RANK, WIDTH), LINE, axis=0, tiled=True)
     x = exchange(x_mine, PLANE).reshape(tokens, WIDTH)
-    ids = x[:, 592:594].astype(jnp.int32)
 
     part = attend_backward(
         queries,
@@ -400,10 +465,19 @@
         value_projection,
     ).astype(BF16)
 
-    sums = contract(x, w_all, ids)
-    sums = exchange(sums.reshape(SLICES, tok_rows, 128), PLANE).astype(F32)
-    sums = jnp.sum(sums, axis=0)
-    attention = exchange(part.reshape(8, tok_rows, width_d), TP)
+    x, part = lax.optimization_barrier((x, part))
+    part_rows = lax.psum_scatter(part, LINE, scatter_dimension=0, tiled=True)
+    sums = contract(x, w_all)
+    x, sums = lax.optimization_barrier((x, sums))
+    xs = spread(x)
+    sums = exchange(sums.reshape(SLICES, tok_rows, 128), PLANE)
+    xs, sums, part_rows = lax.optimization_barrier((xs, sums, part_rows))
+    sums = jnp.sum(sums.astype(F32), axis=0)
+    side = lax.axis_index("xl")
+    halves = part_rows.reshape(2, tok_rows, width_d)
+    kept = lax.dynamic_index_in_dim(halves, side, 0, keepdims=False)
+    passed = lax.dynamic_index_in_dim(halves, 1 - side, 0, keepdims=False)
+    passed = lax.ppermute(passed, "xl", [(0, 1), (1, 0)])
 
     weights = jax.nn.softmax(chosen_router_logits, axis=-1)
     weights_b = weights.astype(BF16).astype(F32)
@@ -415,12 +489,13 @@
         gates.append(jnp.sum(adapter_scale * z * p, axis=-1, keepdims=True).astype(BF16))
         sent.append((adapter_scale * w * p).astype(BF16))
         sent.append(adapter_scale * (w * z).astype(BF16))
-    d = lax.all_gather(jnp.concatenate(sent, axis=1), PLANE, axis=0, tiled=True)
+    mine = jnp.concatenate(sent, axis=1)
+    d = exchange(jnp.broadcast_to(mine[None], (SLICES,) + mine.shape), PLANE)
     gates = jnp.concatenate(gates, axis=1)
 
-    factor_part = factors(x, d.T.astype(F32), jnp.pad(ids.T, ((0, 6), (0, 0))), columns)
+    d = d.reshape(tokens, 128)
+    factor_part, hidden_part = gradients(x, d, xs, w_all)
     factor_rows = lax.psum_scatter(factor_part, LINE, scatter_dimension=0, tiled=True)
-    hidden_part = expand(d, w_all, ids)
     hidden_back = exchange(hidden_part.reshape(SLICES, tok_rows, HWIDE), PLANE)
     factor_back = exchange(factor_rows.reshape(SLICES, RANK, WIDTH), PLANE)
 
@@ -433,7 +508,7 @@
     router_logit_gradient, term = router_term(
         specialist_pairs, weights, gates, dispatcher_map, experts
     )
-    attention_rows = jnp.sum(attention.astype(F32), axis=0)
+    attention_rows = kept.astype(F32) + passed.astype(F32)
     residual_input_gradient = (output_gradient.astype(jnp.float32) + term + attention_rows).astype(
         jnp.bfloat16
     )

time: 496 us -> 426 us (0.86)
  waiting for transfers between devices: 119 us -> 198 us
  blocking collectives: 99.7 us -> 24.8 us
  Pallas kernels: 177 us -> 108 us
  other arithmetic: 19.6 us -> 7.38 us
  starting transfers between devices: 27 us -> 38.8 us
    all_to_all x2 -> x1, blocking collectives: 99.7 us -> 24.8 us  [exchange(): return lax.all_to_all(x, axes, split_axis=0, concat_axis=0, tiled=True)]
    pallas_call x3, Pallas kernels: 150 us -> 80.7 us  [the longest x1 37.4 us: gradients(): pl.pallas_call(gradients_kernel, grid=(GROUPS // STEP,), in_specs=[pl.Blo...]
    all_to_all x4 -> x5, waiting for transfers between devices: 81.2 us -> 144 us  [exchange(): return lax.all_to_all(x, axes, split_axis=0, concat_axis=0, tiled=True)]
    all_gather x2 -> x1, waiting for transfers between devices: 37.8 us -> 0.02 us  [local(): lax.all_gather(w_rows.reshape(SLICES * RANK, WIDTH), LINE, axis=0, tiled=...]
    reduce_scatter x0 -> x1, waiting for transfers between devices: none -> 35.1 us  [local(): part_rows = lax.psum_scatter(part, LINE, scatter_dimension=0, tiled=True)]
    ppermute x0 -> x1, waiting for transfers between devices: none -> 19.2 us  [local(): passed = lax.ppermute(passed, 'xl', [(0, 1), (1, 0)])]
    all_to_all x4 -> x5, starting transfers between devices: 26.7 us -> 38.1 us  [exchange(): return lax.all_to_all(x, axes, split_axis=0, concat_axis=0, tiled=True)]
    convert_element_type x3 -> x0, other arithmetic: 6.5 us -> none  [the longest x1 3.01 us: local(): ids = x[:, 592:594].astype(jnp.int32)]
  transfers between devices with their start and end apart: 7 -> 9, of which waited for: 4 -> 7; matrix products, arithmetic and copies ran while one was open for 11% -> 9% of each run, Pallas kernels for 22% -> 14%
where the time goes in v2:
time: 426 us; the launch traced here: 424 us
  waiting for transfers between devices  198 us (46%)
  Pallas kernels  108 us (25%)
  starting transfers between devices  38.8 us (9%)
  matrix products  28 us (7%)
  blocking collectives  24.8 us (6%)
  between operations  14.2 us (3%)
  other arithmetic  7.38 us (2%)
  local copies, waits for them, and re-layouts  5.13 us (1%)
    all_to_all x5, waiting for transfers between devices, exchange(): return lax.all_to_all(x, axes, split_axis=0, concat_axis=0, tiled=True)  144 us
    all_to_all x5, starting transfers between devices, exchange(): return lax.all_to_all(x, axes, split_axis=0, concat_axis=0, tiled=True)  38.1 us
    pallas_call x1, Pallas kernels, gradients(): pl.pallas_call(gradients_kernel, grid=(GROUPS // STEP,), in_specs=[pl.Blo...  37.4 us
    reduce_scatter x1, waiting for transfers between devices, local(): part_rows = lax.psum_scatter(part, LINE, scatter_dimension=0, tiled=True)  35.1 us
    pallas_call x1, Pallas kernels, contract(): pl.pallas_call(contract_kernel, grid=(GROUPS // STEP,), in_specs=[pl.Bloc...  30.6 us
    all_to_all x1, blocking collectives, exchange(): return lax.all_to_all(x, axes, split_axis=0, concat_axis=0, tiled=True)  24.8 us
    ppermute x1, waiting for transfers between devices, local(): passed = lax.ppermute(passed, 'xl', [(0, 1), (1, 0)])  19.2 us
    pallas_call x2, Pallas kernels, pack(): pl.pallas_call(pack_kernel, grid=(8,), in_specs=[pl.BlockSpec((rows, 2048...  14 us
  transfers between devices with their start and end apart: 9, of which 7 were waited for; matrix products, arithmetic and copies ran while one was open for 9% of the time, Pallas kernels for 14%

profile of v2, /device:TPU:1, one launch (start us, length us, event | category | flops | bytes accessed | tf_op | source)
XLA Modules:
  0.0 424.4 jit_solution(11378861359780232841)
XLA Ops:
  7.8 5.9 %pack_slices.2 = bf16[32,32,768]{2,1,0:T(8,128)(2,1)} custom-call(bf16[32,18432]{1,0:T(8,128)(2,1)} %bitcast.148, bf16[32,18432]{1,0:T(8,128)(2,1)} %bitcast.149, bf16[32,4608]{1,0:T(8,128)(2,1)} %bitcast.153, bf16[32,4608]{1,0:T(8,128)(2,1)} %bitcast.154, f32[32,128]{1,0:T(8,128)} %broadcast_in_dim.118.id_ref), custom_call_target="tpu_custom_call" | custom-call | flops 1572864 | bytes 3145728 | tf_op jit(solution)/shard_map/pack_slices/pallas_call | solution.py:115
  13.7 9.4 %all-to-all-start = ((bf16[32,32,768]{2,1,0:T(8,128)(2,1)}), bf16[32,32,768]{2,1,0:T(8,128)(2,1)S(1)}, u32[]{:S(2)}, u32[]{:S(2)}) async-start(bf16[32,32,768]{2,1,0:T(8,128)(2,1)} %pack_slices.2), calls=%async_computation | async-start | bytes 3145728 | tf_op jit(solution)/shard_map/all_to_all | solution.py:417
  24.5 8.1 %pack_slices.3 = bf16[32,128,768]{2,1,0:T(8,128)(2,1)} custom-call(bf16[128,18432]{1,0:T(8,128)(2,1)} %hr_ref.1, bf16[128,18432]{1,0:T(8,128)(2,1)} %hr_ref.1, bf16[128,4608]{1,0:T(8,128)(2,1)} %gr_ref.1, bf16[128,4608]{1,0:T(8,128)(2,1)} %gr_ref.1, f32[128,128]{1,0:T(8,128)} %select_select_fusion.id_ref), custom_call_target="tpu_custom_call" | custom-call | flops 6291456 | bytes 12582912 | tf_op jit(solution)/shard_map/pack_slices/pallas_call | solution.py:115
  32.7 13.4 %all-to-all-done = bf16[32,32,768]{2,1,0:T(8,128)(2,1)S(1)} async-done(((bf16[32,32,768]{2,1,0:T(8,128)(2,1)}), bf16[32,32,768]{2,1,0:T(8,128)(2,1)S(1)}, u32[]{:S(2)}, u32[]{:S(2)}) %all-to-all-start) | async-done | bytes 1572896 | tf_op jit(solution)/shard_map/all_to_all | solution.py:417
  46.1 1.1 copy-done.2
  47.5 1.2 copy.53
  49.6 5.1 %fusion.4 = (f32[2,1024]{1,0:T(2,128)S(1)}, f32[1024,1024,2]{1,0,2:T(8,128)}) fusion(pred[1024,1024]{0,1:T(8,128)(4,1)S(1)} %fusion.14, bf16[1024,2,128]{0,2,1:T(8,128)(2,1)S(1)} %bitcast.161, bf16[1024,128]{1,0:T(8,128)(2,1)S(1)} %copy-done.12), kind=kOutput, calls=%fused_computation.11 | convolution fusion | flops 545257472 | bytes 10231808 | tf_op jit(solution)/shard_map/ikgd,jkd->kgij/dot_general | solution.py:57
  54.8 4.8 %all-to-all-start.1 = ((bf16[32,128,768]{2,1,0:T(8,128)(2,1)}), bf16[32,128,768]{2,1,0:T(8,128)(2,1)}, u32[]{:S(2)}, u32[]{:S(2)}) async-start(bf16[32,128,768]{2,1,0:T(8,128)(2,1)} %pack_slices.3), calls=%async_computation.1 | async-start | bytes 12582912 | tf_op jit(solution)/shard_map/all_to_all | solution.py:417
  59.9 5.8 %fusion.1 = (f32[2,1024]{1,0:T(2,128)S(1)}, f32[1024,1024,2]{1,0,2:T(8,128)S(1)}) fusion(f32[2,1024]{1,0:T(2,128)S(1)} %get-tuple-element.45, f32[1024,1024,2]{1,0,2:T(8,128)} %get-tuple-element.46, pred[1024,1024]{0,1:T(8,128)(4,1)S(1)} %fusion.14, bf16[1024,2,128]{0,2,1:T(8,128)(2,1)S(1)} %bitcast.159, bf16[1024,128]{1,0:T(8,128)(2,1)S(1)} %copy-done.11), kind=kOutput, calls=%fused_computation.6 | convolution fusion | flops 549451776 | bytes 18628608 | tf_op jit(solution)/shard_map/ikgd,jkd->kgij/dot_general | solution.py:62
  65.8 3.8 fusion.10
  69.6 0.8 fusion.18
  70.4 1.5 fusion.26
  72.0 3.3 fusion.23
  75.3 7.7 %convolution_convert_fusion = bf16[1024,4608]{1,0:T(8,128)(2,1)} fusion(bf16[4608,128]{1,0:T(8,128)(2,1)S(1)} %copy-done.9, bf16[4608,128]{1,0:T(8,128)(2,1)S(1)} %copy-done.10, bf16[4608,256]{1,0:T(8,128)(2,1)S(1)} %copy-done.8, bf16[1024,128]{0,1:T(8,128)(2,1)S(1)} %fusion.23, bf16[1024,128]{0,1:T(8,128)(2,1)S(1)} %fusion.26, bf16[1024,256]{0,1:T(8,128)(2,1)S(1)} %bitcast.169), kind=kOutput, calls=%fused_computation | convolution fusion | flops 4853858304 | bytes 15204352 | tf_op jit(solution)/shard_map/te,de->td/dot_general | solution.py:89
  83.0 55.5 %all-to-all-done.1 = bf16[32,128,768]{2,1,0:T(8,128)(2,1)} async-done(((bf16[32,128,768]{2,1,0:T(8,128)(2,1)}), bf16[32,128,768]{2,1,0:T(8,128)(2,1)}, u32[]{:S(2)}, u32[]{:S(2)}) %all-to-all-start.1) | async-done | bytes 6291488 | tf_op jit(solution)/shard_map/all_to_all | solution.py:417
  138.6 30.6 %contract_experts.1 = bf16[4096,128]{1,0:T(8,128)(2,1)} custom-call(bf16[4096,768]{1,0:T(8,128)(2,1)} %bitcast.7.x_ref.t_ref, bf16[4096,768]{1,0:T(8,128)(2,1)} %all-gather.2.cloned.1.call-done.w_ref), custom_call_target="tpu_custom_call" | custom-call | flops 6442450944 | bytes 12582912 | tf_op jit(solution)/shard_map/contract_experts/pallas_call | solution.py:284
  169.1 12.8 %all-to-all-start.2 = ((bf16[32,128,128]{2,1,0:T(8,128)(2,1)}), bf16[32,128,128]{2,1,0:T(8,128)(2,1)S(1)}, u32[]{:S(2)}, u32[]{:S(2)}) async-start(bf16[32,128,128]{2,1,0:T(8,128)(2,1)} %bitcast.156), calls=%async_computation.2 | async-start | bytes 2097152 | tf_op jit(solution)/shard_map/all_to_all | solution.py:417
  182.1 12.8 %spread_rows.1.x_ref = bf16[16,16,48,768]{3,2,1,0:T(8,128)(2,1)} custom-call(bf16[4096,768]{1,0:T(8,128)(2,1)} %bitcast.7.x_ref.t_ref), custom_call_target="tpu_custom_call" | custom-call | flops 4831838208 | bytes 25165824 | tf_op jit(solution)/shard_map/spread_rows/pallas_call | solution.py:218
  194.8 4.4 %all-to-all-done.2 = bf16[32,128,128]{2,1,0:T(8,128)(2,1)S(1)} async-done(((bf16[32,128,128]{2,1,0:T(8,128)(2,1)}), bf16[32,128,128]{2,1,0:T(8,128)(2,1)S(1)}, u32[]{:S(2)}, u32[]{:S(2)}) %all-to-all-start.2) | async-done | bytes 1048608 | tf_op jit(solution)/shard_map/all_to_all | solution.py:417
  199.2 35.1 %reduce-scatter.3.cloned.1.call-done = bf16[256,4608]{1,0:T(8,128)(2,1)} async-done(((bf16[1024,4608]{1,0:T(8,128)(2,1)}), bf16[256,4608]{1,0:T(8,128)(2,1)}) %reduce-scatter.3.cloned.1.call-update) | async-done | bytes 2359312 | tf_op jit(solution)/shard_map/reduce_scatter | solution.py:469
  235.2 24.8 %all_to_all.30 = bf16[32,128,128]{2,1,0:T(8,128)(2,1)} all-to-all(bf16[32,128,128]{2,1,0:T(8,128)(2,1)S(1)} %broadcast_in_dim.137), channel_id=1, replica_groups=mesh['y'=4,'xl'=2,'xh'=2,'z'=4,'c'=2] {'xl','xh','z','c'}, dimensions={0} | all-to-all | bytes 2097152 | tf_op jit(solution)/shard_map/all_to_all | solution.py:417
  260.0 37.4 %factor_and_hidden_gradients.1 = (bf16[4096,768]{1,0:T(8,128)(2,1)}, bf16[4096,640]{1,0:T(8,128)(2,1)}) custom-call(bf16[4096,768]{1,0:T(8,128)(2,1)} %bitcast.7.x_ref.t_ref, bf16[4096,128]{1,0:T(8,128)(2,1)} %bitcast.157, bf16[16,16,48,768]{3,2,1,0:T(8,128)(2,1)} %spread_rows.1.x_ref, bf16[4096,768]{1,0:T(8,128)(2,1)} %all-gather.2.cloned.1.call-done.w_ref), custom_call_target="tpu_custom_call" | custom-call | flops 12884901888 | bytes 44040192 | tf_op jit(solution)/shard_map/factor_and_hidden_gradients/pallas_call | solution.py:366
  297.4 5.1 %all-to-all-start.4 = ((bf16[32,128,640]{2,1,0:T(8,128)(2,1)}), bf16[32,128,640]{2,1,0:T(8,128)(2,1)}, u32[]{:S(2)}, u32[]{:S(2)}) async-start(bf16[32,128,640]{2,1,0:T(8,128)(2,1)} %bitcast.147), calls=%async_computation.5 | async-start | bytes 10485760 | tf_op jit(solution)/shard_map/all_to_all | solution.py:417
  302.5 1.1 dynamic-slice_bitcast_fusion
  304.0 62.8 %all-to-all-done.4.main_ref.rem_ref = bf16[32,128,640]{2,1,0:T(8,128)(2,1)} async-done(((bf16[32,128,640]{2,1,0:T(8,128)(2,1)}), bf16[32,128,640]{2,1,0:T(8,128)(2,1)}, u32[]{:S(2)}, u32[]{:S(2)}) %all-to-all-start.4) | async-done | bytes 5242912 | tf_op jit(solution)/shard_map/all_to_all | solution.py:417
  366.8 5.9 %all-to-all-start.5 = ((bf16[32,32,768]{2,1,0:T(8,128)(2,1)}), bf16[32,32,768]{2,1,0:T(8,128)(2,1)S(1)}, u32[]{:S(2)}, u32[]{:S(2)}) async-start(bf16[32,32,768]{2,1,0:T(8,128)(2,1)} %bitcast.152), calls=%async_computation.7 | async-start | bytes 3145728 | tf_op jit(solution)/shard_map/all_to_all | solution.py:417
  372.9 19.2 %collective-permute-done = bf16[128,4608]{1,0:T(8,128)(2,1)} collective-permute-done((bf16[128,4608]{1,0:T(8,128)(2,1)}, bf16[128,4608]{1,0:T(8,128)(2,1)}, u32[]{:S(2)}, u32[]{:S(2)}) %collective-permute-start) | collective-permute-done | bytes 1179680 | tf_op jit(solution)/shard_map/ppermute | solution.py:480
  392.1 3.6 fusion.17
  395.7 7.4 %unpack_slices.2 = bf16[128,18432]{1,0:T(8,128)(2,1)} custom-call(bf16[32,128,640]{2,1,0:T(8,128)(2,1)} %all-to-all-done.4.main_ref.rem_ref, bf16[32,128,640]{2,1,0:T(8,128)(2,1)} %all-to-all-done.4.main_ref.rem_ref), custom_call_target="tpu_custom_call" | custom-call | flops 2359296 | bytes 9728000 | tf_op jit(solution)/shard_map/unpack_slices/pallas_call | solution.py:152
  403.1 7.9 %all-to-all-done.5.main_ref.rem_ref = bf16[32,32,768]{2,1,0:T(8,128)(2,1)S(1)} async-done(((bf16[32,32,768]{2,1,0:T(8,128)(2,1)}), bf16[32,32,768]{2,1,0:T(8,128)(2,1)S(1)}, u32[]{:S(2)}, u32[]{:S(2)}) %all-to-all-start.5) | async-done | bytes 1572896 | tf_op jit(solution)/shard_map/all_to_all | solution.py:417
  411.4 0.8 maximum_bitcast_fusion
  412.2 5.6 %unpack_slices.3 = bf16[32,18432]{1,0:T(8,128)(2,1)} custom-call(bf16[32,32,768]{2,1,0:T(8,128)(2,1)} %copy-done.1, bf16[32,32,768]{2,1,0:T(8,128)(2,1)} %copy-done.1), custom_call_target="tpu_custom_call" | custom-call | flops 589824 | bytes 2432000 | tf_op jit(solution)/shard_map/unpack_slices/pallas_call | solution.py:152
  (75 shorter events, 5.4 us)
Async XLA Ops:
  7.2 384.9 %copy-start = (bf16[4608,128]{1,0:T(8,128)(2,1)S(1)}, bf16[4608,128]{1,0:T(8,128)(2,1)}, u32[]{:S(2)}) copy-start(bf16[4608,128]{1,0:T(8,128)(2,1)} %param.21) | copy-start | bytes 3538948
  7.2 16.0 %copy-start.7 = (s32[128,2]{0,1:T(2,128)S(1)}, s32[128,2]{0,1:T(2,128)}, u32[]{:S(2)}) copy-start(s32[128,2]{0,1:T(2,128)} %param.17) | copy-start | bytes 3076
  13.7 32.4 %all-to-all-start = ((bf16[32,32,768]{2,1,0:T(8,128)(2,1)}), bf16[32,32,768]{2,1,0:T(8,128)(2,1)S(1)}, u32[]{:S(2)}, u32[]{:S(2)}) async-start(bf16[32,32,768]{2,1,0:T(8,128)(2,1)} %pack_slices.2), calls=%async_computation | async-start | bytes 3145728 | tf_op jit(solution)/shard_map/all_to_all | solution.py:417
  23.1 115.4 %all-gather.2.cloned.1.call-start = ((), (), s32[]{:S(2)}) async-start(), calls=%async_computation.8 | async-start | bytes 7864320 | tf_op jit(solution)/shard_map/all_gather | solution.py:454
  24.5 22.7 %copy-start.4 = (bf16[1024,256]{1,0:T(8,128)(2,1)S(1)}, bf16[1024,256]{1,0:T(8,128)(2,1)}, u32[]{:S(2)}) copy-start(bf16[1024,256]{1,0:T(8,128)(2,1)} %param.25) | copy-start | bytes 1572868
  24.5 24.2 %copy-start.14 = (s32[1,8]{1,0:T(1,128)S(1)}, s32[1,8]{1,0:T(1,128)}, u32[]{:S(2)}) copy-start(s32[1,8]{1,0:T(1,128)} %param.29) | copy-start | bytes 100
  32.7 16.9 %copy-start.12 = (bf16[1024,128]{1,0:T(8,128)(2,1)S(1)}, bf16[1024,128]{1,0:T(8,128)(2,1)}, u32[]{:S(2)}) copy-start(bf16[1024,128]{1,0:T(8,128)(2,1)} %param.23) | copy-start | bytes 786436
  46.1 1.1 copy-start.2
  54.8 5.1 %copy-start.11 = (bf16[1024,128]{1,0:T(8,128)(2,1)S(1)}, bf16[1024,128]{1,0:T(8,128)(2,1)}, u32[]{:S(2)}) copy-start(bf16[1024,128]{1,0:T(8,128)(2,1)} %param.24) | copy-start | bytes 786436
  54.8 83.7 %all-to-all-start.1 = ((bf16[32,128,768]{2,1,0:T(8,128)(2,1)}), bf16[32,128,768]{2,1,0:T(8,128)(2,1)}, u32[]{:S(2)}, u32[]{:S(2)}) async-start(bf16[32,128,768]{2,1,0:T(8,128)(2,1)} %pack_slices.3), calls=%async_computation.1 | async-start | bytes 12582912 | tf_op jit(solution)/shard_map/all_to_all | solution.py:417
  59.6 174.7 %reduce-scatter.3.cloned.1.call-start = ((), (), s32[]{:S(2)}) async-start(), calls=%async_computation.9 | async-start | bytes 11796480 | tf_op jit(solution)/shard_map/reduce_scatter | solution.py:469
  59.8 5.8 %slice-start = ((s8[8388608]{0:T(1024)(128)(4,1)}), s8[4194304]{0:T(1024)(128)(4,1)S(1)}, s32[]{:S(2)}) async-start(s8[8388608]{0:T(1024)(128)(4,1)} %bitcast.144), calls=%async_computation.11 | async-start | bytes 8388608
  59.9 5.9 %slice-start.1 = ((s8[8388608]{0:T(1024)(128)(4,1)}), s8[4194304]{0:T(1024)(128)(4,1)S(1)}, s32[]{:S(2)}) async-start(s8[8388608]{0:T(1024)(128)(4,1)} %bitcast.144), calls=%async_computation.12 | async-start | bytes 8388608
  65.8 3.8 copy-start.13
  71.9 3.3 copy-start.8
  71.9 3.3 copy-start.9
  72.0 3.3 copy-start.10
  138.5 43.5 %copy-start.5 = (f32[128,2]{0,1:T(2,128)S(1)}, f32[128,2]{0,1:T(2,128)}, u32[]{:S(2)}) copy-start(f32[128,2]{0,1:T(2,128)} %param.18) | copy-start | bytes 3076
  169.1 30.1 %all-to-all-start.2 = ((bf16[32,128,128]{2,1,0:T(8,128)(2,1)}), bf16[32,128,128]{2,1,0:T(8,128)(2,1)S(1)}, u32[]{:S(2)}, u32[]{:S(2)}) async-start(bf16[32,128,128]{2,1,0:T(8,128)(2,1)} %bitcast.156), calls=%async_computation.2 | async-start | bytes 2097152 | tf_op jit(solution)/shard_map/all_to_all | solution.py:417
  182.0 184.9 %reduce-scatter.5.cloned.1.call-start = ((), (), s32[]{:S(2)}) async-start(), calls=%async_computation.10 | async-start | bytes 7864320 | tf_op jit(solution)/shard_map/reduce_scatter | solution.py:498
  297.4 5.1 %copy-start.3 = (bf16[256,4608]{1,0:T(8,128)(2,1)S(1)}, bf16[256,4608]{1,0:T(8,128)(2,1)}, u32[]{:S(2)}) copy-start(bf16[256,4608]{1,0:T(8,128)(2,1)} %reduce-scatter.3.cloned.1.call-done) | copy-start | bytes 7077892
  297.4 69.4 %all-to-all-start.4 = ((bf16[32,128,640]{2,1,0:T(8,128)(2,1)}), bf16[32,128,640]{2,1,0:T(8,128)(2,1)}, u32[]{:S(2)}, u32[]{:S(2)}) async-start(bf16[32,128,640]{2,1,0:T(8,128)(2,1)} %bitcast.147), calls=%async_computation.5 | async-start | bytes 10485760 | tf_op jit(solution)/shard_map/all_to_all | solution.py:417
  303.6 88.5 %collective-permute-start = (bf16[128,4608]{1,0:T(8,128)(2,1)}, bf16[128,4608]{1,0:T(8,128)(2,1)}, u32[]{:S(2)}, u32[]{:S(2)}) collective-permute-start(bf16[128,4608]{1,0:T(8,128)(2,1)} %dynamic-slice_bitcast_fusion), channel_id=1, source_target_pairs={{0,16},{16,0},{1,17},{17,1},{2,18},{18,2},{3,19},{19,3},{4,20},{20... | collective-permute-start | bytes 3538952 | tf_op jit(solution)/shard_map/ppermute | solution.py:480
  366.8 44.2 %all-to-all-start.5 = ((bf16[32,32,768]{2,1,0:T(8,128)(2,1)}), bf16[32,32,768]{2,1,0:T(8,128)(2,1)S(1)}, u32[]{:S(2)}, u32[]{:S(2)}) async-start(bf16[32,32,768]{2,1,0:T(8,128)(2,1)} %bitcast.152), calls=%async_computation.7 | async-start | bytes 3145728 | tf_op jit(solution)/shard_map/all_to_all | solution.py:417
  372.8 30.3 %copy-start.6 = (f32[128,2]{0,1:T(2,128)}, f32[128,2]{0,1:T(2,128)S(1)}, u32[]{:S(2)}) copy-start(f32[128,2]{0,1:T(2,128)S(1)} %fusion.54) | copy-start | bytes 3076
  411.0 1.2 copy-start.1
Sparse Core Ops, SparseCore 0:
  47.4 63.2 all-gather.1
  138.6 95.6 reduce-scatter.2
  297.5 59.6 reduce-scatter.4

commit v3 on v2

--- a/solution.py
+++ b/solution.py
@@ -21,7 +21,7 @@
 PAIR_ROWS = 48
 SLOTS = GROUPS * PAIR_ROWS
 GROUP_ROWS = PAIRS * PAIR_ROWS
-STEP = 2
+STEP = 4
 UNROLL = 4
 
 adapter_scale = 2.0
@@ -32,12 +32,31 @@
 VMEM = 60 * 1024 * 1024
 
 
+def attend_scores(queries, keys, lengths):
+    rows = queries.shape[0]
+    kv_count = keys.shape[1] // HD
+    group = queries.shape[1] // keys.shape[1]
+    query4 = queries.reshape(rows, kv_count, group, HD)
+    key3 = keys.reshape(rows, kv_count, HD)
+    places = jnp.arange(rows, dtype=jnp.int32)
+    bounds = jnp.cumsum(lengths)
+    docs = jnp.sum((places[:, None] >= bounds[None, :]).astype(jnp.int32), axis=1)
+    allowed = (docs[:, None] == docs[None, :]) & (places[:, None] >= places[None, :])
+    raw = (
+        jnp.einsum("ikgd,jkd->kgij", query4, key3, preferred_element_type=jnp.float32) * query_scale
+    )
+    expo = jnp.where(allowed, jnp.exp(score_cap * jnp.tanh(raw / score_cap)), 0.0)
+    return raw, jnp.sum(expo, axis=-1, keepdims=True), allowed
+
+
 def attend_backward(
+    raw,
+    total,
+    allowed,
     queries,
     keys,
     values,
     context_gradient,
-    lengths,
     query_projection,
     key_projection,
     value_projection,
@@ -49,16 +68,9 @@
     ctx4 = context_gradient.reshape(rows, kv_count, group, HD)
     key3 = keys.reshape(rows, kv_count, HD)
     value3 = values.reshape(rows, kv_count, HD)
-    places = jnp.arange(rows, dtype=jnp.int32)
-    bounds = jnp.cumsum(lengths)
-    docs = jnp.sum((places[:, None] >= bounds[None, :]).astype(jnp.int32), axis=1)
-    allowed = (docs[:, None] == docs[None, :]) & (places[:, None] >= places[None, :])
-    raw = (
-        jnp.einsum("ikgd,jkd->kgij", query4, key3, preferred_element_type=jnp.float32) * query_scale
-    )
     bent = jnp.tanh(raw / score_cap)
     expo = jnp.where(allowed, jnp.exp(score_cap * bent), 0.0)
-    probs = expo / jnp.sum(expo, axis=-1, keepdims=True)
+    probs = expo / total
     dprobs = jnp.einsum("ikgd,jkd->kgij", ctx4, value3, preferred_element_type=jnp.float32)
     dsoft = probs * (dprobs - jnp.sum(probs * dprobs, axis=-1, keepdims=True))
     dscore = (dsoft * (1.0 - bent * bent)).astype(jnp.bfloat16)
@@ -97,14 +109,12 @@
     rows = hm_ref.shape[0]
     lane = lanes_of((rows, 128))
     ids = id_ref[...]
-    extra = gr_ref[...].astype(F32)
-    extra = jnp.where(pl.program_id(0) % 2 == 0, extra, pltpu.roll(extra, 64, 1))
-    for q in range(4):
+    for q in range(8):
         out_ref[q, :, 0:512] = hm_ref[:, 512 * q : 512 * q + 512]
         hid = hr_ref[:, 128 * (q // 2) : 128 * (q // 2) + 128].astype(F32)
         if q % 2:
             hid = pltpu.roll(hid, 64, 1)
-        grad = pltpu.roll(extra, 64 - 16 * q, 1)
+        grad = pltpu.roll(gr_ref[...].astype(F32), (64 - 16 * q) % 128, 1)
         tail = jnp.where(lane < 64, hid, jnp.where(lane < 80, grad, ids))
         out_ref[q, :, 512:640] = tail.astype(BF16)
         out_ref[q, :, 640:768] = gm_ref[:, 128 * q : 128 * q + 128]
@@ -114,15 +124,15 @@
     rows = hid.shape[0]
     return pl.pallas_call(
         pack_kernel,
-        grid=(8,),
+        grid=(4,),
         in_specs=[
-            pl.BlockSpec((rows, 2048), lambda i: (0, i)),
-            pl.BlockSpec((rows, 256), lambda i: (0, 64 + i)),
-            pl.BlockSpec((rows, 512), lambda i: (0, i)),
-            pl.BlockSpec((rows, 128), lambda i: (0, 32 + i // 2)),
+            pl.BlockSpec((rows, 4096), lambda i: (0, i)),
+            pl.BlockSpec((rows, 512), lambda i: (0, 32 + i)),
+            pl.BlockSpec((rows, 1024), lambda i: (0, i)),
+            pl.BlockSpec((rows, 128), lambda i: (0, 32 + i)),
             pl.BlockSpec((rows, 128), lambda i: (0, 0)),
         ],
-        out_specs=pl.BlockSpec((4, rows, WIDTH), lambda i: (i, 0, 0)),
+        out_specs=pl.BlockSpec((8, rows, WIDTH), lambda i: (i, 0, 0)),
         out_shape=jax.ShapeDtypeStruct((SLICES, rows, WIDTH), BF16),
         compiler_params=pltpu.CompilerParams(vmem_limit_bytes=VMEM),
         cost_estimate=pl.CostEstimate(
@@ -133,12 +143,14 @@
 
 
 def unpack_kernel(main_ref, rem_ref, out_ref):
-    @pl.when(pl.program_id(0) < 8)
+    step = pl.program_id(0)
+
+    @pl.when(step < 4)
     def _():
-        for q in range(4):
+        for q in range(8):
             out_ref[:, 512 * q : 512 * q + 512] = main_ref[q]
 
-    @pl.when(pl.program_id(0) == 8)
+    @pl.when(step == 4)
     def _():
         lane = lanes_of(rem_ref.shape[1:])
         for d in range(16):
@@ -151,12 +163,12 @@
     rows = blocks.shape[1]
     return pl.pallas_call(
         unpack_kernel,
-        grid=(9,),
+        grid=(5,),
         in_specs=[
-            pl.BlockSpec((4, rows, 512), lambda i: (jnp.minimum(i, 7), 0, 0)),
-            pl.BlockSpec((SLICES, rows, 128), lambda i: (0, 0, 4)),
-        ],
-        out_specs=pl.BlockSpec((rows, 2048), lambda i: (0, i)),
+            pl.BlockSpec((8, rows, 512), lambda i: (jnp.minimum(i, 3), 0, 0)),
+            pl.BlockSpec((SLICES, rows, 128), lambda i: (0, 0, 4), pipeline_mode=pl.Buffered(1)),
+        ],
+        out_specs=pl.BlockSpec((rows, 4096), lambda i: (0, i)),
         out_shape=jax.ShapeDtypeStruct((rows, 18432), BF16),
         compiler_params=pltpu.CompilerParams(vmem_limit_bytes=VMEM),
         cost_estimate=pl.CostEstimate(
@@ -271,9 +283,9 @@
         def body(q, carry):
             s0, s1 = slots_in_columns(x_ref[pair_at(q), 512:640])
             z = zs_ref[:, q].reshape(SLOTS, 128)
-            first = jnp.dot(hot((256, SLOTS), 1, s0), z, preferred_element_type=F32)
-            second = jnp.dot(hot((256, SLOTS), 1, s1), z, preferred_element_type=F32)
-            out = jnp.where(half < 64, first, pltpu.roll(second, 64, 1))
+            place = hot((512, SLOTS), 1, jnp.concatenate([s0, s1], axis=0))
+            found = jnp.dot(place, z, preferred_element_type=F32)
+            out = jnp.where(half < 64, found[0:256], pltpu.roll(found[256:512], 64, 1))
             out_ref[pair_at(q)] = out.astype(BF16)
             return carry
 
@@ -312,8 +324,8 @@
         d = d_ref[pair_at(q)].astype(F32)
         d0 = jnp.where(half < 64, d, 0.0).astype(BF16)
         d1 = jnp.where(half < 64, pltpu.roll(d, 64, 1), 0.0).astype(BF16)
-        rows = jnp.dot(hot((SLOTS, 256), 0, s0), d0, preferred_element_type=F32)
-        rows += jnp.dot(hot((SLOTS, 256), 0, s1), d1, preferred_element_type=F32)
+        place = hot((SLOTS, 512), 0, jnp.concatenate([s0, s1], axis=1))
+        rows = jnp.dot(place, jnp.concatenate([d0, d1], axis=0), preferred_element_type=F32)
         ds_ref[:, q] = rows.astype(BF16).reshape(GROUPS, PAIR_ROWS, 128)
         return carry
 
@@ -450,23 +462,24 @@
     w_mine = pack(lowering_maps[0].T, raising_maps[0], jnp.zeros((RANK, 128), F32))
     x_mine = pack(hidden, output_gradient, id_lanes)
     w_rows = exchange(w_mine, PLANE)
-    w_rows, x_mine = lax.optimization_barrier((w_rows, x_mine))
+    scores = attend_scores(queries, keys, lengths[0])
+    w_rows, x_mine, scores = lax.optimization_barrier((w_rows, x_mine, scores))
     w_all = lax.all_gather(w_rows.reshape(SLICES * RANK, WIDTH), LINE, axis=0, tiled=True)
     x = exchange(x_mine, PLANE).reshape(tokens, WIDTH)
 
     part = attend_backward(
+        *scores,
         queries,
         keys,
         values,
         context_gradient,
-        lengths[0],
         query_projection,
         key_projection,
         value_projection,
     ).astype(BF16)
 
-    x, part = lax.optimization_barrier((x, part))
     part_rows = lax.psum_scatter(part, LINE, scatter_dimension=0, tiled=True)
+    x, _ = lax.optimization_barrier((x, part))
     sums = contract(x, w_all)
     x, sums = lax.optimization_barrier((x, sums))
     xs = spread(x)
@@ -495,6 +508,7 @@
 
     d = d.reshape(tokens, 128)
     factor_part, hidden_part = gradients(x, d, xs, w_all)
+    hidden_part, passed = lax.optimization_barrier((hidden_part, passed))
     factor_rows = lax.psum_scatter(factor_part, LINE, scatter_dimension=0, tiled=True)
     hidden_back = exchange(hidden_part.reshape(SLICES, tok_rows, HWIDE), PLANE)
     factor_back = exchange(factor_rows.reshape(SLICES, RANK, WIDTH), PLANE)

time: 426 us -> 404 us (0.948)
  blocking collectives: 24.8 us -> 103 us
  waiting for transfers between devices: 198 us -> 120 us
  starting transfers between devices: 38.8 us -> 24.1 us
  Pallas kernels: 108 us -> 96.5 us
  other arithmetic: 7.38 us -> 13 us
    all_to_all x1 -> x2, blocking collectives: 24.8 us -> 103 us  [exchange(): return lax.all_to_all(x, axes, split_axis=0, concat_axis=0, tiled=True)]
    all_to_all x5 -> x4, waiting for transfers between devices: 144 us -> 89.1 us  [exchange(): return lax.all_to_all(x, axes, split_axis=0, concat_axis=0, tiled=True)]
    reduce_scatter x1, waiting for transfers between devices: 35.1 us -> 3.25 us  [local(): part_rows = lax.psum_scatter(part, LINE, scatter_dimension=0, tiled=True)]
    all_to_all x5 -> x4, starting transfers between devices: 38.1 us -> 23.4 us  [exchange(): return lax.all_to_all(x, axes, split_axis=0, concat_axis=0, tiled=True)]
    ppermute x1, waiting for transfers between devices: 19.2 us -> 27.7 us  [local(): passed = lax.ppermute(passed, 'xl', [(0, 1), (1, 0)])]
    pallas_call x4, Pallas kernels: 27.1 us -> 19.1 us  [the longest x2 9.68 us: pack(): pl.pallas_call(pack_kernel, grid=(4,), in_specs=[pl.BlockSpec((rows, 4096...]
  transfers between devices with their start and end apart: 9 -> 8, of which waited for: 7 -> 6; matrix products, arithmetic and copies ran while one was open for 9% -> 9% of each run, Pallas kernels for 14% -> 13%
where the time goes in v3:
time: 404 us; the launch traced here: 403 us
  waiting for transfers between devices  120 us (30%)
  blocking collectives  103 us (25%)
  Pallas kernels  96.5 us (24%)
  matrix products  24.4 us (6%)
  starting transfers between devices  24.1 us (6%)
  between operations  14.2 us (4%)
  other arithmetic  13 us (3%)
  local copies, waits for them, and re-layouts  7.85 us (2%)
    all_to_all x2, blocking collectives, exchange(): return lax.all_to_all(x, axes, split_axis=0, concat_axis=0, tiled=True)  103 us
    all_to_all x4, waiting for transfers between devices, exchange(): return lax.all_to_all(x, axes, split_axis=0, concat_axis=0, tiled=True)  89.1 us
    pallas_call x1, Pallas kernels, gradients(): pl.pallas_call(gradients_kernel, grid=(GROUPS // STEP,), in_specs=[pl.Blo...  35.8 us
    pallas_call x1, Pallas kernels, contract(): pl.pallas_call(contract_kernel, grid=(GROUPS // STEP,), in_specs=[pl.Bloc...  29 us
    ppermute x1, waiting for transfers between devices, local(): passed = lax.ppermute(passed, 'xl', [(0, 1), (1, 0)])  27.7 us
    all_to_all x4, starting transfers between devices, exchange(): return lax.all_to_all(x, axes, split_axis=0, concat_axis=0, tiled=True)  23.4 us
    pallas_call x1, Pallas kernels, spread(): pl.pallas_call(spread_kernel, grid=(PAIRS // 2,), in_specs=[pl.BlockSpec(...  12.7 us
    pallas_call x2, Pallas kernels, pack(): pl.pallas_call(pack_kernel, grid=(4,), in_specs=[pl.BlockSpec((rows, 4096...  9.68 us
  transfers between devices with their start and end apart: 8, of which 6 were waited for; matrix products, arithmetic and copies ran while one was open for 9% of the time, Pallas kernels for 13%

profile of v3, /device:TPU:1, one launch (start us, length us, event | category | flops | bytes accessed | tf_op | source)
XLA Modules:
  0.0 402.8 jit_solution(2836977051343364012)
XLA Ops:
  7.8 3.6 pack_slices.2
  11.4 9.4 %all-to-all-start = ((bf16[32,32,768]{2,1,0:T(8,128)(2,1)}), bf16[32,32,768]{2,1,0:T(8,128)(2,1)S(1)}, u32[]{:S(2)}, u32[]{:S(2)}) async-start(bf16[32,32,768]{2,1,0:T(8,128)(2,1)} %pack_slices.2), calls=%async_computation | async-start | bytes 3145728 | tf_op jit(solution)/shard_map/all_to_all | solution.py:429
  21.8 1.0 copy.53
  23.6 6.1 %pack_slices.3 = bf16[32,128,768]{2,1,0:T(8,128)(2,1)} custom-call(bf16[128,18432]{1,0:T(8,128)(2,1)} %hr_ref.1, bf16[128,18432]{1,0:T(8,128)(2,1)} %hr_ref.1, bf16[128,4608]{1,0:T(8,128)(2,1)} %gr_ref.1, bf16[128,4608]{1,0:T(8,128)(2,1)} %gr_ref.1, f32[128,128]{1,0:T(8,128)} %select_select_fusion.id_ref), custom_call_target="tpu_custom_call" | custom-call | flops 6291456 | bytes 12582912 | tf_op jit(solution)/shard_map/pack_slices/pallas_call | solution.py:125
  30.3 3.2 fusion
  33.5 4.3 %multiply_bitcast_fusion = f32[1,2,1024,1024]{2,3,1,0:T(8,128)} fusion(f32[1024,1024,2]{1,0,2:T(8,128)S(1)} %get-tuple-element.54), kind=kLoop, calls=%fused_computation.11 | loop fusion | flops 2097152 | bytes 16777216 | tf_op jit(solution)/shard_map/mul | solution.py:46
  37.8 6.1 %all-to-all-done = bf16[32,32,768]{2,1,0:T(8,128)(2,1)S(1)} async-done(((bf16[32,32,768]{2,1,0:T(8,128)(2,1)}), bf16[32,32,768]{2,1,0:T(8,128)(2,1)S(1)}, u32[]{:S(2)}, u32[]{:S(2)}) %all-to-all-start) | async-done | bytes 1572896 | tf_op jit(solution)/shard_map/all_to_all | solution.py:429
  43.8 1.1 copy-done.2
  45.5 5.9 %fusion.1 = (f32[2,1024]{1,0:T(2,128)S(1)}, f32[1024,1024,2]{1,0,2:T(8,128)S(1)}) fusion(f32[2,1024]{1,0:T(2,128)S(1)} %get-tuple-element.53, f32[1,2,1024,1024]{2,3,1,0:T(8,128)} %multiply_bitcast_fusion, pred[1024,1024]{0,1:T(8,128)(4,1)} %copy-done.3, bf16[1024,2,128]{0,2,1:T(8,128)(2,1)S(1)} %bitcast.151, bf16[1024,128]{1,0:T(8,128)(2,1)S(1)} %copy-done.19), kind=kOutput, calls=%fused_computation.5 | convolution fusion | flops 549451776 | bytes 18628608 | tf_op jit(solution)/shard_map/ikgd,jkd->kgij/dot_general | solution.py:74
  52.2 3.8 fusion.10
  57.1 1.5 fusion.25
  58.7 3.3 fusion.22
  62.0 7.6 %convolution_convert_fusion = bf16[1024,4608]{1,0:T(8,128)(2,1)} fusion(bf16[4608,128]{1,0:T(8,128)(2,1)S(1)} %copy-done.17, bf16[4608,128]{1,0:T(8,128)(2,1)S(1)} %copy-done.18, bf16[4608,256]{1,0:T(8,128)(2,1)S(1)} %copy-done.16, bf16[1024,128]{0,1:T(8,128)(2,1)S(1)} %fusion.22, bf16[1024,128]{0,1:T(8,128)(2,1)S(1)} %fusion.25, ...), kind=kOutput, calls=%fused_computation | convolution fusion | flops 4853858304 | bytes 15204352 | tf_op jit(solution)/shard_map/te,de->td/dot_general | solution.py:101
  69.6 77.9 %all_to_all.30 = bf16[32,128,768]{2,1,0:T(8,128)(2,1)} all-to-all(bf16[32,128,768]{2,1,0:T(8,128)(2,1)} %pack_slices.3), channel_id=1, replica_groups=mesh['y'=4,'xl'=2,'xh'=2,'z'=4,'c'=2] {'xl','xh','z','c'}, dimensions={0} | all-to-all | bytes 12582912 | tf_op jit(solution)/shard_map/all_to_all | solution.py:429
  147.5 29.0 %contract_experts.1 = bf16[4096,128]{1,0:T(8,128)(2,1)} custom-call(bf16[4096,768]{1,0:T(8,128)(2,1)} %bitcast.133, bf16[4096,768]{1,0:T(8,128)(2,1)} %all-gather.2.cloned.1.call-done.w_ref), custom_call_target="tpu_custom_call" | custom-call | flops 6442450944 | bytes 12582912 | tf_op jit(solution)/shard_map/contract_experts/pallas_call | solution.py:296
  176.4 3.7 all-to-all-start.2
  180.3 12.7 %spread_rows.1.x_ref = bf16[16,16,48,768]{3,2,1,0:T(8,128)(2,1)} custom-call(bf16[4096,768]{1,0:T(8,128)(2,1)} %bitcast.134), custom_call_target="tpu_custom_call" | custom-call | flops 4831838208 | bytes 25165824 | tf_op jit(solution)/shard_map/spread_rows/pallas_call | solution.py:230
  193.0 4.4 %all-to-all-done.2 = bf16[32,128,128]{2,1,0:T(8,128)(2,1)S(1)} async-done(((bf16[32,128,128]{2,1,0:T(8,128)(2,1)}), bf16[32,128,128]{2,1,0:T(8,128)(2,1)S(1)}, u32[]{:S(2)}, u32[]{:S(2)}) %all-to-all-start.2) | async-done | bytes 1048608 | tf_op jit(solution)/shard_map/all_to_all | solution.py:429
  197.4 3.2 reduce-scatter.3.cloned.1.call-done
  201.5 24.8 %all_to_all.31 = bf16[32,128,128]{2,1,0:T(8,128)(2,1)} all-to-all(bf16[32,128,128]{2,1,0:T(8,128)(2,1)S(1)} %broadcast_in_dim.145), channel_id=1, replica_groups=mesh['y'=4,'xl'=2,'xh'=2,'z'=4,'c'=2] {'xl','xh','z','c'}, dimensions={0} | all-to-all | bytes 2097152 | tf_op jit(solution)/shard_map/all_to_all | solution.py:429
  226.3 35.8 %factor_and_hidden_gradients.1 = (bf16[4096,768]{1,0:T(8,128)(2,1)}, bf16[4096,640]{1,0:T(8,128)(2,1)}) custom-call(bf16[4096,768]{1,0:T(8,128)(2,1)} %bitcast.135, bf16[4096,128]{1,0:T(8,128)(2,1)} %bitcast.147, bf16[16,16,48,768]{3,2,1,0:T(8,128)(2,1)} %spread_rows.1.x_ref, bf16[4096,768]{1,0:T(8,128)(2,1)} %all-gather.2.cloned.1.call-done.w_ref), custom_call_target="tpu_custom_call" | custom-call | flops 12884901888 | bytes 44040192 | tf_op jit(solution)/shard_map/factor_and_hidden_gradients/pallas_call | solution.py:378
  262.1 1.6 copy-done.5
  264.2 27.7 %collective-permute-done = bf16[128,4608]{1,0:T(8,128)(2,1)S(1)} collective-permute-done((bf16[128,4608]{1,0:T(8,128)(2,1)S(1)}, bf16[128,4608]{1,0:T(8,128)(2,1)S(1)}, u32[]{:S(2)}, u32[]{:S(2)}) %collective-permute-start) | collective-permute-done | bytes 1179680 | tf_op jit(solution)/shard_map/ppermute | solution.py:493
  291.9 1.0 copy-done.7
  292.9 4.7 %all-to-all-start.4 = ((bf16[32,128,640]{2,1,0:T(8,128)(2,1)}), bf16[32,128,640]{2,1,0:T(8,128)(2,1)}, u32[]{:S(2)}, u32[]{:S(2)}) async-start(bf16[32,128,640]{2,1,0:T(8,128)(2,1)} %bitcast.137), calls=%async_computation.5 | async-start | bytes 10485760 | tf_op jit(solution)/shard_map/all_to_all | solution.py:429
  297.7 65.1 %all-to-all-done.4.main_ref.rem_ref = bf16[32,128,640]{2,1,0:T(8,128)(2,1)} async-done(((bf16[32,128,640]{2,1,0:T(8,128)(2,1)}), bf16[32,128,640]{2,1,0:T(8,128)(2,1)}, u32[]{:S(2)}, u32[]{:S(2)}) %all-to-all-start.4) | async-done | bytes 5242912 | tf_op jit(solution)/shard_map/all_to_all | solution.py:429
  362.8 5.5 %all-to-all-start.5 = ((bf16[32,32,768]{2,1,0:T(8,128)(2,1)}), bf16[32,32,768]{2,1,0:T(8,128)(2,1)S(1)}, u32[]{:S(2)}, u32[]{:S(2)}) async-start(bf16[32,32,768]{2,1,0:T(8,128)(2,1)} %bitcast.142), calls=%async_computation.7 | async-start | bytes 3145728 | tf_op jit(solution)/shard_map/all_to_all | solution.py:429
  368.4 1.9 convolution_add_fusion
  370.7 1.4 fusion.16
  372.1 5.8 %unpack_slices.2 = bf16[128,18432]{1,0:T(8,128)(2,1)} custom-call(bf16[32,128,640]{2,1,0:T(8,128)(2,1)} %all-to-all-done.4.main_ref.rem_ref, bf16[32,128,640]{2,1,0:T(8,128)(2,1)} %all-to-all-done.4.main_ref.rem_ref), custom_call_target="tpu_custom_call" | custom-call | flops 2359296 | bytes 9728000 | tf_op jit(solution)/shard_map/unpack_slices/pallas_call | solution.py:164
  377.8 13.5 %all-to-all-done.5.main_ref.rem_ref = bf16[32,32,768]{2,1,0:T(8,128)(2,1)S(1)} async-done(((bf16[32,32,768]{2,1,0:T(8,128)(2,1)}), bf16[32,32,768]{2,1,0:T(8,128)(2,1)S(1)}, u32[]{:S(2)}, u32[]{:S(2)}) %all-to-all-start.5) | async-done | bytes 1572896 | tf_op jit(solution)/shard_map/all_to_all | solution.py:429
  392.6 3.7 unpack_slices.3
  (92 shorter events, 8.4 us)
Async XLA Ops:
  7.2 361.2 %copy-start = (bf16[4608,128]{1,0:T(8,128)(2,1)S(1)}, bf16[4608,128]{1,0:T(8,128)(2,1)}, u32[]{:S(2)}) copy-start(bf16[4608,128]{1,0:T(8,128)(2,1)} %param.21) | copy-start | bytes 3538948
  7.2 13.8 %copy-start.15 = (s32[128,2]{0,1:T(2,128)S(1)}, s32[128,2]{0,1:T(2,128)}, u32[]{:S(2)}) copy-start(s32[128,2]{0,1:T(2,128)} %param.17) | copy-start | bytes 3076
  7.2 14.3 %copy-start.22 = (s32[1,8]{1,0:T(1,128)S(1)}, s32[1,8]{1,0:T(1,128)}, u32[]{:S(2)}) copy-start(s32[1,8]{1,0:T(1,128)} %param.29) | copy-start | bytes 100
  7.2 14.6 %copy-start.9 = (bf16[1024,256]{1,0:T(8,128)(2,1)S(1)}, bf16[1024,256]{1,0:T(8,128)(2,1)}, u32[]{:S(2)}) copy-start(bf16[1024,256]{1,0:T(8,128)(2,1)} %param.22) | copy-start | bytes 1572868
  11.4 32.4 %all-to-all-start = ((bf16[32,32,768]{2,1,0:T(8,128)(2,1)}), bf16[32,32,768]{2,1,0:T(8,128)(2,1)S(1)}, u32[]{:S(2)}, u32[]{:S(2)}) async-start(bf16[32,32,768]{2,1,0:T(8,128)(2,1)} %pack_slices.2), calls=%async_computation | async-start | bytes 3145728 | tf_op jit(solution)/shard_map/all_to_all | solution.py:429
  20.9 126.6 %all-gather.2.cloned.1.call-start = ((), (), s32[]{:S(2)}) async-start(), calls=%async_computation.8 | async-start | bytes 7864320 | tf_op jit(solution)/shard_map/all_gather | solution.py:467
  23.6 6.7 %copy-start.11 = (bf16[1024,256]{0,1:T(8,128)(2,1)S(1)}, bf16[1024,256]{0,1:T(8,128)(2,1)}, u32[]{:S(2)}) copy-start(bf16[1024,256]{0,1:T(8,128)(2,1)} %copy.53) | copy-start | bytes 1572868
  23.6 6.7 %copy-start.20 = (bf16[1024,128]{1,0:T(8,128)(2,1)S(1)}, bf16[1024,128]{1,0:T(8,128)(2,1)}, u32[]{:S(2)}) copy-start(bf16[1024,128]{1,0:T(8,128)(2,1)} %param.23) | copy-start | bytes 786436
  30.2 3.2 copy-start.3
  33.5 11.8 %copy-start.10 = (bf16[1024,256]{1,0:T(8,128)(2,1)S(1)}, bf16[1024,256]{1,0:T(8,128)(2,1)}, u32[]{:S(2)}) copy-start(bf16[1024,256]{1,0:T(8,128)(2,1)} %param.25) | copy-start | bytes 1572868
  33.5 12.0 %copy-start.19 = (bf16[1024,128]{1,0:T(8,128)(2,1)S(1)}, bf16[1024,128]{1,0:T(8,128)(2,1)}, u32[]{:S(2)}) copy-start(bf16[1024,128]{1,0:T(8,128)(2,1)} %param.24) | copy-start | bytes 786436
  43.8 1.1 copy-start.2
  45.0 155.6 %reduce-scatter.3.cloned.1.call-start = ((), (), s32[]{:S(2)}) async-start(), calls=%async_computation.9 | async-start | bytes 11796480 | tf_op jit(solution)/shard_map/reduce_scatter | solution.py:481
  45.5 6.0 %slice-start = ((s8[8388608]{0:T(1024)(128)(4,1)}), s8[4194304]{0:T(1024)(128)(4,1)S(1)}, s32[]{:S(2)}) async-start(s8[8388608]{0:T(1024)(128)(4,1)} %bitcast.131), calls=%async_computation.11 | async-start | bytes 8388608
  45.5 6.7 %slice-start.1 = ((s8[8388608]{0:T(1024)(128)(4,1)}), s8[4194304]{0:T(1024)(128)(4,1)S(1)}, s32[]{:S(2)}) async-start(s8[8388608]{0:T(1024)(128)(4,1)} %bitcast.131), calls=%async_computation.12 | async-start | bytes 8388608
  45.5 6.7 %copy-start.4 = (pred[1024,1024]{0,1:T(8,128)(4,1)S(1)}, pred[1024,1024]{0,1:T(8,128)(4,1)}, u32[]{:S(2)}) copy-start(pred[1024,1024]{0,1:T(8,128)(4,1)} %copy-done.3) | copy-start | bytes 3145732
  52.2 3.8 copy-start.21
  56.0 1.1 copy-start.12
  58.6 3.3 copy-start.16
  58.6 3.3 copy-start.17
  58.6 3.3 copy-start.18
  147.5 32.7 %copy-start.13 = (f32[128,2]{0,1:T(2,128)S(1)}, f32[128,2]{0,1:T(2,128)}, u32[]{:S(2)}) copy-start(f32[128,2]{0,1:T(2,128)} %param.18) | copy-start | bytes 3076
  176.4 21.0 %all-to-all-start.2 = ((bf16[32,128,128]{2,1,0:T(8,128)(2,1)}), bf16[32,128,128]{2,1,0:T(8,128)(2,1)S(1)}, u32[]{:S(2)}, u32[]{:S(2)}) async-start(bf16[32,128,128]{2,1,0:T(8,128)(2,1)} %bitcast.146), calls=%async_computation.2 | async-start | bytes 2097152 | tf_op jit(solution)/shard_map/all_to_all | solution.py:429
  180.1 182.7 %reduce-scatter.5.cloned.1.call-start = ((), (), s32[]{:S(2)}) async-start(), calls=%async_computation.10 | async-start | bytes 7864320 | tf_op jit(solution)/shard_map/reduce_scatter | solution.py:512
  262.0 1.7 copy-start.5
  263.8 28.1 %collective-permute-start = (bf16[128,4608]{1,0:T(8,128)(2,1)S(1)}, bf16[128,4608]{1,0:T(8,128)(2,1)S(1)}, u32[]{:S(2)}, u32[]{:S(2)}) collective-permute-start(bf16[128,4608]{1,0:T(8,128)(2,1)S(1)} %dynamic-slice_bitcast_fusion), channel_id=1, source_target_pairs={{0,16},{16,0},{1,17},{17,1},{2,18},{18,2},{3,19},{19,3},{4,20},{20... | collective-permute-start | bytes 3538952 | tf_op jit(solution)/shard_map/ppermute | solution.py:493
  292.9 69.9 %all-to-all-start.4 = ((bf16[32,128,640]{2,1,0:T(8,128)(2,1)}), bf16[32,128,640]{2,1,0:T(8,128)(2,1)}, u32[]{:S(2)}, u32[]{:S(2)}) async-start(bf16[32,128,640]{2,1,0:T(8,128)(2,1)} %bitcast.137), calls=%async_computation.5 | async-start | bytes 10485760 | tf_op jit(solution)/shard_map/all_to_all | solution.py:429
  297.6 74.5 %copy-start.14 = (f32[128,2]{0,1:T(2,128)}, f32[128,2]{0,1:T(2,128)S(1)}, u32[]{:S(2)}) copy-start(f32[128,2]{0,1:T(2,128)S(1)} %fusion.53) | copy-start | bytes 3076
  362.8 28.5 %all-to-all-start.5 = ((bf16[32,32,768]{2,1,0:T(8,128)(2,1)}), bf16[32,32,768]{2,1,0:T(8,128)(2,1)S(1)}, u32[]{:S(2)}, u32[]{:S(2)}) async-start(bf16[32,32,768]{2,1,0:T(8,128)(2,1)} %bitcast.142), calls=%async_computation.7 | async-start | bytes 3145728 | tf_op jit(solution)/shard_map/all_to_all | solution.py:429
  368.4 2.0 copy-start.6
  368.4 2.3 copy-start.8
  391.3 1.2 copy-start.1
  (1 other events, 1.0 us)
Sparse Core Ops, SparseCore 0:
  45.1 63.2 all-gather.1
  110.9 89.7 reduce-scatter.2
  262.2 59.7 reduce-scatter.4

commit v4 on v3

--- a/solution.py
+++ b/solution.py
@@ -308,7 +308,7 @@
         ],
         compiler_params=pltpu.CompilerParams(vmem_limit_bytes=VMEM),
         cost_estimate=pl.CostEstimate(
-            flops=2 * GROUPS * GROUP_ROWS * 256 * 1024,
+            flops=60 * GROUPS * GROUP_ROWS * 256 * 1024,
             bytes_accessed=4 * x.shape[0] * WIDTH,
             transcendentals=0,
         ),
@@ -398,7 +398,7 @@
         ],
         compiler_params=pltpu.CompilerParams(vmem_limit_bytes=VMEM),
         cost_estimate=pl.CostEstimate(
-            flops=4 * GROUPS * GROUP_ROWS * 256 * 1024,
+            flops=12 * GROUPS * GROUP_ROWS * 256 * 1024,
             bytes_accessed=2 * GROUPS * GROUP_ROWS * WIDTH + 8 * rows * WIDTH,
             transcendentals=0,
         ),
@@ -484,7 +484,7 @@
     x, sums = lax.optimization_barrier((x, sums))
     xs = spread(x)
     sums = exchange(sums.reshape(SLICES, tok_rows, 128), PLANE)
-    xs, sums, part_rows = lax.optimization_barrier((xs, sums, part_rows))
+    xs, sums = lax.optimization_barrier((xs, sums))
     sums = jnp.sum(sums.astype(F32), axis=0)
     side = lax.axis_index("xl")
     halves = part_rows.reshape(2, tok_rows, width_d)
@@ -508,7 +508,9 @@
 
     d = d.reshape(tokens, 128)
     factor_part, hidden_part = gradients(x, d, xs, w_all)
-    hidden_part, passed = lax.optimization_barrier((hidden_part, passed))
+    factor_part, hidden_part, passed = lax.optimization_barrier(
+        (factor_part, hidden_part, passed)
+    )
     factor_rows = lax.psum_scatter(factor_part, LINE, scatter_dimension=0, tiled=True)
     hidden_back = exchange(hidden_part.reshape(SLICES, tok_rows, HWIDE), PLANE)
     factor_back = exchange(factor_rows.reshape(SLICES, RANK, WIDTH), PLANE)

time: 404 us -> 359 us (0.89)
  blocking collectives: 103 us -> 0 us
  waiting for transfers between devices: 120 us -> 157 us
  starting transfers between devices: 24.1 us -> 43.4 us
    all_to_all x2 -> x0, blocking collectives: 103 us -> none  [exchange(): return lax.all_to_all(x, axes, split_axis=0, concat_axis=0, tiled=True)]
    all_to_all x4 -> x6, waiting for transfers between devices: 89.1 us -> 150 us  [exchange(): return lax.all_to_all(x, axes, split_axis=0, concat_axis=0, tiled=True)]
    ppermute x1, waiting for transfers between devices: 27.7 us -> 0.01 us  [local(): passed = lax.ppermute(passed, 'xl', [(0, 1), (1, 0)])]
    all_to_all x4 -> x6, starting transfers between devices: 23.4 us -> 41.8 us  [exchange(): return lax.all_to_all(x, axes, split_axis=0, concat_axis=0, tiled=True)]
  transfers between devices with their start and end apart: 8 -> 10, of which waited for: 6 -> 7; matrix products, arithmetic and copies ran while one was open for 9% -> 11% of each run, Pallas kernels for 13% -> 25%
where the time goes in v4:
time: 359 us; the launch traced here: 358 us
  waiting for transfers between devices  157 us (44%)
  Pallas kernels  96.7 us (27%)
  starting transfers between devices  43.4 us (12%)
  matrix products  24.8 us (7%)
  between operations  14.3 us (4%)
  other arithmetic  13 us (4%)
  local copies, waits for them, and re-layouts  8.8 us (2%)
    all_to_all x6, waiting for transfers between devices, exchange(): return lax.all_to_all(x, axes, split_axis=0, concat_axis=0, tiled=True)  150 us
    all_to_all x6, starting transfers between devices, exchange(): return lax.all_to_all(x, axes, split_axis=0, concat_axis=0, tiled=True)  41.8 us
    pallas_call x1, Pallas kernels, gradients(): pl.pallas_call(gradients_kernel, grid=(GROUPS // STEP,), in_specs=[pl.Blo...  35.8 us
    pallas_call x1, Pallas kernels, contract(): pl.pallas_call(contract_kernel, grid=(GROUPS // STEP,), in_specs=[pl.Bloc...  29.1 us
    pallas_call x1, Pallas kernels, spread(): pl.pallas_call(spread_kernel, grid=(PAIRS // 2,), in_specs=[pl.BlockSpec(...  12.7 us
    pallas_call x2, Pallas kernels, pack(): pl.pallas_call(pack_kernel, grid=(4,), in_specs=[pl.BlockSpec((rows, 4096...  9.68 us
    pallas_call x2, Pallas kernels, unpack(): pl.pallas_call(unpack_kernel, grid=(5,), in_specs=[pl.BlockSpec((8, rows,...  9.46 us
    dot_general x1, matrix products, attend_backward(): jnp.einsum('te,de->td', grads, maps, preferred_element_type=jnp.float32)  7.6 us
  transfers between devices with their start and end apart: 10, of which 7 were waited for; matrix products, arithmetic and copies ran while one was open for 11% of the time, Pallas kernels for 25%

profile of v4, /device:TPU:1, one launch (start us, length us, event | category | flops | bytes accessed | tf_op | source)
XLA Modules:
  0.0 357.5 jit_solution(9116096807757103988)
XLA Ops:
  7.8 3.6 %pack_slices.2 = bf16[32,32,768]{2,1,0:T(8,128)(2,1)} custom-call(bf16[32,18432]{1,0:T(8,128)(2,1)} %bitcast.135, bf16[32,18432]{1,0:T(8,128)(2,1)} %bitcast.136, bf16[32,4608]{1,0:T(8,128)(2,1)} %bitcast.140, bf16[32,4608]{1,0:T(8,128)(2,1)} %bitcast.141, f32[32,128]{1,0:T(8,128)} %broadcast_in_dim.124.id_ref), custom_call_target="tpu_custom_call" | custom-call | flops 1572864 | bytes 3145728 | tf_op jit(solution)/shard_map/pack_slices/pallas_call | solution.py:125
  11.4 9.4 %all-to-all-start = ((bf16[32,32,768]{2,1,0:T(8,128)(2,1)}), bf16[32,32,768]{2,1,0:T(8,128)(2,1)S(1)}, u32[]{:S(2)}, u32[]{:S(2)}) async-start(bf16[32,32,768]{2,1,0:T(8,128)(2,1)} %pack_slices.2), calls=%async_computation | async-start | bytes 3145728 | tf_op jit(solution)/shard_map/all_to_all | solution.py:429
  23.6 6.1 %pack_slices.3 = bf16[32,128,768]{2,1,0:T(8,128)(2,1)} custom-call(bf16[128,18432]{1,0:T(8,128)(2,1)} %hr_ref.1, bf16[128,18432]{1,0:T(8,128)(2,1)} %hr_ref.1, bf16[128,4608]{1,0:T(8,128)(2,1)} %gr_ref.1, bf16[128,4608]{1,0:T(8,128)(2,1)} %gr_ref.1, f32[128,128]{1,0:T(8,128)} %select_select_fusion.id_ref), custom_call_target="tpu_custom_call" | custom-call | flops 6291456 | bytes 12582912 | tf_op jit(solution)/shard_map/pack_slices/pallas_call | solution.py:125
  30.3 3.2 fusion
  33.5 4.2 %multiply_bitcast_fusion = f32[1,2,1024,1024]{2,3,1,0:T(8,128)} fusion(f32[1024,1024,2]{1,0,2:T(8,128)S(1)} %get-tuple-element.54), kind=kLoop, calls=%fused_computation.11 | loop fusion | flops 2097152 | bytes 16777216 | tf_op jit(solution)/shard_map/mul | solution.py:46
  37.7 6.1 %all-to-all-done = bf16[32,32,768]{2,1,0:T(8,128)(2,1)S(1)} async-done(((bf16[32,32,768]{2,1,0:T(8,128)(2,1)}), bf16[32,32,768]{2,1,0:T(8,128)(2,1)S(1)}, u32[]{:S(2)}, u32[]{:S(2)}) %all-to-all-start) | async-done | bytes 1572896 | tf_op jit(solution)/shard_map/all_to_all | solution.py:429
  45.3 4.8 %all-to-all-start.1 = ((bf16[32,128,768]{2,1,0:T(8,128)(2,1)}), bf16[32,128,768]{2,1,0:T(8,128)(2,1)}, u32[]{:S(2)}, u32[]{:S(2)}) async-start(bf16[32,128,768]{2,1,0:T(8,128)(2,1)} %pack_slices.3), calls=%async_computation.1 | async-start | bytes 12582912 | tf_op jit(solution)/shard_map/all_to_all | solution.py:429
  50.4 6.3 %fusion.1 = (f32[2,1024]{1,0:T(2,128)S(1)}, f32[1024,1024,2]{1,0,2:T(8,128)S(1)}) fusion(f32[2,1024]{1,0:T(2,128)S(1)} %get-tuple-element.53, f32[1,2,1024,1024]{2,3,1,0:T(8,128)} %multiply_bitcast_fusion, pred[1024,1024]{0,1:T(8,128)(4,1)S(1)} %copy-done.4, bf16[1024,2,128]{0,2,1:T(8,128)(2,1)S(1)} %bitcast.147, bf16[1024,128]{1,0:T(8,128)(2,1)S(1)} %copy-done.19), kind=kOutput, calls=%fused_computation.5 | convolution fusion | flops 549451776 | bytes 18628608 | tf_op jit(solution)/shard_map/ikgd,jkd->kgij/dot_general | solution.py:74
  57.8 3.8 %fusion.10 = bf16[2,1024,1024]{1,2,0:T(8,128)(2,1)S(1)} fusion(f32[1,2,1024,1024]{2,3,1,0:T(8,128)S(1)} %bitcast.132, f32[1024,1024,2]{1,0,2:T(8,128)S(1)} %get-tuple-element.56, f32[2,1024]{1,0:T(2,128)S(1)} %get-tuple-element.55, f32[2,1024]{1,0:T(2,128)S(1)} %get-tuple-element.53, pred[1024,1024]{0,1:T(8,128)(4,1)S(1)} %copy-done.4), kind=kLoop, calls=%fused_computation.18 | loop fusion | flops 20971520 | bytes 22036480 | tf_op jit(solution)/shard_map/reshape.13
  62.7 1.5 fusion.25
  64.2 3.3 fusion.22
  67.5 7.6 %convolution_convert_fusion = bf16[1024,4608]{1,0:T(8,128)(2,1)} fusion(bf16[4608,128]{1,0:T(8,128)(2,1)S(1)} %copy-done.17, bf16[4608,128]{1,0:T(8,128)(2,1)S(1)} %copy-done.18, bf16[4608,256]{1,0:T(8,128)(2,1)S(1)} %copy-done.16, bf16[1024,128]{0,1:T(8,128)(2,1)S(1)} %fusion.22, bf16[1024,128]{0,1:T(8,128)(2,1)S(1)} %fusion.25, ...), kind=kOutput, calls=%fused_computation | convolution fusion | flops 4853858304 | bytes 15204352 | tf_op jit(solution)/shard_map/te,de->td/dot_general | solution.py:101
  75.2 53.8 %all-to-all-done.1 = bf16[32,128,768]{2,1,0:T(8,128)(2,1)} async-done(((bf16[32,128,768]{2,1,0:T(8,128)(2,1)}), bf16[32,128,768]{2,1,0:T(8,128)(2,1)}, u32[]{:S(2)}, u32[]{:S(2)}) %all-to-all-start.1) | async-done | bytes 6291488 | tf_op jit(solution)/shard_map/all_to_all | solution.py:429
  129.0 29.1 %contract_experts.1 = bf16[4096,128]{1,0:T(8,128)(2,1)} custom-call(bf16[4096,768]{1,0:T(8,128)(2,1)} %bitcast.15.x_ref.t_ref, bf16[4096,768]{1,0:T(8,128)(2,1)} %all-gather.2.cloned.1.call-done.w_ref), custom_call_target="tpu_custom_call" | custom-call | flops 193273528320 | bytes 12582912 | tf_op jit(solution)/shard_map/contract_experts/pallas_call | solution.py:296
  158.1 12.7 %all-to-all-start.2 = ((bf16[32,128,128]{2,1,0:T(8,128)(2,1)}), bf16[32,128,128]{2,1,0:T(8,128)(2,1)S(1)}, u32[]{:S(2)}, u32[]{:S(2)}) async-start(bf16[32,128,128]{2,1,0:T(8,128)(2,1)} %bitcast.143), calls=%async_computation.2 | async-start | bytes 2097152 | tf_op jit(solution)/shard_map/all_to_all | solution.py:429
  170.9 12.7 %spread_rows.1.x_ref = bf16[16,16,48,768]{3,2,1,0:T(8,128)(2,1)} custom-call(bf16[4096,768]{1,0:T(8,128)(2,1)} %bitcast.15.x_ref.t_ref), custom_call_target="tpu_custom_call" | custom-call | flops 4831838208 | bytes 25165824 | tf_op jit(solution)/shard_map/spread_rows/pallas_call | solution.py:230
  183.6 4.5 %all-to-all-done.2 = bf16[32,128,128]{2,1,0:T(8,128)(2,1)S(1)} async-done(((bf16[32,128,128]{2,1,0:T(8,128)(2,1)}), bf16[32,128,128]{2,1,0:T(8,128)(2,1)S(1)}, u32[]{:S(2)}, u32[]{:S(2)}) %all-to-all-start.2) | async-done | bytes 1048608 | tf_op jit(solution)/shard_map/all_to_all | solution.py:429
  188.7 1.2 broadcast_in_dim.145
  189.9 4.5 %all-to-all-start.3 = ((bf16[32,128,128]{2,1,0:T(8,128)(2,1)}), bf16[32,128,128]{2,1,0:T(8,128)(2,1)}, u32[]{:S(2)}, u32[]{:S(2)}) async-start(bf16[32,128,128]{2,1,0:T(8,128)(2,1)} %broadcast_in_dim.145), calls=%async_computation.4 | async-start | bytes 2097152 | tf_op jit(solution)/shard_map/all_to_all | solution.py:429
  194.4 6.2 %reduce-scatter.3.cloned.1.call-done = bf16[256,4608]{1,0:T(8,128)(2,1)} async-done(((bf16[1024,4608]{1,0:T(8,128)(2,1)}), bf16[256,4608]{1,0:T(8,128)(2,1)}) %reduce-scatter.3.cloned.1.call-update) | async-done | bytes 2359312 | tf_op jit(solution)/shard_map/reduce_scatter | solution.py:481
  200.6 1.3 dynamic-slice_bitcast_fusion
  202.0 1.3 collective-permute-start
  203.3 7.8 %all-to-all-done.3 = bf16[32,128,128]{2,1,0:T(8,128)(2,1)} async-done(((bf16[32,128,128]{2,1,0:T(8,128)(2,1)}), bf16[32,128,128]{2,1,0:T(8,128)(2,1)}, u32[]{:S(2)}, u32[]{:S(2)}) %all-to-all-start.3) | async-done | bytes 1048608 | tf_op jit(solution)/shard_map/all_to_all | solution.py:429
  211.0 35.8 %factor_and_hidden_gradients.1 = (bf16[4096,768]{1,0:T(8,128)(2,1)}, bf16[4096,640]{1,0:T(8,128)(2,1)}) custom-call(bf16[4096,768]{1,0:T(8,128)(2,1)} %bitcast.15.x_ref.t_ref, bf16[4096,128]{1,0:T(8,128)(2,1)} %bitcast.40.d_ref, bf16[16,16,48,768]{3,2,1,0:T(8,128)(2,1)} %spread_rows.1.x_ref, bf16[4096,768]{1,0:T(8,128)(2,1)} %all-gather.2.cloned.1.call-done.w_ref), custom_call_target="tpu_custom_call" | custom-call | flops 38654705664 | bytes 44040192 | tf_op jit(solution)/shard_map/factor_and_hidden_gradients/pallas_call | solution.py:378
  247.8 4.7 %all-to-all-start.4 = ((bf16[32,128,640]{2,1,0:T(8,128)(2,1)}), bf16[32,128,640]{2,1,0:T(8,128)(2,1)}, u32[]{:S(2)}, u32[]{:S(2)}) async-start(bf16[32,128,640]{2,1,0:T(8,128)(2,1)} %bitcast.134), calls=%async_computation.5 | async-start | bytes 10485760 | tf_op jit(solution)/shard_map/all_to_all | solution.py:429
  252.7 64.7 %all-to-all-done.4.main_ref.rem_ref = bf16[32,128,640]{2,1,0:T(8,128)(2,1)} async-done(((bf16[32,128,640]{2,1,0:T(8,128)(2,1)}), bf16[32,128,640]{2,1,0:T(8,128)(2,1)}, u32[]{:S(2)}, u32[]{:S(2)}) %all-to-all-start.4) | async-done | bytes 5242912 | tf_op jit(solution)/shard_map/all_to_all | solution.py:429
  317.4 5.7 %all-to-all-start.5 = ((bf16[32,32,768]{2,1,0:T(8,128)(2,1)}), bf16[32,32,768]{2,1,0:T(8,128)(2,1)S(1)}, u32[]{:S(2)}, u32[]{:S(2)}) async-start(bf16[32,32,768]{2,1,0:T(8,128)(2,1)} %bitcast.139), calls=%async_computation.7 | async-start | bytes 3145728 | tf_op jit(solution)/shard_map/all_to_all | solution.py:429
  323.1 1.9 convolution_add_fusion
  325.4 1.4 fusion.16
  326.8 5.8 %unpack_slices.2 = bf16[128,18432]{1,0:T(8,128)(2,1)} custom-call(bf16[32,128,640]{2,1,0:T(8,128)(2,1)} %all-to-all-done.4.main_ref.rem_ref, bf16[32,128,640]{2,1,0:T(8,128)(2,1)} %all-to-all-done.4.main_ref.rem_ref), custom_call_target="tpu_custom_call" | custom-call | flops 2359296 | bytes 9728000 | tf_op jit(solution)/shard_map/unpack_slices/pallas_call | solution.py:164
  332.6 13.5 %all-to-all-done.5.main_ref.rem_ref = bf16[32,32,768]{2,1,0:T(8,128)(2,1)S(1)} async-done(((bf16[32,32,768]{2,1,0:T(8,128)(2,1)}), bf16[32,32,768]{2,1,0:T(8,128)(2,1)S(1)}, u32[]{:S(2)}, u32[]{:S(2)}) %all-to-all-start.5) | async-done | bytes 1572896 | tf_op jit(solution)/shard_map/all_to_all | solution.py:429
  347.3 3.7 %unpack_slices.3 = bf16[32,18432]{1,0:T(8,128)(2,1)} custom-call(bf16[32,32,768]{2,1,0:T(8,128)(2,1)} %copy-done.1, bf16[32,32,768]{2,1,0:T(8,128)(2,1)} %copy-done.1), custom_call_target="tpu_custom_call" | custom-call | flops 589824 | bytes 2432000 | tf_op jit(solution)/shard_map/unpack_slices/pallas_call | solution.py:164
  (94 shorter events, 11.1 us)
Async XLA Ops:
  7.2 315.9 %copy-start = (bf16[4608,128]{1,0:T(8,128)(2,1)S(1)}, bf16[4608,128]{1,0:T(8,128)(2,1)}, u32[]{:S(2)}) copy-start(bf16[4608,128]{1,0:T(8,128)(2,1)} %param.21) | copy-start | bytes 3538948
  7.2 13.8 %copy-start.14 = (s32[128,2]{0,1:T(2,128)S(1)}, s32[128,2]{0,1:T(2,128)}, u32[]{:S(2)}) copy-start(s32[128,2]{0,1:T(2,128)} %param.17) | copy-start | bytes 3076
  7.2 13.9 %copy-start.22 = (s32[1,8]{1,0:T(1,128)S(1)}, s32[1,8]{1,0:T(1,128)}, u32[]{:S(2)}) copy-start(s32[1,8]{1,0:T(1,128)} %param.29) | copy-start | bytes 100
  7.2 14.6 %copy-start.8 = (bf16[1024,256]{1,0:T(8,128)(2,1)S(1)}, bf16[1024,256]{1,0:T(8,128)(2,1)}, u32[]{:S(2)}) copy-start(bf16[1024,256]{1,0:T(8,128)(2,1)} %param.22) | copy-start | bytes 1572868
  11.4 32.4 %all-to-all-start = ((bf16[32,32,768]{2,1,0:T(8,128)(2,1)}), bf16[32,32,768]{2,1,0:T(8,128)(2,1)S(1)}, u32[]{:S(2)}, u32[]{:S(2)}) async-start(bf16[32,32,768]{2,1,0:T(8,128)(2,1)} %pack_slices.2), calls=%async_computation | async-start | bytes 3145728 | tf_op jit(solution)/shard_map/all_to_all | solution.py:429
  20.9 108.1 %all-gather.2.cloned.1.call-start = ((), (), s32[]{:S(2)}) async-start(), calls=%async_computation.8 | async-start | bytes 7864320 | tf_op jit(solution)/shard_map/all_gather | solution.py:467
  23.6 6.7 %copy-start.10 = (bf16[1024,256]{0,1:T(8,128)(2,1)S(1)}, bf16[1024,256]{0,1:T(8,128)(2,1)}, u32[]{:S(2)}) copy-start(bf16[1024,256]{0,1:T(8,128)(2,1)} %copy.53) | copy-start | bytes 1572868
  23.6 6.7 %copy-start.20 = (bf16[1024,128]{1,0:T(8,128)(2,1)S(1)}, bf16[1024,128]{1,0:T(8,128)(2,1)}, u32[]{:S(2)}) copy-start(bf16[1024,128]{1,0:T(8,128)(2,1)} %param.23) | copy-start | bytes 786436
  30.2 3.2 copy-start.3
  33.5 11.5 %copy-start.9 = (bf16[1024,256]{1,0:T(8,128)(2,1)S(1)}, bf16[1024,256]{1,0:T(8,128)(2,1)}, u32[]{:S(2)}) copy-start(bf16[1024,256]{1,0:T(8,128)(2,1)} %param.25) | copy-start | bytes 1572868
  45.2 5.1 %copy-start.4 = (pred[1024,1024]{0,1:T(8,128)(4,1)S(1)}, pred[1024,1024]{0,1:T(8,128)(4,1)}, u32[]{:S(2)}) copy-start(pred[1024,1024]{0,1:T(8,128)(4,1)} %copy-done.3) | copy-start | bytes 3145732
  45.2 5.1 %copy-start.19 = (bf16[1024,128]{1,0:T(8,128)(2,1)S(1)}, bf16[1024,128]{1,0:T(8,128)(2,1)}, u32[]{:S(2)}) copy-start(bf16[1024,128]{1,0:T(8,128)(2,1)} %param.24) | copy-start | bytes 786436
  45.3 83.7 %all-to-all-start.1 = ((bf16[32,128,768]{2,1,0:T(8,128)(2,1)}), bf16[32,128,768]{2,1,0:T(8,128)(2,1)}, u32[]{:S(2)}, u32[]{:S(2)}) async-start(bf16[32,128,768]{2,1,0:T(8,128)(2,1)} %pack_slices.3), calls=%async_computation.1 | async-start | bytes 12582912 | tf_op jit(solution)/shard_map/all_to_all | solution.py:429
  50.1 150.6 %reduce-scatter.3.cloned.1.call-start = ((), (), s32[]{:S(2)}) async-start(), calls=%async_computation.9 | async-start | bytes 11796480 | tf_op jit(solution)/shard_map/reduce_scatter | solution.py:481
  50.3 6.4 %slice-start = ((s8[8388608]{0:T(1024)(128)(4,1)}), s8[4194304]{0:T(1024)(128)(4,1)S(1)}, s32[]{:S(2)}) async-start(s8[8388608]{0:T(1024)(128)(4,1)} %bitcast.131), calls=%async_computation.11 | async-start | bytes 8388608
  50.3 7.5 %slice-start.1 = ((s8[8388608]{0:T(1024)(128)(4,1)}), s8[4194304]{0:T(1024)(128)(4,1)S(1)}, s32[]{:S(2)}) async-start(s8[8388608]{0:T(1024)(128)(4,1)} %bitcast.131), calls=%async_computation.12 | async-start | bytes 8388608
  57.8 3.8 %copy-start.21 = (bf16[1024,128]{1,0:T(8,128)(2,1)S(1)}, bf16[1024,128]{1,0:T(8,128)(2,1)}, u32[]{:S(2)}) copy-start(bf16[1024,128]{1,0:T(8,128)(2,1)} %param.23) | copy-start | bytes 786436
  64.2 3.3 copy-start.16
  64.2 3.3 copy-start.17
  64.2 3.3 copy-start.18
  129.0 41.8 %copy-start.12 = (f32[128,2]{0,1:T(2,128)S(1)}, f32[128,2]{0,1:T(2,128)}, u32[]{:S(2)}) copy-start(f32[128,2]{0,1:T(2,128)} %param.18) | copy-start | bytes 3076
  158.1 30.0 %all-to-all-start.2 = ((bf16[32,128,128]{2,1,0:T(8,128)(2,1)}), bf16[32,128,128]{2,1,0:T(8,128)(2,1)S(1)}, u32[]{:S(2)}, u32[]{:S(2)}) async-start(bf16[32,128,128]{2,1,0:T(8,128)(2,1)} %bitcast.143), calls=%async_computation.2 | async-start | bytes 2097152 | tf_op jit(solution)/shard_map/all_to_all | solution.py:429
  189.9 21.1 %all-to-all-start.3 = ((bf16[32,128,128]{2,1,0:T(8,128)(2,1)}), bf16[32,128,128]{2,1,0:T(8,128)(2,1)}, u32[]{:S(2)}, u32[]{:S(2)}) async-start(bf16[32,128,128]{2,1,0:T(8,128)(2,1)} %broadcast_in_dim.145), calls=%async_computation.4 | async-start | bytes 2097152 | tf_op jit(solution)/shard_map/all_to_all | solution.py:429
  194.4 123.0 %reduce-scatter.5.cloned.1.call-start = ((), (), s32[]{:S(2)}) async-start(), calls=%async_computation.10 | async-start | bytes 7864320 | tf_op jit(solution)/shard_map/reduce_scatter | solution.py:514
  202.0 44.8 %collective-permute-start = (bf16[128,4608]{1,0:T(8,128)(2,1)S(1)}, bf16[128,4608]{1,0:T(8,128)(2,1)S(1)}, u32[]{:S(2)}, u32[]{:S(2)}) collective-permute-start(bf16[128,4608]{1,0:T(8,128)(2,1)S(1)} %dynamic-slice_bitcast_fusion), channel_id=1, source_target_pairs={{0,16},{16,0},{1,17},{17,1},{2,18},{18,2},{3,19},{19,3},{4,20},{20... | collective-permute-start | bytes 3538952 | tf_op jit(solution)/shard_map/ppermute | solution.py:493
  246.8 5.7 %copy-start.15 = (s32[128,2]{0,1:T(2,128)S(1)}, s32[128,2]{0,1:T(2,128)}, u32[]{:S(2)}) copy-start(s32[128,2]{0,1:T(2,128)} %param.17) | copy-start | bytes 3076
  247.8 69.5 %all-to-all-start.4 = ((bf16[32,128,640]{2,1,0:T(8,128)(2,1)}), bf16[32,128,640]{2,1,0:T(8,128)(2,1)}, u32[]{:S(2)}, u32[]{:S(2)}) async-start(bf16[32,128,640]{2,1,0:T(8,128)(2,1)} %bitcast.134), calls=%async_computation.5 | async-start | bytes 10485760 | tf_op jit(solution)/shard_map/all_to_all | solution.py:429
  252.5 74.3 %copy-start.13 = (f32[128,2]{0,1:T(2,128)}, f32[128,2]{0,1:T(2,128)S(1)}, u32[]{:S(2)}) copy-start(f32[128,2]{0,1:T(2,128)S(1)} %fusion.53) | copy-start | bytes 3076
  317.4 28.7 %all-to-all-start.5 = ((bf16[32,32,768]{2,1,0:T(8,128)(2,1)}), bf16[32,32,768]{2,1,0:T(8,128)(2,1)S(1)}, u32[]{:S(2)}, u32[]{:S(2)}) async-start(bf16[32,32,768]{2,1,0:T(8,128)(2,1)} %bitcast.139), calls=%async_computation.7 | async-start | bytes 3145728 | tf_op jit(solution)/shard_map/all_to_all | solution.py:429
  323.1 2.0 copy-start.5
  323.1 2.3 copy-start.7
  346.0 1.2 copy-start.1
  (3 other events, 3.2 us)
Sparse Core Ops, SparseCore 0:
  45.1 63.2 all-gather.1
  110.9 89.7 reduce-scatter.2
  247.0 61.8 reduce-scatter.4

commit v5 on v4

--- a/solution.py
+++ b/solution.py
@@ -178,6 +178,48 @@
     )(blocks, blocks)
 
 
+def unpack_rows_kernel(main_ref, rem_ref, out_ref):
+    step = pl.program_id(0)
+
+    @pl.when(step < 8)
+    def _():
+        for q in range(4):
+            out_ref[:, 512 * q : 512 * q + 512] = main_ref[q, 0:128]
+
+    @pl.when(step == 8)
+    def _():
+        first = lanes_of((16, 128)) < 64
+        for d in range(16):
+            for b in range(8):
+                tile = slice(128 * (b // 2), 128 * (b // 2) + 128)
+                low = rem_ref[2 * d, :, tile].astype(F32)
+                high = rem_ref[2 * d + 1, :, tile].astype(F32)
+                if b % 2:
+                    low = pltpu.roll(low, 64, 1)
+                else:
+                    high = pltpu.roll(high, 64, 1)
+                both = jnp.where(first, low, high).astype(BF16)
+                out_ref[16 * b : 16 * b + 16, 128 * d : 128 * d + 128] = both
+
+
+def unpack_rows(blocks):
+    return pl.pallas_call(
+        unpack_rows_kernel,
+        grid=(9,),
+        in_specs=[
+            pl.BlockSpec((4, 144, 512), lambda i: (jnp.minimum(i, 7), 0, 0)),
+            pl.BlockSpec((SLICES, 16, 512), lambda i: (0, 8, 0), pipeline_mode=pl.Buffered(1)),
+        ],
+        out_specs=pl.BlockSpec((128, 2048), lambda i: (0, i)),
+        out_shape=jax.ShapeDtypeStruct((128, 18432), BF16),
+        compiler_params=pltpu.CompilerParams(vmem_limit_bytes=VMEM),
+        cost_estimate=pl.CostEstimate(
+            flops=128 * 18432, bytes_accessed=128 * 4 * 19000, transcendentals=0
+        ),
+        name="unpack_rows",
+    )(blocks, blocks)
+
+
 def hot(shape, axis, *slots):
     places = lax.broadcasted_iota(jnp.int32, shape, axis)
     found = places == slots[0]
@@ -366,7 +408,15 @@
         def body(q, carry):
             both = hot((256, SLOTS), 1, *slots_in_columns(t_ref[pair_at(q)]))
             g = gs_ref[:, q].reshape(SLOTS, HWIDE)
-            hidden_ref[pair_at(q)] = jnp.dot(both, g, preferred_element_type=F32).astype(BF16)
+            out = jnp.dot(both, g, preferred_element_type=F32)
+            for h in range(2):
+                block = out[128 * h : 128 * h + 128]
+                hidden_ref[2 * q + h, 0:128] = block[:, 0:512].astype(BF16)
+                for c in range(4):
+                    low = block[32 * c : 32 * c + 16, 512:640]
+                    high = pltpu.roll(block[32 * c + 16 : 32 * c + 32, 512:640], 64, 1)
+                    both_halves = jnp.where(lanes_of((16, 128)) < 64, low, high).astype(BF16)
+                    hidden_ref[2 * q + h, 128:144, 128 * c : 128 * c + 128] = both_halves
             return carry
 
         lax.fori_loop(0, PAIRS, body, 0, unroll=UNROLL)
@@ -386,11 +436,11 @@
         ],
         out_specs=[
             pl.BlockSpec((256 * STEP, WIDTH), lambda i: (i, 0)),
-            pl.BlockSpec((rows, HWIDE), lambda i: (0, 0), pipeline_mode=once),
+            pl.BlockSpec((SLICES, 144, 512), lambda i: (0, 0, 0), pipeline_mode=once),
         ],
         out_shape=[
             jax.ShapeDtypeStruct((GROUPS * 256, WIDTH), BF16),
-            jax.ShapeDtypeStruct((rows, HWIDE), BF16),
+            jax.ShapeDtypeStruct((SLICES, 144, 512), BF16),
         ],
         scratch_shapes=[
             pltpu.VMEM((GROUPS, PAIRS, PAIR_ROWS, 128), BF16),
@@ -512,10 +562,10 @@
         (factor_part, hidden_part, passed)
     )
     factor_rows = lax.psum_scatter(factor_part, LINE, scatter_dimension=0, tiled=True)
-    hidden_back = exchange(hidden_part.reshape(SLICES, tok_rows, HWIDE), PLANE)
+    hidden_back = exchange(hidden_part, PLANE)
     factor_back = exchange(factor_rows.reshape(SLICES, RANK, WIDTH), PLANE)
 
-    gated_hidden_gradient = unpack(hidden_back)
+    gated_hidden_gradient = unpack_rows(hidden_back)
     down_factor_grad = unpack(factor_back).T
     up_main = factor_back[:, :, 640:768].transpose(1, 0, 2).reshape(RANK, 4096)
     up_rest = factor_back[:, :, 576:592].transpose(1, 0, 2).reshape(RANK, 512)

time: 359 us -> 353 us (0.983)
  waiting for transfers between devices: 157 us -> 149 us
    all_to_all x6, waiting for transfers between devices: 150 us -> 143 us  [exchange(): return lax.all_to_all(x, axes, split_axis=0, concat_axis=0, tiled=True)]
    pallas_call x0 -> x1, Pallas kernels: none -> 7.31 us  [unpack_rows(): pl.pallas_call(unpack_rows_kernel, grid=(9,), in_specs=[pl.BlockSpec((4,...]
    pallas_call x2 -> x1, Pallas kernels: 9.46 us -> 3.71 us  [unpack(): pl.pallas_call(unpack_kernel, grid=(5,), in_specs=[pl.BlockSpec((8, rows,...]
  transfers between devices with their start and end apart: 10 -> 10, of which waited for: 7 -> 7; matrix products, arithmetic and copies ran while one was open for 11% -> 12% of each run, Pallas kernels for 25% -> 26%
where the time goes in v5:
time: 353 us; the launch traced here: 352 us
  waiting for transfers between devices  149 us (42%)
  Pallas kernels  98.6 us (28%)
  starting transfers between devices  43 us (12%)
  matrix products  24.8 us (7%)
  between operations  14.3 us (4%)
  other arithmetic  13 us (4%)
  local copies, waits for them, and re-layouts  8.8 us (2%)
    all_to_all x6, waiting for transfers between devices, exchange(): return lax.all_to_all(x, axes, split_axis=0, concat_axis=0, tiled=True)  143 us
    all_to_all x6, starting transfers between devices, exchange(): return lax.all_to_all(x, axes, split_axis=0, concat_axis=0, tiled=True)  41.4 us
    pallas_call x1, Pallas kernels, gradients(): pl.pallas_call(gradients_kernel, grid=(GROUPS // STEP,), in_specs=[pl.Blo...  36.1 us
    pallas_call x1, Pallas kernels, contract(): pl.pallas_call(contract_kernel, grid=(GROUPS // STEP,), in_specs=[pl.Bloc...  29.1 us
    pallas_call x1, Pallas kernels, spread(): pl.pallas_call(spread_kernel, grid=(PAIRS // 2,), in_specs=[pl.BlockSpec(...  12.7 us
    pallas_call x2, Pallas kernels, pack(): pl.pallas_call(pack_kernel, grid=(4,), in_specs=[pl.BlockSpec((rows, 4096...  9.68 us
    dot_general x1, matrix products, attend_backward(): jnp.einsum('te,de->td', grads, maps, preferred_element_type=jnp.float32)  7.6 us
    pallas_call x1, Pallas kernels, unpack_rows(): pl.pallas_call(unpack_rows_kernel, grid=(9,), in_specs=[pl.BlockSpec((4,...  7.31 us
  transfers between devices with their start and end apart: 10, of which 7 were waited for; matrix products, arithmetic and copies ran while one was open for 12% of the time, Pallas kernels for 26%

profile of v5, /device:TPU:1, one launch (start us, length us, event | category | flops | bytes accessed | tf_op | source)
XLA Modules:
  0.0 351.6 jit_solution(5371038403233634992)
XLA Ops:
  7.8 3.6 %pack_slices.2 = bf16[32,32,768]{2,1,0:T(8,128)(2,1)} custom-call(bf16[32,18432]{1,0:T(8,128)(2,1)} %bitcast.133, bf16[32,18432]{1,0:T(8,128)(2,1)} %bitcast.134, bf16[32,4608]{1,0:T(8,128)(2,1)} %bitcast.138, bf16[32,4608]{1,0:T(8,128)(2,1)} %bitcast.139, f32[32,128]{1,0:T(8,128)} %broadcast_in_dim.124.id_ref), custom_call_target="tpu_custom_call" | custom-call | flops 1572864 | bytes 3145728 | tf_op jit(solution)/shard_map/pack_slices/pallas_call | solution.py:125
  11.4 9.4 %all-to-all-start = ((bf16[32,32,768]{2,1,0:T(8,128)(2,1)}), bf16[32,32,768]{2,1,0:T(8,128)(2,1)S(1)}, u32[]{:S(2)}, u32[]{:S(2)}) async-start(bf16[32,32,768]{2,1,0:T(8,128)(2,1)} %pack_slices.2), calls=%async_computation | async-start | bytes 3145728 | tf_op jit(solution)/shard_map/all_to_all | solution.py:479
  23.6 6.1 %pack_slices.3 = bf16[32,128,768]{2,1,0:T(8,128)(2,1)} custom-call(bf16[128,18432]{1,0:T(8,128)(2,1)} %hr_ref.1, bf16[128,18432]{1,0:T(8,128)(2,1)} %hr_ref.1, bf16[128,4608]{1,0:T(8,128)(2,1)} %gr_ref.1, bf16[128,4608]{1,0:T(8,128)(2,1)} %gr_ref.1, f32[128,128]{1,0:T(8,128)} %select_select_fusion.id_ref), custom_call_target="tpu_custom_call" | custom-call | flops 6291456 | bytes 12582912 | tf_op jit(solution)/shard_map/pack_slices/pallas_call | solution.py:125
  30.3 3.2 fusion
  33.5 4.2 %multiply_bitcast_fusion = f32[1,2,1024,1024]{2,3,1,0:T(8,128)} fusion(f32[1024,1024,2]{1,0,2:T(8,128)S(1)} %get-tuple-element.54), kind=kLoop, calls=%fused_computation.11 | loop fusion | flops 2097152 | bytes 16777216 | tf_op jit(solution)/shard_map/mul | solution.py:46
  37.7 6.1 %all-to-all-done = bf16[32,32,768]{2,1,0:T(8,128)(2,1)S(1)} async-done(((bf16[32,32,768]{2,1,0:T(8,128)(2,1)}), bf16[32,32,768]{2,1,0:T(8,128)(2,1)S(1)}, u32[]{:S(2)}, u32[]{:S(2)}) %all-to-all-start) | async-done | bytes 1572896 | tf_op jit(solution)/shard_map/all_to_all | solution.py:479
  45.3 4.8 %all-to-all-start.1 = ((bf16[32,128,768]{2,1,0:T(8,128)(2,1)}), bf16[32,128,768]{2,1,0:T(8,128)(2,1)}, u32[]{:S(2)}, u32[]{:S(2)}) async-start(bf16[32,128,768]{2,1,0:T(8,128)(2,1)} %pack_slices.3), calls=%async_computation.1 | async-start | bytes 12582912 | tf_op jit(solution)/shard_map/all_to_all | solution.py:479
  50.4 6.3 %fusion.1 = (f32[2,1024]{1,0:T(2,128)S(1)}, f32[1024,1024,2]{1,0,2:T(8,128)S(1)}) fusion(f32[2,1024]{1,0:T(2,128)S(1)} %get-tuple-element.53, f32[1,2,1024,1024]{2,3,1,0:T(8,128)} %multiply_bitcast_fusion, pred[1024,1024]{0,1:T(8,128)(4,1)S(1)} %copy-done.4, bf16[1024,2,128]{0,2,1:T(8,128)(2,1)S(1)} %bitcast.145, bf16[1024,128]{1,0:T(8,128)(2,1)S(1)} %copy-done.19), kind=kOutput, calls=%fused_computation.5 | convolution fusion | flops 549451776 | bytes 18628608 | tf_op jit(solution)/shard_map/ikgd,jkd->kgij/dot_general | solution.py:74
  57.8 3.8 %fusion.10 = bf16[2,1024,1024]{1,2,0:T(8,128)(2,1)S(1)} fusion(f32[1,2,1024,1024]{2,3,1,0:T(8,128)S(1)} %bitcast.131, f32[1024,1024,2]{1,0,2:T(8,128)S(1)} %get-tuple-element.56, f32[2,1024]{1,0:T(2,128)S(1)} %get-tuple-element.55, f32[2,1024]{1,0:T(2,128)S(1)} %get-tuple-element.53, pred[1024,1024]{0,1:T(8,128)(4,1)S(1)} %copy-done.4), kind=kLoop, calls=%fused_computation.18 | loop fusion | flops 20971520 | bytes 22036480 | tf_op jit(solution)/shard_map/reshape.13
  62.7 1.5 fusion.25
  64.2 3.3 fusion.22
  67.5 7.6 %convolution_convert_fusion = bf16[1024,4608]{1,0:T(8,128)(2,1)} fusion(bf16[4608,128]{1,0:T(8,128)(2,1)S(1)} %copy-done.17, bf16[4608,128]{1,0:T(8,128)(2,1)S(1)} %copy-done.18, bf16[4608,256]{1,0:T(8,128)(2,1)S(1)} %copy-done.16, bf16[1024,128]{0,1:T(8,128)(2,1)S(1)} %fusion.22, bf16[1024,128]{0,1:T(8,128)(2,1)S(1)} %fusion.25, ...), kind=kOutput, calls=%fused_computation | convolution fusion | flops 4853858304 | bytes 15204352 | tf_op jit(solution)/shard_map/te,de->td/dot_general | solution.py:101
  75.2 53.8 %all-to-all-done.1 = bf16[32,128,768]{2,1,0:T(8,128)(2,1)} async-done(((bf16[32,128,768]{2,1,0:T(8,128)(2,1)}), bf16[32,128,768]{2,1,0:T(8,128)(2,1)}, u32[]{:S(2)}, u32[]{:S(2)}) %all-to-all-start.1) | async-done | bytes 6291488 | tf_op jit(solution)/shard_map/all_to_all | solution.py:479
  129.0 29.1 %contract_experts.1 = bf16[4096,128]{1,0:T(8,128)(2,1)} custom-call(bf16[4096,768]{1,0:T(8,128)(2,1)} %bitcast.15.x_ref.t_ref, bf16[4096,768]{1,0:T(8,128)(2,1)} %all-gather.2.cloned.1.call-done.w_ref), custom_call_target="tpu_custom_call" | custom-call | flops 193273528320 | bytes 12582912 | tf_op jit(solution)/shard_map/contract_experts/pallas_call | solution.py:338
  158.1 12.7 %all-to-all-start.2 = ((bf16[32,128,128]{2,1,0:T(8,128)(2,1)}), bf16[32,128,128]{2,1,0:T(8,128)(2,1)S(1)}, u32[]{:S(2)}, u32[]{:S(2)}) async-start(bf16[32,128,128]{2,1,0:T(8,128)(2,1)} %bitcast.141), calls=%async_computation.2 | async-start | bytes 2097152 | tf_op jit(solution)/shard_map/all_to_all | solution.py:479
  170.9 12.7 %spread_rows.1.x_ref = bf16[16,16,48,768]{3,2,1,0:T(8,128)(2,1)} custom-call(bf16[4096,768]{1,0:T(8,128)(2,1)} %bitcast.15.x_ref.t_ref), custom_call_target="tpu_custom_call" | custom-call | flops 4831838208 | bytes 25165824 | tf_op jit(solution)/shard_map/spread_rows/pallas_call | solution.py:272
  183.6 4.5 %all-to-all-done.2 = bf16[32,128,128]{2,1,0:T(8,128)(2,1)S(1)} async-done(((bf16[32,128,128]{2,1,0:T(8,128)(2,1)}), bf16[32,128,128]{2,1,0:T(8,128)(2,1)S(1)}, u32[]{:S(2)}, u32[]{:S(2)}) %all-to-all-start.2) | async-done | bytes 1048608 | tf_op jit(solution)/shard_map/all_to_all | solution.py:479
  188.7 1.2 broadcast_in_dim.145
  189.9 4.4 %all-to-all-start.3 = ((bf16[32,128,128]{2,1,0:T(8,128)(2,1)}), bf16[32,128,128]{2,1,0:T(8,128)(2,1)}, u32[]{:S(2)}, u32[]{:S(2)}) async-start(bf16[32,128,128]{2,1,0:T(8,128)(2,1)} %broadcast_in_dim.145), calls=%async_computation.4 | async-start | bytes 2097152 | tf_op jit(solution)/shard_map/all_to_all | solution.py:479
  194.4 6.2 %reduce-scatter.3.cloned.1.call-done = bf16[256,4608]{1,0:T(8,128)(2,1)} async-done(((bf16[1024,4608]{1,0:T(8,128)(2,1)}), bf16[256,4608]{1,0:T(8,128)(2,1)}) %reduce-scatter.3.cloned.1.call-update) | async-done | bytes 2359312 | tf_op jit(solution)/shard_map/reduce_scatter | solution.py:531
  200.6 1.3 dynamic-slice_bitcast_fusion
  202.0 1.3 collective-permute-start
  203.3 7.8 %all-to-all-done.3 = bf16[32,128,128]{2,1,0:T(8,128)(2,1)} async-done(((bf16[32,128,128]{2,1,0:T(8,128)(2,1)}), bf16[32,128,128]{2,1,0:T(8,128)(2,1)}, u32[]{:S(2)}, u32[]{:S(2)}) %all-to-all-start.3) | async-done | bytes 1048608 | tf_op jit(solution)/shard_map/all_to_all | solution.py:479
  211.0 36.1 %factor_and_hidden_gradients.1 = (bf16[4096,768]{1,0:T(8,128)(2,1)}, bf16[32,144,512]{2,1,0:T(8,128)(2,1)}) custom-call(bf16[4096,768]{1,0:T(8,128)(2,1)} %bitcast.15.x_ref.t_ref, bf16[4096,128]{1,0:T(8,128)(2,1)} %bitcast.40.d_ref, bf16[16,16,48,768]{3,2,1,0:T(8,128)(2,1)} %spread_rows.1.x_ref, bf16[4096,768]{1,0:T(8,128)(2,1)} %all-gather.2.cloned.1.call-done.w_ref), custom_call_target="tpu_custom_call" | custom-call | flops 38654705664 | bytes 44040192 | tf_op jit(solution)/shard_map/factor_and_hidden_gradients/pallas_call | solution.py:428
  248.1 4.6 %all-to-all-start.4 = ((bf16[32,144,512]{2,1,0:T(8,128)(2,1)}), bf16[32,144,512]{2,1,0:T(8,128)(2,1)}, u32[]{:S(2)}, u32[]{:S(2)}) async-start(bf16[32,144,512]{2,1,0:T(8,128)(2,1)} %get-tuple-element.33), calls=%async_computation.5 | async-start | bytes 9437184 | tf_op jit(solution)/shard_map/all_to_all | solution.py:479
  253.0 58.9 %all-to-all-done.4.main_ref.rem_ref = bf16[32,144,512]{2,1,0:T(8,128)(2,1)} async-done(((bf16[32,144,512]{2,1,0:T(8,128)(2,1)}), bf16[32,144,512]{2,1,0:T(8,128)(2,1)}, u32[]{:S(2)}, u32[]{:S(2)}) %all-to-all-start.4) | async-done | bytes 4718624 | tf_op jit(solution)/shard_map/all_to_all | solution.py:479
  311.8 5.4 %all-to-all-start.5 = ((bf16[32,32,768]{2,1,0:T(8,128)(2,1)}), bf16[32,32,768]{2,1,0:T(8,128)(2,1)S(1)}, u32[]{:S(2)}, u32[]{:S(2)}) async-start(bf16[32,32,768]{2,1,0:T(8,128)(2,1)} %bitcast.137), calls=%async_computation.7 | async-start | bytes 3145728 | tf_op jit(solution)/shard_map/all_to_all | solution.py:479
  317.2 1.9 convolution_add_fusion
  319.6 1.4 fusion.16
  320.9 7.3 %unpack_rows.1 = bf16[128,18432]{1,0:T(8,128)(2,1)} custom-call(bf16[32,144,512]{2,1,0:T(8,128)(2,1)} %all-to-all-done.4.main_ref.rem_ref, bf16[32,144,512]{2,1,0:T(8,128)(2,1)} %all-to-all-done.4.main_ref.rem_ref), custom_call_target="tpu_custom_call" | custom-call | flops 2359296 | bytes 9728000 | tf_op jit(solution)/shard_map/unpack_rows/pallas_call | solution.py:206
  328.2 11.9 %all-to-all-done.5.main_ref.rem_ref = bf16[32,32,768]{2,1,0:T(8,128)(2,1)S(1)} async-done(((bf16[32,32,768]{2,1,0:T(8,128)(2,1)}), bf16[32,32,768]{2,1,0:T(8,128)(2,1)S(1)}, u32[]{:S(2)}, u32[]{:S(2)}) %all-to-all-start.5) | async-done | bytes 1572896 | tf_op jit(solution)/shard_map/all_to_all | solution.py:479
  341.4 3.7 %unpack_slices.1 = bf16[32,18432]{1,0:T(8,128)(2,1)} custom-call(bf16[32,32,768]{2,1,0:T(8,128)(2,1)} %copy-done.1, bf16[32,32,768]{2,1,0:T(8,128)(2,1)} %copy-done.1), custom_call_target="tpu_custom_call" | custom-call | flops 589824 | bytes 2432000 | tf_op jit(solution)/shard_map/unpack_slices/pallas_call | solution.py:164
  (94 shorter events, 11.1 us)
Async XLA Ops:
  7.2 310.0 %copy-start = (bf16[4608,128]{1,0:T(8,128)(2,1)S(1)}, bf16[4608,128]{1,0:T(8,128)(2,1)}, u32[]{:S(2)}) copy-start(bf16[4608,128]{1,0:T(8,128)(2,1)} %param.21) | copy-start | bytes 3538948
  7.2 13.8 %copy-start.14 = (s32[128,2]{0,1:T(2,128)S(1)}, s32[128,2]{0,1:T(2,128)}, u32[]{:S(2)}) copy-start(s32[128,2]{0,1:T(2,128)} %param.17) | copy-start | bytes 3076
  7.2 13.9 %copy-start.22 = (s32[1,8]{1,0:T(1,128)S(1)}, s32[1,8]{1,0:T(1,128)}, u32[]{:S(2)}) copy-start(s32[1,8]{1,0:T(1,128)} %param.29) | copy-start | bytes 100
  7.2 14.6 %copy-start.8 = (bf16[1024,256]{1,0:T(8,128)(2,1)S(1)}, bf16[1024,256]{1,0:T(8,128)(2,1)}, u32[]{:S(2)}) copy-start(bf16[1024,256]{1,0:T(8,128)(2,1)} %param.22) | copy-start | bytes 1572868
  11.4 32.4 %all-to-all-start = ((bf16[32,32,768]{2,1,0:T(8,128)(2,1)}), bf16[32,32,768]{2,1,0:T(8,128)(2,1)S(1)}, u32[]{:S(2)}, u32[]{:S(2)}) async-start(bf16[32,32,768]{2,1,0:T(8,128)(2,1)} %pack_slices.2), calls=%async_computation | async-start | bytes 3145728 | tf_op jit(solution)/shard_map/all_to_all | solution.py:479
  20.9 108.1 %all-gather.2.cloned.1.call-start = ((), (), s32[]{:S(2)}) async-start(), calls=%async_computation.8 | async-start | bytes 7864320 | tf_op jit(solution)/shard_map/all_gather | solution.py:517
  23.6 6.7 %copy-start.10 = (bf16[1024,256]{0,1:T(8,128)(2,1)S(1)}, bf16[1024,256]{0,1:T(8,128)(2,1)}, u32[]{:S(2)}) copy-start(bf16[1024,256]{0,1:T(8,128)(2,1)} %copy.53) | copy-start | bytes 1572868
  23.6 6.7 %copy-start.20 = (bf16[1024,128]{1,0:T(8,128)(2,1)S(1)}, bf16[1024,128]{1,0:T(8,128)(2,1)}, u32[]{:S(2)}) copy-start(bf16[1024,128]{1,0:T(8,128)(2,1)} %param.23) | copy-start | bytes 786436
  30.2 3.2 copy-start.3
  33.5 11.5 %copy-start.9 = (bf16[1024,256]{1,0:T(8,128)(2,1)S(1)}, bf16[1024,256]{1,0:T(8,128)(2,1)}, u32[]{:S(2)}) copy-start(bf16[1024,256]{1,0:T(8,128)(2,1)} %param.25) | copy-start | bytes 1572868
  45.2 5.1 %copy-start.4 = (pred[1024,1024]{0,1:T(8,128)(4,1)S(1)}, pred[1024,1024]{0,1:T(8,128)(4,1)}, u32[]{:S(2)}) copy-start(pred[1024,1024]{0,1:T(8,128)(4,1)} %copy-done.3) | copy-start | bytes 3145732
  45.2 5.1 %copy-start.19 = (bf16[1024,128]{1,0:T(8,128)(2,1)S(1)}, bf16[1024,128]{1,0:T(8,128)(2,1)}, u32[]{:S(2)}) copy-start(bf16[1024,128]{1,0:T(8,128)(2,1)} %param.24) | copy-start | bytes 786436
  45.3 83.7 %all-to-all-start.1 = ((bf16[32,128,768]{2,1,0:T(8,128)(2,1)}), bf16[32,128,768]{2,1,0:T(8,128)(2,1)}, u32[]{:S(2)}, u32[]{:S(2)}) async-start(bf16[32,128,768]{2,1,0:T(8,128)(2,1)} %pack_slices.3), calls=%async_computation.1 | async-start | bytes 12582912 | tf_op jit(solution)/shard_map/all_to_all | solution.py:479
  50.1 150.6 %reduce-scatter.3.cloned.1.call-start = ((), (), s32[]{:S(2)}) async-start(), calls=%async_computation.9 | async-start | bytes 11796480 | tf_op jit(solution)/shard_map/reduce_scatter | solution.py:531
  50.3 6.4 %slice-start = ((s8[8388608]{0:T(1024)(128)(4,1)}), s8[4194304]{0:T(1024)(128)(4,1)S(1)}, s32[]{:S(2)}) async-start(s8[8388608]{0:T(1024)(128)(4,1)} %bitcast.130), calls=%async_computation.11 | async-start | bytes 8388608
  50.3 7.5 %slice-start.1 = ((s8[8388608]{0:T(1024)(128)(4,1)}), s8[4194304]{0:T(1024)(128)(4,1)S(1)}, s32[]{:S(2)}) async-start(s8[8388608]{0:T(1024)(128)(4,1)} %bitcast.130), calls=%async_computation.12 | async-start | bytes 8388608
  57.8 3.8 %copy-start.21 = (bf16[1024,128]{1,0:T(8,128)(2,1)S(1)}, bf16[1024,128]{1,0:T(8,128)(2,1)}, u32[]{:S(2)}) copy-start(bf16[1024,128]{1,0:T(8,128)(2,1)} %param.23) | copy-start | bytes 786436
  64.2 3.3 copy-start.16
  64.2 3.3 copy-start.17
  64.2 3.3 copy-start.18
  129.0 41.8 %copy-start.12 = (f32[128,2]{0,1:T(2,128)S(1)}, f32[128,2]{0,1:T(2,128)}, u32[]{:S(2)}) copy-start(f32[128,2]{0,1:T(2,128)} %param.18) | copy-start | bytes 3076
  158.1 30.0 %all-to-all-start.2 = ((bf16[32,128,128]{2,1,0:T(8,128)(2,1)}), bf16[32,128,128]{2,1,0:T(8,128)(2,1)S(1)}, u32[]{:S(2)}, u32[]{:S(2)}) async-start(bf16[32,128,128]{2,1,0:T(8,128)(2,1)} %bitcast.141), calls=%async_computation.2 | async-start | bytes 2097152 | tf_op jit(solution)/shard_map/all_to_all | solution.py:479
  189.9 21.1 %all-to-all-start.3 = ((bf16[32,128,128]{2,1,0:T(8,128)(2,1)}), bf16[32,128,128]{2,1,0:T(8,128)(2,1)}, u32[]{:S(2)}, u32[]{:S(2)}) async-start(bf16[32,128,128]{2,1,0:T(8,128)(2,1)} %broadcast_in_dim.145), calls=%async_computation.4 | async-start | bytes 2097152 | tf_op jit(solution)/shard_map/all_to_all | solution.py:479
  194.4 117.5 %reduce-scatter.5.cloned.1.call-start = ((), (), s32[]{:S(2)}) async-start(), calls=%async_computation.10 | async-start | bytes 7864320 | tf_op jit(solution)/shard_map/reduce_scatter | solution.py:564
  202.0 45.1 %collective-permute-start = (bf16[128,4608]{1,0:T(8,128)(2,1)S(1)}, bf16[128,4608]{1,0:T(8,128)(2,1)S(1)}, u32[]{:S(2)}, u32[]{:S(2)}) collective-permute-start(bf16[128,4608]{1,0:T(8,128)(2,1)S(1)} %dynamic-slice_bitcast_fusion), channel_id=1, source_target_pairs={{0,16},{16,0},{1,17},{17,1},{2,18},{18,2},{3,19},{19,3},{4,20},{20... | collective-permute-start | bytes 3538952 | tf_op jit(solution)/shard_map/ppermute | solution.py:543
  247.1 5.7 %copy-start.15 = (s32[128,2]{0,1:T(2,128)S(1)}, s32[128,2]{0,1:T(2,128)}, u32[]{:S(2)}) copy-start(s32[128,2]{0,1:T(2,128)} %param.17) | copy-start | bytes 3076
  248.1 63.7 %all-to-all-start.4 = ((bf16[32,144,512]{2,1,0:T(8,128)(2,1)}), bf16[32,144,512]{2,1,0:T(8,128)(2,1)}, u32[]{:S(2)}, u32[]{:S(2)}) async-start(bf16[32,144,512]{2,1,0:T(8,128)(2,1)} %get-tuple-element.33), calls=%async_computation.5 | async-start | bytes 9437184 | tf_op jit(solution)/shard_map/all_to_all | solution.py:479
  252.8 68.1 %copy-start.13 = (f32[128,2]{0,1:T(2,128)}, f32[128,2]{0,1:T(2,128)S(1)}, u32[]{:S(2)}) copy-start(f32[128,2]{0,1:T(2,128)S(1)} %fusion.53) | copy-start | bytes 3076
  311.8 28.3 %all-to-all-start.5 = ((bf16[32,32,768]{2,1,0:T(8,128)(2,1)}), bf16[32,32,768]{2,1,0:T(8,128)(2,1)S(1)}, u32[]{:S(2)}, u32[]{:S(2)}) async-start(bf16[32,32,768]{2,1,0:T(8,128)(2,1)} %bitcast.137), calls=%async_computation.7 | async-start | bytes 3145728 | tf_op jit(solution)/shard_map/all_to_all | solution.py:479
  317.2 2.0 copy-start.5
  317.2 2.3 copy-start.7
  340.2 1.2 copy-start.1
  (3 other events, 3.2 us)
Sparse Core Ops, SparseCore 0:
  45.1 63.2 all-gather.1
  110.9 89.7 reduce-scatter.2
  247.3 61.9 reduce-scatter.4

commit v6 on v5

--- a/solution.py
+++ b/solution.py
@@ -22,7 +22,7 @@
 SLOTS = GROUPS * PAIR_ROWS
 GROUP_ROWS = PAIRS * PAIR_ROWS
 STEP = 4
-UNROLL = 4
+UNROLL = 8
 
 adapter_scale = 2.0
 score_cap = 50.0

time: 353 us -> 355 us (level); the launches traced: 352 us -> 350 us
  transfers between devices with their start and end apart: 10 -> 10, of which waited for: 7 -> 7; matrix products, arithmetic and copies ran while one was open for 12% -> 12% of each run, Pallas kernels for 26% -> 25%
where the time goes in v6:
time: 355 us; the launch traced here: 350 us
  waiting for transfers between devices  149 us (42%)
  Pallas kernels  96.3 us (27%)
  starting transfers between devices  43 us (12%)
  matrix products  24.8 us (7%)
  between operations  14.7 us (4%)
  other arithmetic  13 us (4%)
  local copies, waits for them, and re-layouts  8.8 us (2%)
    all_to_all x6, waiting for transfers between devices, exchange(): return lax.all_to_all(x, axes, split_axis=0, concat_axis=0, tiled=True)  142 us
    all_to_all x6, starting transfers between devices, exchange(): return lax.all_to_all(x, axes, split_axis=0, concat_axis=0, tiled=True)  41.5 us
    pallas_call x1, Pallas kernels, gradients(): pl.pallas_call(gradients_kernel, grid=(GROUPS // STEP,), in_specs=[pl.Blo...  35.1 us
    pallas_call x1, Pallas kernels, contract(): pl.pallas_call(contract_kernel, grid=(GROUPS // STEP,), in_specs=[pl.Bloc...  27.9 us
    pallas_call x1, Pallas kernels, spread(): pl.pallas_call(spread_kernel, grid=(PAIRS // 2,), in_specs=[pl.BlockSpec(...  12.7 us
    pallas_call x2, Pallas kernels, pack(): pl.pallas_call(pack_kernel, grid=(4,), in_specs=[pl.BlockSpec((rows, 4096...  9.68 us
    dot_general x1, matrix products, attend_backward(): jnp.einsum('te,de->td', grads, maps, preferred_element_type=jnp.float32)  7.6 us
    reduce_scatter x1, waiting for transfers between devices, local(): part_rows = lax.psum_scatter(part, LINE, scatter_dimension=0, tiled=True)  7.41 us
  transfers between devices with their start and end apart: 10, of which 7 were waited for; matrix products, arithmetic and copies ran while one was open for 12% of the time, Pallas kernels for 25%

profile of v6, /device:TPU:1, one launch (start us, length us, event | category | flops | bytes accessed | tf_op | source)
XLA Modules:
  0.0 349.9 jit_solution(16967245629552705110)
XLA Ops:
  7.8 3.6 %pack_slices.2 = bf16[32,32,768]{2,1,0:T(8,128)(2,1)} custom-call(bf16[32,18432]{1,0:T(8,128)(2,1)} %bitcast.133, bf16[32,18432]{1,0:T(8,128)(2,1)} %bitcast.134, bf16[32,4608]{1,0:T(8,128)(2,1)} %bitcast.138, bf16[32,4608]{1,0:T(8,128)(2,1)} %bitcast.139, f32[32,128]{1,0:T(8,128)} %broadcast_in_dim.124.id_ref), custom_call_target="tpu_custom_call" | custom-call | flops 1572864 | bytes 3145728 | tf_op jit(solution)/shard_map/pack_slices/pallas_call | solution.py:125
  11.4 9.4 %all-to-all-start = ((bf16[32,32,768]{2,1,0:T(8,128)(2,1)}), bf16[32,32,768]{2,1,0:T(8,128)(2,1)S(1)}, u32[]{:S(2)}, u32[]{:S(2)}) async-start(bf16[32,32,768]{2,1,0:T(8,128)(2,1)} %pack_slices.2), calls=%async_computation | async-start | bytes 3145728 | tf_op jit(solution)/shard_map/all_to_all | solution.py:479
  23.6 6.1 %pack_slices.3 = bf16[32,128,768]{2,1,0:T(8,128)(2,1)} custom-call(bf16[128,18432]{1,0:T(8,128)(2,1)} %hr_ref.1, bf16[128,18432]{1,0:T(8,128)(2,1)} %hr_ref.1, bf16[128,4608]{1,0:T(8,128)(2,1)} %gr_ref.1, bf16[128,4608]{1,0:T(8,128)(2,1)} %gr_ref.1, f32[128,128]{1,0:T(8,128)} %select_select_fusion.id_ref), custom_call_target="tpu_custom_call" | custom-call | flops 6291456 | bytes 12582912 | tf_op jit(solution)/shard_map/pack_slices/pallas_call | solution.py:125
  30.3 3.2 fusion
  33.5 4.2 %multiply_bitcast_fusion = f32[1,2,1024,1024]{2,3,1,0:T(8,128)} fusion(f32[1024,1024,2]{1,0,2:T(8,128)S(1)} %get-tuple-element.54), kind=kLoop, calls=%fused_computation.11 | loop fusion | flops 2097152 | bytes 16777216 | tf_op jit(solution)/shard_map/mul | solution.py:46
  37.7 6.1 %all-to-all-done = bf16[32,32,768]{2,1,0:T(8,128)(2,1)S(1)} async-done(((bf16[32,32,768]{2,1,0:T(8,128)(2,1)}), bf16[32,32,768]{2,1,0:T(8,128)(2,1)S(1)}, u32[]{:S(2)}, u32[]{:S(2)}) %all-to-all-start) | async-done | bytes 1572896 | tf_op jit(solution)/shard_map/all_to_all | solution.py:479
  45.3 4.8 %all-to-all-start.1 = ((bf16[32,128,768]{2,1,0:T(8,128)(2,1)}), bf16[32,128,768]{2,1,0:T(8,128)(2,1)}, u32[]{:S(2)}, u32[]{:S(2)}) async-start(bf16[32,128,768]{2,1,0:T(8,128)(2,1)} %pack_slices.3), calls=%async_computation.1 | async-start | bytes 12582912 | tf_op jit(solution)/shard_map/all_to_all | solution.py:479
  50.3 6.3 %fusion.1 = (f32[2,1024]{1,0:T(2,128)S(1)}, f32[1024,1024,2]{1,0,2:T(8,128)S(1)}) fusion(f32[2,1024]{1,0:T(2,128)S(1)} %get-tuple-element.53, f32[1,2,1024,1024]{2,3,1,0:T(8,128)} %multiply_bitcast_fusion, pred[1024,1024]{0,1:T(8,128)(4,1)S(1)} %copy-done.4, bf16[1024,2,128]{0,2,1:T(8,128)(2,1)S(1)} %bitcast.145, bf16[1024,128]{1,0:T(8,128)(2,1)S(1)} %copy-done.19), kind=kOutput, calls=%fused_computation.5 | convolution fusion | flops 549451776 | bytes 18628608 | tf_op jit(solution)/shard_map/ikgd,jkd->kgij/dot_general | solution.py:74
  57.8 3.8 %fusion.10 = bf16[2,1024,1024]{1,2,0:T(8,128)(2,1)S(1)} fusion(f32[1,2,1024,1024]{2,3,1,0:T(8,128)S(1)} %bitcast.131, f32[1024,1024,2]{1,0,2:T(8,128)S(1)} %get-tuple-element.56, f32[2,1024]{1,0:T(2,128)S(1)} %get-tuple-element.55, f32[2,1024]{1,0:T(2,128)S(1)} %get-tuple-element.53, pred[1024,1024]{0,1:T(8,128)(4,1)S(1)} %copy-done.4), kind=kLoop, calls=%fused_computation.18 | loop fusion | flops 20971520 | bytes 22036480 | tf_op jit(solution)/shard_map/reshape.13
  62.7 1.5 fusion.25
  64.2 3.3 fusion.22
  67.5 7.6 %convolution_convert_fusion = bf16[1024,4608]{1,0:T(8,128)(2,1)} fusion(bf16[4608,128]{1,0:T(8,128)(2,1)S(1)} %copy-done.17, bf16[4608,128]{1,0:T(8,128)(2,1)S(1)} %copy-done.18, bf16[4608,256]{1,0:T(8,128)(2,1)S(1)} %copy-done.16, bf16[1024,128]{0,1:T(8,128)(2,1)S(1)} %fusion.22, bf16[1024,128]{0,1:T(8,128)(2,1)S(1)} %fusion.25, ...), kind=kOutput, calls=%fused_computation | convolution fusion | flops 4853858304 | bytes 15204352 | tf_op jit(solution)/shard_map/te,de->td/dot_general | solution.py:101
  75.2 53.8 %all-to-all-done.1 = bf16[32,128,768]{2,1,0:T(8,128)(2,1)} async-done(((bf16[32,128,768]{2,1,0:T(8,128)(2,1)}), bf16[32,128,768]{2,1,0:T(8,128)(2,1)}, u32[]{:S(2)}, u32[]{:S(2)}) %all-to-all-start.1) | async-done | bytes 6291488 | tf_op jit(solution)/shard_map/all_to_all | solution.py:479
  129.0 27.9 %contract_experts.1 = bf16[4096,128]{1,0:T(8,128)(2,1)} custom-call(bf16[4096,768]{1,0:T(8,128)(2,1)} %bitcast.15.x_ref.t_ref, bf16[4096,768]{1,0:T(8,128)(2,1)} %all-gather.2.cloned.1.call-done.w_ref), custom_call_target="tpu_custom_call" | custom-call | flops 193273528320 | bytes 12582912 | tf_op jit(solution)/shard_map/contract_experts/pallas_call | solution.py:338
  156.8 12.8 %all-to-all-start.2 = ((bf16[32,128,128]{2,1,0:T(8,128)(2,1)}), bf16[32,128,128]{2,1,0:T(8,128)(2,1)S(1)}, u32[]{:S(2)}, u32[]{:S(2)}) async-start(bf16[32,128,128]{2,1,0:T(8,128)(2,1)} %bitcast.141), calls=%async_computation.2 | async-start | bytes 2097152 | tf_op jit(solution)/shard_map/all_to_all | solution.py:479
  169.7 12.7 %spread_rows.1.x_ref = bf16[16,16,48,768]{3,2,1,0:T(8,128)(2,1)} custom-call(bf16[4096,768]{1,0:T(8,128)(2,1)} %bitcast.15.x_ref.t_ref), custom_call_target="tpu_custom_call" | custom-call | flops 4831838208 | bytes 25165824 | tf_op jit(solution)/shard_map/spread_rows/pallas_call | solution.py:272
  182.4 4.5 %all-to-all-done.2 = bf16[32,128,128]{2,1,0:T(8,128)(2,1)S(1)} async-done(((bf16[32,128,128]{2,1,0:T(8,128)(2,1)}), bf16[32,128,128]{2,1,0:T(8,128)(2,1)S(1)}, u32[]{:S(2)}, u32[]{:S(2)}) %all-to-all-start.2) | async-done | bytes 1048608 | tf_op jit(solution)/shard_map/all_to_all | solution.py:479
  187.5 1.2 broadcast_in_dim.145
  188.7 4.4 %all-to-all-start.3 = ((bf16[32,128,128]{2,1,0:T(8,128)(2,1)}), bf16[32,128,128]{2,1,0:T(8,128)(2,1)}, u32[]{:S(2)}, u32[]{:S(2)}) async-start(bf16[32,128,128]{2,1,0:T(8,128)(2,1)} %broadcast_in_dim.145), calls=%async_computation.4 | async-start | bytes 2097152 | tf_op jit(solution)/shard_map/all_to_all | solution.py:479
  193.2 7.4 %reduce-scatter.3.cloned.1.call-done = bf16[256,4608]{1,0:T(8,128)(2,1)} async-done(((bf16[1024,4608]{1,0:T(8,128)(2,1)}), bf16[256,4608]{1,0:T(8,128)(2,1)}) %reduce-scatter.3.cloned.1.call-update) | async-done | bytes 2359312 | tf_op jit(solution)/shard_map/reduce_scatter | solution.py:531
  200.6 1.3 dynamic-slice_bitcast_fusion
  202.0 1.3 collective-permute-start
  203.2 6.6 %all-to-all-done.3 = bf16[32,128,128]{2,1,0:T(8,128)(2,1)} async-done(((bf16[32,128,128]{2,1,0:T(8,128)(2,1)}), bf16[32,128,128]{2,1,0:T(8,128)(2,1)}, u32[]{:S(2)}, u32[]{:S(2)}) %all-to-all-start.3) | async-done | bytes 1048608 | tf_op jit(solution)/shard_map/all_to_all | solution.py:479
  209.9 35.1 %factor_and_hidden_gradients.1 = (bf16[4096,768]{1,0:T(8,128)(2,1)}, bf16[32,144,512]{2,1,0:T(8,128)(2,1)}) custom-call(bf16[4096,768]{1,0:T(8,128)(2,1)} %bitcast.15.x_ref.t_ref, bf16[4096,128]{1,0:T(8,128)(2,1)} %bitcast.40.d_ref, bf16[16,16,48,768]{3,2,1,0:T(8,128)(2,1)} %spread_rows.1.x_ref, bf16[4096,768]{1,0:T(8,128)(2,1)} %all-gather.2.cloned.1.call-done.w_ref), custom_call_target="tpu_custom_call" | custom-call | flops 38654705664 | bytes 44040192 | tf_op jit(solution)/shard_map/factor_and_hidden_gradients/pallas_call | solution.py:428
  245.9 4.6 %all-to-all-start.4 = ((bf16[32,144,512]{2,1,0:T(8,128)(2,1)}), bf16[32,144,512]{2,1,0:T(8,128)(2,1)}, u32[]{:S(2)}, u32[]{:S(2)}) async-start(bf16[32,144,512]{2,1,0:T(8,128)(2,1)} %get-tuple-element.33), calls=%async_computation.5 | async-start | bytes 9437184 | tf_op jit(solution)/shard_map/all_to_all | solution.py:479
  250.8 58.9 %all-to-all-done.4.main_ref.rem_ref = bf16[32,144,512]{2,1,0:T(8,128)(2,1)} async-done(((bf16[32,144,512]{2,1,0:T(8,128)(2,1)}), bf16[32,144,512]{2,1,0:T(8,128)(2,1)}, u32[]{:S(2)}, u32[]{:S(2)}) %all-to-all-start.4) | async-done | bytes 4718624 | tf_op jit(solution)/shard_map/all_to_all | solution.py:479
  309.7 5.4 %all-to-all-start.5 = ((bf16[32,32,768]{2,1,0:T(8,128)(2,1)}), bf16[32,32,768]{2,1,0:T(8,128)(2,1)S(1)}, u32[]{:S(2)}, u32[]{:S(2)}) async-start(bf16[32,32,768]{2,1,0:T(8,128)(2,1)} %bitcast.137), calls=%async_computation.7 | async-start | bytes 3145728 | tf_op jit(solution)/shard_map/all_to_all | solution.py:479
  315.1 1.9 convolution_add_fusion
  317.4 1.4 fusion.16
  318.8 7.3 %unpack_rows.1 = bf16[128,18432]{1,0:T(8,128)(2,1)} custom-call(bf16[32,144,512]{2,1,0:T(8,128)(2,1)} %all-to-all-done.4.main_ref.rem_ref, bf16[32,144,512]{2,1,0:T(8,128)(2,1)} %all-to-all-done.4.main_ref.rem_ref), custom_call_target="tpu_custom_call" | custom-call | flops 2359296 | bytes 9728000 | tf_op jit(solution)/shard_map/unpack_rows/pallas_call | solution.py:206
  326.1 11.9 %all-to-all-done.5.main_ref.rem_ref = bf16[32,32,768]{2,1,0:T(8,128)(2,1)S(1)} async-done(((bf16[32,32,768]{2,1,0:T(8,128)(2,1)}), bf16[32,32,768]{2,1,0:T(8,128)(2,1)S(1)}, u32[]{:S(2)}, u32[]{:S(2)}) %all-to-all-start.5) | async-done | bytes 1572896 | tf_op jit(solution)/shard_map/all_to_all | solution.py:479
  339.2 3.7 %unpack_slices.1 = bf16[32,18432]{1,0:T(8,128)(2,1)} custom-call(bf16[32,32,768]{2,1,0:T(8,128)(2,1)} %copy-done.1, bf16[32,32,768]{2,1,0:T(8,128)(2,1)} %copy-done.1), custom_call_target="tpu_custom_call" | custom-call | flops 589824 | bytes 2432000 | tf_op jit(solution)/shard_map/unpack_slices/pallas_call | solution.py:164
  (94 shorter events, 11.1 us)
Async XLA Ops:
  7.2 307.9 %copy-start = (bf16[4608,128]{1,0:T(8,128)(2,1)S(1)}, bf16[4608,128]{1,0:T(8,128)(2,1)}, u32[]{:S(2)}) copy-start(bf16[4608,128]{1,0:T(8,128)(2,1)} %param.21) | copy-start | bytes 3538948
  7.2 13.8 %copy-start.14 = (s32[128,2]{0,1:T(2,128)S(1)}, s32[128,2]{0,1:T(2,128)}, u32[]{:S(2)}) copy-start(s32[128,2]{0,1:T(2,128)} %param.17) | copy-start | bytes 3076
  7.2 13.9 %copy-start.22 = (s32[1,8]{1,0:T(1,128)S(1)}, s32[1,8]{1,0:T(1,128)}, u32[]{:S(2)}) copy-start(s32[1,8]{1,0:T(1,128)} %param.29) | copy-start | bytes 100
  7.2 14.6 %copy-start.8 = (bf16[1024,256]{1,0:T(8,128)(2,1)S(1)}, bf16[1024,256]{1,0:T(8,128)(2,1)}, u32[]{:S(2)}) copy-start(bf16[1024,256]{1,0:T(8,128)(2,1)} %param.22) | copy-start | bytes 1572868
  11.4 32.4 %all-to-all-start = ((bf16[32,32,768]{2,1,0:T(8,128)(2,1)}), bf16[32,32,768]{2,1,0:T(8,128)(2,1)S(1)}, u32[]{:S(2)}, u32[]{:S(2)}) async-start(bf16[32,32,768]{2,1,0:T(8,128)(2,1)} %pack_slices.2), calls=%async_computation | async-start | bytes 3145728 | tf_op jit(solution)/shard_map/all_to_all | solution.py:479
  20.9 108.1 %all-gather.2.cloned.1.call-start = ((), (), s32[]{:S(2)}) async-start(), calls=%async_computation.8 | async-start | bytes 7864320 | tf_op jit(solution)/shard_map/all_gather | solution.py:517
  23.6 6.7 %copy-start.10 = (bf16[1024,256]{0,1:T(8,128)(2,1)S(1)}, bf16[1024,256]{0,1:T(8,128)(2,1)}, u32[]{:S(2)}) copy-start(bf16[1024,256]{0,1:T(8,128)(2,1)} %copy.53) | copy-start | bytes 1572868
  23.6 6.7 %copy-start.20 = (bf16[1024,128]{1,0:T(8,128)(2,1)S(1)}, bf16[1024,128]{1,0:T(8,128)(2,1)}, u32[]{:S(2)}) copy-start(bf16[1024,128]{1,0:T(8,128)(2,1)} %param.23) | copy-start | bytes 786436
  30.2 3.2 copy-start.3
  33.5 11.5 %copy-start.9 = (bf16[1024,256]{1,0:T(8,128)(2,1)S(1)}, bf16[1024,256]{1,0:T(8,128)(2,1)}, u32[]{:S(2)}) copy-start(bf16[1024,256]{1,0:T(8,128)(2,1)} %param.25) | copy-start | bytes 1572868
  45.2 5.1 %copy-start.4 = (pred[1024,1024]{0,1:T(8,128)(4,1)S(1)}, pred[1024,1024]{0,1:T(8,128)(4,1)}, u32[]{:S(2)}) copy-start(pred[1024,1024]{0,1:T(8,128)(4,1)} %copy-done.3) | copy-start | bytes 3145732
  45.2 5.1 %copy-start.19 = (bf16[1024,128]{1,0:T(8,128)(2,1)S(1)}, bf16[1024,128]{1,0:T(8,128)(2,1)}, u32[]{:S(2)}) copy-start(bf16[1024,128]{1,0:T(8,128)(2,1)} %param.24) | copy-start | bytes 786436
  45.3 83.7 %all-to-all-start.1 = ((bf16[32,128,768]{2,1,0:T(8,128)(2,1)}), bf16[32,128,768]{2,1,0:T(8,128)(2,1)}, u32[]{:S(2)}, u32[]{:S(2)}) async-start(bf16[32,128,768]{2,1,0:T(8,128)(2,1)} %pack_slices.3), calls=%async_computation.1 | async-start | bytes 12582912 | tf_op jit(solution)/shard_map/all_to_all | solution.py:479
  50.1 150.6 %reduce-scatter.3.cloned.1.call-start = ((), (), s32[]{:S(2)}) async-start(), calls=%async_computation.9 | async-start | bytes 11796480 | tf_op jit(solution)/shard_map/reduce_scatter | solution.py:531
  50.3 6.4 %slice-start = ((s8[8388608]{0:T(1024)(128)(4,1)}), s8[4194304]{0:T(1024)(128)(4,1)S(1)}, s32[]{:S(2)}) async-start(s8[8388608]{0:T(1024)(128)(4,1)} %bitcast.130), calls=%async_computation.11 | async-start | bytes 8388608
  50.3 7.5 %slice-start.1 = ((s8[8388608]{0:T(1024)(128)(4,1)}), s8[4194304]{0:T(1024)(128)(4,1)S(1)}, s32[]{:S(2)}) async-start(s8[8388608]{0:T(1024)(128)(4,1)} %bitcast.130), calls=%async_computation.12 | async-start | bytes 8388608
  57.8 3.8 %copy-start.21 = (bf16[1024,128]{1,0:T(8,128)(2,1)S(1)}, bf16[1024,128]{1,0:T(8,128)(2,1)}, u32[]{:S(2)}) copy-start(bf16[1024,128]{1,0:T(8,128)(2,1)} %param.23) | copy-start | bytes 786436
  64.2 3.3 copy-start.16
  64.2 3.3 copy-start.17
  64.2 3.3 copy-start.18
  129.0 40.7 %copy-start.12 = (f32[128,2]{0,1:T(2,128)S(1)}, f32[128,2]{0,1:T(2,128)}, u32[]{:S(2)}) copy-start(f32[128,2]{0,1:T(2,128)} %param.18) | copy-start | bytes 3076
  156.8 30.0 %all-to-all-start.2 = ((bf16[32,128,128]{2,1,0:T(8,128)(2,1)}), bf16[32,128,128]{2,1,0:T(8,128)(2,1)S(1)}, u32[]{:S(2)}, u32[]{:S(2)}) async-start(bf16[32,128,128]{2,1,0:T(8,128)(2,1)} %bitcast.141), calls=%async_computation.2 | async-start | bytes 2097152 | tf_op jit(solution)/shard_map/all_to_all | solution.py:479
  188.7 21.1 %all-to-all-start.3 = ((bf16[32,128,128]{2,1,0:T(8,128)(2,1)}), bf16[32,128,128]{2,1,0:T(8,128)(2,1)}, u32[]{:S(2)}, u32[]{:S(2)}) async-start(bf16[32,128,128]{2,1,0:T(8,128)(2,1)} %broadcast_in_dim.145), calls=%async_computation.4 | async-start | bytes 2097152 | tf_op jit(solution)/shard_map/all_to_all | solution.py:479
  193.2 116.5 %reduce-scatter.5.cloned.1.call-start = ((), (), s32[]{:S(2)}) async-start(), calls=%async_computation.10 | async-start | bytes 7864320 | tf_op jit(solution)/shard_map/reduce_scatter | solution.py:564
  202.0 42.9 %collective-permute-start = (bf16[128,4608]{1,0:T(8,128)(2,1)S(1)}, bf16[128,4608]{1,0:T(8,128)(2,1)S(1)}, u32[]{:S(2)}, u32[]{:S(2)}) collective-permute-start(bf16[128,4608]{1,0:T(8,128)(2,1)S(1)} %dynamic-slice_bitcast_fusion), channel_id=1, source_target_pairs={{0,16},{16,0},{1,17},{17,1},{2,18},{18,2},{3,19},{19,3},{4,20},{20... | collective-permute-start | bytes 3538952 | tf_op jit(solution)/shard_map/ppermute | solution.py:543
  245.0 5.7 %copy-start.15 = (s32[128,2]{0,1:T(2,128)S(1)}, s32[128,2]{0,1:T(2,128)}, u32[]{:S(2)}) copy-start(s32[128,2]{0,1:T(2,128)} %param.17) | copy-start | bytes 3076
  245.9 63.7 %all-to-all-start.4 = ((bf16[32,144,512]{2,1,0:T(8,128)(2,1)}), bf16[32,144,512]{2,1,0:T(8,128)(2,1)}, u32[]{:S(2)}, u32[]{:S(2)}) async-start(bf16[32,144,512]{2,1,0:T(8,128)(2,1)} %get-tuple-element.33), calls=%async_computation.5 | async-start | bytes 9437184 | tf_op jit(solution)/shard_map/all_to_all | solution.py:479
  250.6 68.1 %copy-start.13 = (f32[128,2]{0,1:T(2,128)}, f32[128,2]{0,1:T(2,128)S(1)}, u32[]{:S(2)}) copy-start(f32[128,2]{0,1:T(2,128)S(1)} %fusion.53) | copy-start | bytes 3076
  309.7 28.3 %all-to-all-start.5 = ((bf16[32,32,768]{2,1,0:T(8,128)(2,1)}), bf16[32,32,768]{2,1,0:T(8,128)(2,1)S(1)}, u32[]{:S(2)}, u32[]{:S(2)}) async-start(bf16[32,32,768]{2,1,0:T(8,128)(2,1)} %bitcast.137), calls=%async_computation.7 | async-start | bytes 3145728 | tf_op jit(solution)/shard_map/all_to_all | solution.py:479
  315.1 2.0 copy-start.5
  315.1 2.3 copy-start.7
  338.0 1.2 copy-start.1
  (3 other events, 3.2 us)
Sparse Core Ops, SparseCore 0:
  45.1 63.2 all-gather.1
  110.9 89.7 reduce-scatter.2
  245.1 61.8 reduce-scatter.4
